TPU v7x, 32 devices: a whole 2x2x4 slice. The times are simulated.
32 devices in a mesh: pipe: 2 (over core), dp: 4 (over z), seq: 4 (over y, x).
Axes of the slice: x: 2, y: 2, z: 4, core: 2. Of those that a mesh axis runs over, the one named last changes fastest.
Arguments:
- inputs: bfloat16 [96, 1024, 1024], P('dp', 'seq'), may hold values from -6 to 6
- cotangent: bfloat16 [96, 1024, 1024], P('dp', 'seq'), may hold values from -6 to 6
- mask_flags: int32 [96, 1024], P('dp', 'seq'), may hold values from 0 to 1, as said below
- residue_types: int32 [96, 1024], P('dp', 'seq'), may hold values from 0 to 29
- predicted: int32 [96, 1024], P('dp', 'seq'), may hold values from 0 to 29
- outer_params: float32 [2, 3, 1024], P('pipe')
- narrow: bfloat16 [2, 1024, 512], P('pipe'), may hold values from -0.1875 to 0.1875
- dilated: bfloat16 [2, 5, 512, 512], P('pipe'), may hold values from -0.125 to 0.125
- restore: bfloat16 [2, 512, 1024], P('pipe'), may hold values from -0.25 to 0.25
- inner_params: float32 [2, 6, 512], P('pipe')
Outputs:
- block_output: bfloat16 [96, 1024, 1024], P('dp', 'seq', 'pipe')
- input_grad: bfloat16 [96, 1024, 1024], P('dp', 'seq', 'pipe')
- outer_grad: float32 [2, 3, 1024], P('pipe')
- narrow_grad: float32 [2, 1024, 512], P('pipe')
- dilated_grad: float32 [2, 5, 512, 512], P('pipe')
- restore_grad: float32 [2, 512, 1024], P('pipe')
- inner_grad: float32 [2, 6, 512], P('pipe')
- accuracy: int32 [2, 30], replicated
Inputs may be any that keep to these rules, and one draw needn't show every extreme that they name: `mask_flags`: the first residue of every sequence is masked.
All inputs are finite; a program needn't handle non-finite values.
Results may differ from a plain program's by a relative error of at most 0.015.
Values may be sent and summed in bfloat16 or wider, within the bound.
A program may use at most 320 MiB of HBM per device.

v0:
```python
import jax
import jax.numpy as jnp
from jax import lax
from jax.sharding import PartitionSpec as P

KERNEL = 5
FIRST_DILATION = 2
SECOND_DILATION = 4
TYPES = 30
LENGTH = 1024
REACH = 8


epsilon = 1e-05


def extended(block, sides, width):
    for axis, dim in sides:
        count = lax.axis_size(axis)
        forward = [(i, i + 1) for i in range(count - 1)]
        backward = [(target, source) for source, target in forward]
        low = lax.ppermute(
            lax.slice_in_dim(block, block.shape[dim] - width, None, axis=dim), axis, forward
        )
        high = lax.ppermute(lax.slice_in_dim(block, 0, width, axis=dim), axis, backward)
        block = jnp.concatenate([low, block, high], axis=dim)
    return block


def shifted(block, axis, distance):
    devices = range(lax.axis_size(axis))
    route = [(i - distance, i) for i in devices if i - distance in devices]
    return lax.ppermute(block, axis, route)


def partner(block, axis, bit):
    count = lax.axis_size(axis)
    route = []
    for low in range(count):
        high = low | 1 << bit
        if high != low and high < count:
            route += [(low, high), (high, low)]
    return lax.ppermute(block, axis, route)


def norm_act(values, gain_row, shift_row):
    average = jnp.mean(values, axis=-1, keepdims=True)
    centered = values - average
    spread = jnp.mean(centered * centered, axis=-1, keepdims=True)
    normed = centered * lax.rsqrt(spread + epsilon)
    return jax.nn.gelu(normed * gain_row + shift_row, approximate=False)


def gather_taps(padded, dilation_factor, row_count, direction):
    pieces = []
    for offset in range(KERNEL):
        start_row = REACH + direction * (offset - KERNEL // 2) * dilation_factor
        pieces.append(lax.dynamic_slice_in_dim(padded, start_row, row_count, 0))
    return jnp.concatenate(pieces, axis=1)


def conv_rims(values):
    return extended(values, (("seq", 0),), REACH)


def block_forward(
    activation_flow, outer, inner, narrow_w, dilated_w, restore_w, dilation_factor, spread_fn
):
    first_act = norm_act(activation_flow, outer[0], outer[1]).astype(jnp.bfloat16)
    hidden = jnp.dot(first_act, narrow_w, preferred_element_type=jnp.float32) + inner[0]
    second_act = norm_act(hidden, inner[2], inner[3]).astype(jnp.bfloat16)
    padded = spread_fn(second_act)
    windows = gather_taps(padded, dilation_factor, activation_flow.shape[0], 1)
    inner_width = dilated_w.shape[-1]
    stacked = dilated_w.reshape(KERNEL * inner_width, inner_width)
    mixed = jnp.dot(windows, stacked, preferred_element_type=jnp.float32) + inner[1]
    third_act = norm_act(mixed, inner[4], inner[5]).astype(jnp.bfloat16)
    result = activation_flow + (
        jnp.dot(third_act, restore_w, preferred_element_type=jnp.float32) + outer[2]
    )
    return (result, hidden, padded, mixed)


def block_backward(
    activation_flow,
    hidden,
    padded,
    mixed,
    grad_out,
    outer,
    inner,
    narrow_w,
    dilated_w,
    restore_w,
    dilation_factor,
):
    row_count = activation_flow.shape[0]
    inner_width = dilated_w.shape[-1]
    third_act, third_back = jax.vjp(norm_act, mixed, inner[4], inner[5])
    grad_low = grad_out.astype(jnp.bfloat16)
    restore_grad = jnp.dot(
        third_act.astype(jnp.bfloat16).T, grad_low, preferred_element_type=jnp.float32
    )
    outer_bias_grad = jnp.sum(grad_low.astype(jnp.float32), axis=0)
    grad_third = jnp.dot(grad_low, restore_w.T, preferred_element_type=jnp.float32)
    grad_mixed, last_gain_grad, last_shift_grad = third_back(grad_third)
    mixed_low = grad_mixed.astype(jnp.bfloat16)
    windows = gather_taps(padded, dilation_factor, row_count, 1)
    dilated_grad = jnp.dot(windows.T, mixed_low, preferred_element_type=jnp.float32).reshape(
        KERNEL, inner_width, inner_width
    )
    conv_bias_grad = jnp.sum(mixed_low.astype(jnp.float32), axis=0)
    grad_padded = extended(mixed_low, (("seq", 0),), REACH)
    back_windows = gather_taps(grad_padded, dilation_factor, row_count, -1)
    flipped = jnp.transpose(dilated_w, (0, 2, 1)).reshape(KERNEL * inner_width, inner_width)
    grad_second = jnp.dot(back_windows, flipped, preferred_element_type=jnp.float32)
    second_act, second_back = jax.vjp(norm_act, hidden, inner[2], inner[3])
    grad_hidden, middle_gain_grad, middle_shift_grad = second_back(grad_second)
    hidden_low = grad_hidden.astype(jnp.bfloat16)
    first_act, first_back = jax.vjp(norm_act, activation_flow, outer[0], outer[1])
    narrow_grad = jnp.dot(
        first_act.astype(jnp.bfloat16).T, hidden_low, preferred_element_type=jnp.float32
    )
    inner_bias_grad = jnp.sum(hidden_low.astype(jnp.float32), axis=0)
    grad_first = jnp.dot(hidden_low, narrow_w.T, preferred_element_type=jnp.float32)
    grad_stream, first_gain_grad, first_shift_grad = first_back(grad_first)
    outer_grad = jnp.stack([first_gain_grad, first_shift_grad, outer_bias_grad])
    inner_grad = jnp.stack(
        [
            inner_bias_grad,
            conv_bias_grad,
            middle_gain_grad,
            middle_shift_grad,
            last_gain_grad,
            last_shift_grad,
        ]
    )
    return (
        grad_out + grad_stream,
        (outer_grad, narrow_grad, dilated_grad, restore_grad, inner_grad),
    )


def place(buffer, values, slot_index, usable):
    previous = lax.dynamic_index_in_dim(buffer, slot_index, 0, keepdims=False)
    chosen = jnp.where(usable, values, previous)
    return lax.dynamic_update_index_in_dim(buffer, chosen, slot_index, 0)


def fetch(buffer, slot_index):
    return lax.dynamic_index_in_dim(buffer, slot_index, 0, keepdims=False)


def shards(
    inputs,
    cotangent,
    mask_flags,
    residue_types,
    predicted,
    outer_params,
    narrow,
    dilated,
    restore,
    inner_params,
):
    relay_section_index = lax.axis_index("pipe")
    dilation_factor = FIRST_DILATION + (SECOND_DILATION - FIRST_DILATION) * relay_section_index
    outer = outer_params[0]
    inner = inner_params[0]
    narrow_w = narrow[0]
    dilated_w = dilated[0]
    restore_w = restore[0]
    micro_count, row_count, model_width = inputs.shape
    inner_width = narrow_w.shape[1]
    type_ids = jnp.arange(TYPES, dtype=jnp.int32)
    matches = residue_types[:, :, None] == type_ids
    right_flags = mask_flags * (predicted == residue_types).astype(jnp.int32)
    right_counts = jnp.sum(jnp.where(matches, right_flags[:, :, None], 0), axis=(0, 1))
    masked_counts = jnp.sum(jnp.where(matches, mask_flags[:, :, None], 0), axis=(0, 1))
    type_table = jnp.stack([right_counts, masked_counts])
    masked_count = lax.psum(jnp.sum(mask_flags), ("dp", "seq"))
    factor = jnp.float32(micro_count * lax.axis_size("dp") * LENGTH) / masked_count.astype(
        jnp.float32
    )
    kept_init = (
        jnp.zeros((micro_count, row_count, model_width), jnp.float32),
        jnp.zeros((micro_count, row_count, inner_width), jnp.float32),
        jnp.zeros((micro_count, row_count + 2 * REACH, inner_width), jnp.bfloat16),
        jnp.zeros((micro_count, row_count, inner_width), jnp.float32),
    )
    finals_init = jnp.zeros((micro_count, row_count, model_width), jnp.bfloat16)
    empty_rows = jnp.zeros((row_count, model_width), jnp.float32)

    def forward_step(step_index, carried):
        arrived, kept, finals = carried
        slot_raw = step_index - relay_section_index
        usable = (slot_raw >= 0) & (slot_raw < micro_count)
        slot_index = jnp.clip(slot_raw, 0, micro_count - 1)
        own_input = fetch(inputs, jnp.minimum(step_index, micro_count - 1)).astype(jnp.float32)
        activation_flow = jnp.where(relay_section_index == 0, own_input, arrived)
        result, hidden, padded, mixed = block_forward(
            activation_flow,
            outer,
            inner,
            narrow_w,
            dilated_w,
            restore_w,
            dilation_factor,
            conv_rims,
        )
        fresh = (activation_flow, hidden, padded, mixed)
        kept = tuple((place(older, newer, slot_index, usable) for older, newer in zip(kept, fresh)))
        finals = place(
            finals, result.astype(jnp.bfloat16), slot_index, usable & (relay_section_index == 1)
        )
        arrived = shifted(result.astype(jnp.bfloat16), "pipe", 1).astype(result.dtype)
        return (arrived, kept, finals)

    arrived, kept, finals = lax.fori_loop(
        0, micro_count + 1, forward_step, (empty_rows, kept_init, finals_init)
    )

    def backward_step(step_index, carried):
        arrived, grad_sums, grads_in = carried
        slot_raw = step_index - 1 + relay_section_index
        usable = (slot_raw >= 0) & (slot_raw < micro_count)
        slot_index = jnp.clip(slot_raw, 0, micro_count - 1)
        seed_index = jnp.minimum(step_index, micro_count - 1)
        seed_flags = fetch(mask_flags, seed_index).astype(jnp.float32)
        seed_grad = fetch(cotangent, seed_index).astype(jnp.float32) * seed_flags[:, None] * factor
        grad_out = jnp.where(relay_section_index == 1, seed_grad, arrived)
        activation_flow = fetch(kept[0], slot_index)
        hidden = fetch(kept[1], slot_index)
        padded = fetch(kept[2], slot_index)
        mixed = fetch(kept[3], slot_index)
        grad_stream, grads = block_backward(
            activation_flow,
            hidden,
            padded,
            mixed,
            grad_out,
            outer,
            inner,
            narrow_w,
            dilated_w,
            restore_w,
            dilation_factor,
        )
        grad_sums = tuple(
            (total + jnp.where(usable, piece, 0.0) for total, piece in zip(grad_sums, grads))
        )
        grads_in = place(
            grads_in,
            grad_stream.astype(jnp.bfloat16),
            slot_index,
            usable & (relay_section_index == 0),
        )
        arrived = shifted(grad_stream.astype(jnp.bfloat16), "pipe", -1).astype(grad_stream.dtype)
        return (arrived, grad_sums, grads_in)

    zero_sums = (
        jnp.zeros(outer.shape, jnp.float32),
        jnp.zeros(narrow_w.shape, jnp.float32),
        jnp.zeros(dilated_w.shape, jnp.float32),
        jnp.zeros(restore_w.shape, jnp.float32),
        jnp.zeros(inner.shape, jnp.float32),
    )
    grads_init = jnp.zeros((micro_count, row_count, model_width), jnp.bfloat16)
    start = (empty_rows, zero_sums, grads_init)
    carried = lax.fori_loop(0, micro_count + 1, backward_step, start)
    outer_sum, narrow_sum, dilated_sum, restore_sum, inner_sum = carried[1]
    totals = lax.psum((outer_sum, narrow_sum, dilated_sum, restore_sum, inner_sum), ("dp", "seq"))
    grads_in = carried[2]
    accuracy = lax.psum(type_table, ("dp", "seq"))
    half_width = model_width // 2
    own_rows = jnp.where(relay_section_index == 0, grads_in, finals)
    outgoing = jnp.where(
        relay_section_index == 0, own_rows[:, :, half_width:], own_rows[:, :, :half_width]
    )
    incoming = partner(outgoing, "pipe", 0)
    input_grad = jnp.where(relay_section_index == 0, own_rows[:, :, :half_width], incoming)
    block_output = jnp.where(relay_section_index == 0, incoming, own_rows[:, :, half_width:])
    return (
        block_output,
        input_grad,
        totals[0][None],
        totals[1][None],
        totals[2][None],
        totals[3][None],
        totals[4][None],
        accuracy,
    )


def solution(mesh):
    in_specs = (
        P("dp", "seq", None),
        P("dp", "seq", None),
        P("dp", "seq"),
        P("dp", "seq"),
        P("dp", "seq"),
        P("pipe", None, None),
        P("pipe", None, None),
        P("pipe", None, None, None),
        P("pipe", None, None),
        P("pipe", None, None),
    )
    out_specs = (
        P("dp", "seq", "pipe"),
        P("dp", "seq", "pipe"),
        P("pipe", None, None),
        P("pipe", None, None),
        P("pipe", None, None, None),
        P("pipe", None, None),
        P("pipe", None, None),
        P(),
    )
    return jax.shard_map(shards, mesh=mesh, in_specs=in_specs, out_specs=out_specs, check_vma=False)
```

profile of v0, /device:TPU:0, one launch (start us, length us, event | category | flops | bytes accessed | tf_op | source)
XLA Modules:
  0.0 2734.4 jit_solution(10775865897695240046)
XLA Ops:
  12.1 16.9 all-reduce
  34.0 11.5 broadcast_in_dim.286
  45.6 6.1 broadcast.1631.clone
  51.7 6.2 broadcast.1632
  57.9 6.1 broadcast.1632.clone
  67.5 862.7 %while.56 = (s32[]{:T(128)}, f32[256,1024]{1,0:T(8,128)S(1)}, f32[24,256,1024]{2,1,0:T(8,128)}, f32[24,256,512]{2,1,0:T(8,128)}, bf16[24,272,512]{2,1,0:T(8,128)...) while((s32[]{:T(128)}, f32[256,1024]{1,0:T(8,128)S(1)}, ...), condition=%wide.region_9.10_spmd.clone, body=%wide.region_2.9_spmd.clone.sunk | while | flops 1269015296 | bytes 44597332 | solution.py:219
  146.5 5.4 collective-permute-start.1
  250.1 5.5 collective-permute-start.1
  284.7 5.5 collective-permute-start.1
  388.4 5.4 collective-permute-start.1
  561.2 5.5 collective-permute-start.1
  595.7 5.5 collective-permute-start.1
  664.8 5.5 collective-permute-start.1
  733.9 5.5 collective-permute-start.1
  768.5 5.5 collective-permute-start.1
  803.0 5.5 collective-permute-start.1
  872.1 5.5 collective-permute-start.1
  930.2 6.0 broadcast.1631
  936.2 1496.4 %while.57 = (s32[]{:T(128)}, f32[256,1024]{1,0:T(8,128)S(1)}, f32[3,1024]{1,0:T(4,128)S(1)}, f32[1024,512]{1,0:T(8,128)S(1)}, f32[5,512,512]{2,1,0:T(8,128)}, /*...) while((s32[]{:T(128)}, f32[256,1024]{1,0:T(8,128)S(1)}, ...), condition=%wide.region_32.33_spmd.clone, body=%wide.region_10.32_spmd.clone.sunk | while | flops 2491227648 | bytes 139638864 | solution.py:270
  2434.0 6.9 broadcast_select_fusion
  2449.2 79.0 %all-reduce.1 = (f32[1,3,1024]{2,0,1:T(1,128)}, f32[1,6,512]{2,0,1:T(1,128)}) all-reduce(f32[1,3,1024]{2,0,1:T(1,128)S(1)} %broadcast_in_dim.288, f32[1,6,512]{2,0,1:T(1,128)S(1)} %broadcast_in_dim.292), channel_id=1, replica_groups=mesh['pipe'=2,'dp'=4,'seq'=4] {'dp','seq'}, use_global_device_ids=true, to_apply=%region_33.34 | all-reduce | flops 6144 | bytes 49152 | tf_op jit(solution)/shard_map/psum | solution.py:272
  2528.2 12.1 broadcast_select_fusion.1
  2540.2 176.8 %all-reduce.5.cloned.1.call-done = (f32[1,1024,512]{2,1,0:T(8,128)}, f32[1,5,512,512]{3,2,1,0:T(8,128)}, f32[1,512,1024]{2,1,0:T(8,128)}) async-done(((f32[1,1024,512]{2,1,0:T(8,128)}, f32[1,5,512,512]{3,2,1,0:T(8,128)}, f32[1,512,1024]{2,1,0:T(8,128)}), (f32[1,1024,512]{2,1,0:T(8,128)}, f32[1,5,512,512]{3,2,1,0:T(8,128)}, f32[1,512,1024]{2,1,0:T(8,128)})) %all-reduce.5.cloned.1.call-update) | async-done | bytes 9437200 | tf_op jit(solution)/shard_map/psum | solution.py:272
  2720.1 6.0 copy.94
  (3195 shorter events, 2296.7 us)
Async XLA Ops:
  7.2 2709.8 %all-reduce.5.cloned.1.call-start = ((), (), s32[]{:S(2)}) async-start(), calls=%async_computation | async-start | bytes 18874368 | tf_op jit(solution)/shard_map/psum | solution.py:272
  962.5 23.6 collective-permute-start.3
  1021.8 23.6 collective-permute-start.3
  1081.4 23.4 collective-permute-start.3
  1200.2 23.4 collective-permute-start.3
  1259.6 23.4 collective-permute-start.3
  1318.9 23.4 collective-permute-start.3
  1378.3 23.4 collective-permute-start.3
  1437.7 23.4 collective-permute-start.3
  1497.0 23.4 collective-permute-start.3
  1556.4 23.4 collective-permute-start.3
  1615.8 23.4 collective-permute-start.3
  1675.2 23.4 collective-permute-start.3
  1734.5 23.4 collective-permute-start.3
  1793.9 23.4 collective-permute-start.3
  1853.2 23.4 collective-permute-start.3
  1912.6 23.4 collective-permute-start.3
  1972.0 23.4 collective-permute-start.3
  2031.3 23.4 collective-permute-start.3
  2090.7 23.4 collective-permute-start.3
  2150.1 23.4 collective-permute-start.3
  2209.5 23.4 collective-permute-start.3
  2328.2 23.4 collective-permute-start.3
  2447.5 80.7 %collective-permute-start.6 = (bf16[24,256,512]{2,1,0:T(8,128)(2,1)}, bf16[24,256,512]{2,1,0:T(8,128)(2,1)}, u32[]{:S(2)}, u32[]{:S(2)}) collective-permute-start(bf16[24,256,512]{2,1,0:T(8,128)(2,1)} %broadcast_select_fusion.3), channel_id=1, source_target_pairs={{0,16},{16,0},{1,17},{17,1},{2,18},{18,2},{3,19},{19,3},{4,20},{20... | collective-permute-start | bytes 18874376 | tf_op jit(solution)/shard_map/ppermute | solution.py:43
  (532 other events, 3171.5 us)
Sparse Core Ops, SparseCore 0:
  2434.1 282.8 all-reduce.4
where the time goes:
time: 2770 us; the launch traced here: 2730 us
  other arithmetic  833 us (30%)
  matrix products  726 us (26%)
  local copies, waits for them, and re-layouts  451 us (16%)
  starting transfers between devices  395 us (14%)
  waiting for transfers between devices  190 us (7%)
  blocking collectives  95.9 us (3%)
  loops' own time  29.2 us (1%)
    ppermute x50, starting transfers between devices, extended(): lax.ppermute(lax.slice_in_dim(block, block.shape[dim] - width, None, axis...  265 us
    dynamic_update_slice x125, other arithmetic, place(): return lax.dynamic_update_index_in_dim(buffer, chosen, slot_index, 0)  248 us
    psum x1, waiting for transfers between devices, shards(): lax.psum((outer_sum, narrow_sum, dilated_sum, restore_sum, inner_sum), ('...  177 us
    while x1075, local copies, waits for them, and re-layouts  174 us
    dynamic_slice x100, local copies, waits for them, and re-layouts, place(): previous = lax.dynamic_index_in_dim(buffer, slot_index, 0, keepdims=False)  153 us
    dot_general x25, matrix products, block_backward(): jnp.dot(hidden_low, narrow_w.T, preferred_element_type=jnp.float32)  130 us
    dot_general x25, matrix products, block_backward(): jnp.dot(back_windows, flipped, preferred_element_type=jnp.float32)  103 us
    dot_general x25, matrix products, block_forward(): jnp.dot(first_act, narrow_w, preferred_element_type=jnp.float32) + inner[0]  98.3 us
  transfers between devices with their start and end apart: 152, of which 26 were waited for; matrix products, arithmetic and copies ran while one was open for 25% of the time, Pallas kernels for 0%

commit v1 on v0

v1 whole, which is shorter than its diff:
```python
import functools

import jax
import jax.numpy as jnp
from jax import lax
from jax.experimental import pallas as pl
from jax.experimental.pallas import tpu as pltpu
from jax.sharding import PartitionSpec as P

KERNEL = 5
FIRST_DILATION = 2
SECOND_DILATION = 4
TYPES = 30
LENGTH = 1024
REACH = 8
EPSILON = 1e-05
VMEM_LIMIT = 60 << 20

f32 = jnp.float32
bf16 = jnp.bfloat16

ROOT_HALF = 0.7071067811865476
INV_ROOT_2PI = 0.3989422804014327
EXP2_SCALE = -0.5 * 1.4426950408889634


def normalized(v):
    scale = 1.0 / v.shape[-1]
    centered = v - jnp.sum(v, axis=-1, keepdims=True) * scale
    spread = jnp.sum(centered * centered, axis=-1, keepdims=True) * scale
    r = lax.rsqrt(spread + EPSILON)
    return centered * r, r


def upper(u):
    return 0.5 * lax.erf(u * ROOT_HALF) + 0.5


def norm_act(v, g, s):
    n, _ = normalized(v)
    u = n * g + s
    return (u * upper(u)).astype(bf16)


def fold(v):
    rows, width = v.shape
    return jnp.sum(v.reshape(rows // 8, 8, width), axis=0)


class Back:
    def __init__(self, v, g, s):
        self.n, self.r = normalized(v)
        self.g = g
        u = self.n * g + s
        phi = upper(u)
        self.act = (u * phi).astype(bf16)
        self.slope = phi + u * (INV_ROOT_2PI * jnp.exp2(u * u * EXP2_SCALE))

    def grad(self, e):
        p = e * self.slope
        pn = p * self.n
        scale = 1.0 / p.shape[-1]
        pg = p * self.g
        a = jnp.sum(pg, axis=-1, keepdims=True) * scale
        b = jnp.sum(pn * self.g, axis=-1, keepdims=True) * scale
        return self.r * (pg - a - self.n * b), fold(pn), fold(p)


def dot(a, b):
    return jnp.dot(a, b, preferred_element_type=f32)


def dot_nt(a, b):
    return lax.dot_general(a, b, (((1,), (1,)), ((), ())), preferred_element_type=f32)


def dot_tn(a, b):
    return lax.dot_general(a, b, (((0,), (0,)), ((), ())), preferred_element_type=f32)


def fill(pad, low, rows_ref, high):
    rows = rows_ref.shape[0]
    pad[0:REACH, :] = low.astype(f32)
    pad[REACH : REACH + rows, :] = rows_ref[...].astype(f32)
    pad[REACH + rows :, :] = high.astype(f32)


def taps(pad, rows, d, direction):
    pieces = []
    for k in range(KERNEL):
        start = REACH + direction * (k - KERNEL // 2) * d
        pieces.append(pad[start : start + rows, :].astype(bf16))
    return pieces


def row(ref, i):
    return ref[0, i : i + 1, :]


def first_half(seqs, x_ref, outer_ref, inner_ref, narrow_ref, hidden_ref, second_ref, edge_ref):
    rows = x_ref.shape[1]
    for i in range(seqs):
        act = norm_act(x_ref[i].astype(f32), row(outer_ref, 0), row(outer_ref, 1))
        hidden = dot(act, narrow_ref[0]) + row(inner_ref, 0)
        hidden_ref[i] = hidden
        second = norm_act(hidden, row(inner_ref, 2), row(inner_ref, 3))
        second_ref[i] = second
        edge_ref[0, i] = second[:REACH]
        edge_ref[1, i] = second[rows - REACH :]


def middle_half(
    seqs,
    d,
    x_ref,
    second_ref,
    halo_ref,
    outer_ref,
    inner_ref,
    dilated_ref,
    restore_ref,
    next_outer_ref,
    next_inner_ref,
    next_narrow_ref,
    mixed_ref,
    middle_ref,
    hidden_ref,
    next_second_ref,
    edge_ref,
    pads,
):
    rows = x_ref.shape[1]
    inner = inner_ref.shape[-1]
    for i in range(seqs):
        pad = pads.at[i]
        fill(pad, halo_ref[0, i], second_ref.at[i], halo_ref[1, i])
        windows = jnp.concatenate(taps(pad, rows, d, 1), axis=1)
        mixed = dot(windows, dilated_ref[0].reshape(KERNEL * inner, inner)) + row(inner_ref, 1)
        mixed_ref[i] = mixed
        third = norm_act(mixed, row(inner_ref, 4), row(inner_ref, 5))
        y = x_ref[i].astype(f32) + (dot(third, restore_ref[0]) + row(outer_ref, 2))
        middle_ref[i] = y
        act = norm_act(y, row(next_outer_ref, 0), row(next_outer_ref, 1))
        hidden = dot(act, next_narrow_ref[0]) + row(next_inner_ref, 0)
        hidden_ref[i] = hidden
        second = norm_act(hidden, row(next_inner_ref, 2), row(next_inner_ref, 3))
        next_second_ref[i] = second
        edge_ref[0, i] = second[:REACH]
        edge_ref[1, i] = second[rows - REACH :]


def start_sums(refs):
    @pl.when(pl.program_id(0) == 0)
    def _():
        for ref in refs:
            ref[...] = jnp.zeros_like(ref)


def column(flags):
    return jnp.transpose(jnp.broadcast_to(flags, (128, flags.shape[1])))


def seeded(cot, flags):
    col = column(flags)
    return cot.astype(f32) * jnp.concatenate([col] * (cot.shape[1] // 128), axis=1)


def turn(
    seqs,
    d,
    middle_ref,
    second_ref,
    halo_ref,
    cot_ref,
    flags_ref,
    outer_ref,
    inner_ref,
    dilated_ref,
    restore_ref,
    own_ref,
    other_ref,
    gm_ref,
    edge_ref,
    restore_sum,
    wide_sum,
    small_sum,
    pads,
):
    rows = middle_ref.shape[1]
    inner = inner_ref.shape[-1]
    half = own_ref.shape[-1]
    core = lax.axis_index("pipe")
    start_sums((restore_sum, wide_sum, small_sum))
    for i in range(seqs):
        pad = pads.at[i]
        fill(pad, halo_ref[0, i], second_ref.at[i], halo_ref[1, i])
        windows = jnp.concatenate(taps(pad, rows, d, 1), axis=1)
        mixed = dot(windows, dilated_ref[0].reshape(KERNEL * inner, inner)) + row(inner_ref, 1)
        back = Back(mixed, row(inner_ref, 4), row(inner_ref, 5))
        y = middle_ref[i] + (dot(back.act, restore_ref[0]) + row(outer_ref, 2))
        y = y.astype(bf16)
        left, right = y[:, :half], y[:, half:]
        own_ref[i] = jnp.where(core == 0, left, right)
        other_ref[i] = jnp.where(core == 0, right, left)
        grad_low = seeded(cot_ref[i], flags_ref[i]).astype(bf16)
        gm = block_out_back(back, grad_low, restore_ref, restore_sum, wide_sum, small_sum)
        gm_ref[i] = gm
        edge_ref[0, i] = gm[:REACH]
        edge_ref[1, i] = gm[rows - REACH :]


def block_out_back(back, grad_low, restore_ref, restore_sum, wide_sum, small_sum):
    restore_sum[...] += dot_tn(back.act, grad_low)
    wide_sum[...] += fold(grad_low.astype(f32))
    gv, gain, shift = back.grad(dot_nt(grad_low, restore_ref[0]))
    gm = gv.astype(bf16)
    small_sum[0:8] += fold(gm.astype(f32))
    small_sum[8:16] += gain
    small_sum[16:24] += shift
    return gm


def block_in_back(
    i,
    d,
    stream,
    grad_out,
    hidden_ref,
    second_ref,
    halo_ref,
    gm_ref,
    gm_halo_ref,
    outer_ref,
    inner_ref,
    narrow_ref,
    dilated_ref,
    narrow_sum,
    dilated_sum,
    wide_sum,
    small_sum,
    pad,
    gm_pad,
):
    rows = stream.shape[0]
    fill(gm_pad, gm_halo_ref[0, i], gm_ref.at[i], gm_halo_ref[1, i])
    grad_second = None
    for k, piece in enumerate(taps(gm_pad, rows, d, -1)):
        term = dot_nt(piece, dilated_ref[0, k])
        grad_second = term if grad_second is None else grad_second + term
    fill(pad, halo_ref[0, i], second_ref.at[i], halo_ref[1, i])
    windows = jnp.concatenate(taps(pad, rows, d, 1), axis=1)
    dilated_sum[...] += dot_tn(windows, gm_ref[i])
    back = Back(hidden_ref[i], row(inner_ref, 2), row(inner_ref, 3))
    gv, gain, shift = back.grad(grad_second)
    gh = gv.astype(bf16)
    small_sum[0:8] += fold(gh.astype(f32))
    small_sum[8:16] += gain
    small_sum[16:24] += shift
    first = Back(stream, row(outer_ref, 0), row(outer_ref, 1))
    narrow_sum[...] += dot_tn(first.act, gh)
    gx, gain, shift = first.grad(dot_nt(gh, narrow_ref[0]))
    wide_sum[0:8] += gain
    wide_sum[8:16] += shift
    return grad_out + gx


def between(
    seqs,
    d,
    middle_ref,
    cot_ref,
    flags_ref,
    hidden_ref,
    second_ref,
    halo_ref,
    gm_ref,
    gm_halo_ref,
    outer_ref,
    inner_ref,
    narrow_ref,
    dilated_ref,
    mixed_ref,
    lower_inner_ref,
    lower_restore_ref,
    gx_ref,
    lower_gm_ref,
    edge_ref,
    narrow_sum,
    dilated_sum,
    wide_sum,
    small_sum,
    lower_restore_sum,
    lower_wide_sum,
    lower_small_sum,
    pads,
    gm_pads,
):
    rows = middle_ref.shape[1]
    start_sums(
        (
            narrow_sum,
            dilated_sum,
            wide_sum,
            small_sum,
            lower_restore_sum,
            lower_wide_sum,
            lower_small_sum,
        )
    )
    for i in range(seqs):
        gx = block_in_back(
            i,
            d,
            middle_ref[i],
            seeded(cot_ref[i], flags_ref[i]),
            hidden_ref,
            second_ref,
            halo_ref,
            gm_ref,
            gm_halo_ref,
            outer_ref,
            inner_ref,
            narrow_ref,
            dilated_ref,
            narrow_sum,
            dilated_sum,
            wide_sum,
            small_sum,
            pads.at[i],
            gm_pads.at[i],
        )
        gx_ref[i] = gx
        lower = Back(mixed_ref[i], row(lower_inner_ref, 4), row(lower_inner_ref, 5))
        gm = block_out_back(
            lower,
            gx.astype(bf16),
            lower_restore_ref,
            lower_restore_sum,
            lower_wide_sum,
            lower_small_sum,
        )
        lower_gm_ref[i] = gm
        edge_ref[0, i] = gm[:REACH]
        edge_ref[1, i] = gm[rows - REACH :]


def last_half(
    seqs,
    d,
    x_ref,
    gx_ref,
    hidden_ref,
    second_ref,
    halo_ref,
    gm_ref,
    gm_halo_ref,
    outer_ref,
    inner_ref,
    narrow_ref,
    dilated_ref,
    own_ref,
    other_ref,
    narrow_sum,
    dilated_sum,
    wide_sum,
    small_sum,
    pads,
    gm_pads,
):
    half = own_ref.shape[-1]
    core = lax.axis_index("pipe")
    start_sums((narrow_sum, dilated_sum, wide_sum, small_sum))
    for i in range(seqs):
        gx = block_in_back(
            i,
            d,
            x_ref[i].astype(f32),
            gx_ref[i],
            hidden_ref,
            second_ref,
            halo_ref,
            gm_ref,
            gm_halo_ref,
            outer_ref,
            inner_ref,
            narrow_ref,
            dilated_ref,
            narrow_sum,
            dilated_sum,
            wide_sum,
            small_sum,
            pads.at[i],
            gm_pads.at[i],
        )
        gx = gx.astype(bf16)
        left, right = gx[:, :half], gx[:, half:]
        own_ref[i] = jnp.where(core == 0, left, right)
        other_ref[i] = jnp.where(core == 0, right, left)


class Caller:
    def __init__(self, name, seqs, count, base):
        self.name, self.seqs, self.count, self.base = name, seqs, count, base
        self.in_specs, self.args, self.out_specs, self.outs, self.scratch = [], [], [], [], []

    def seq(self, *arrays):
        for a in arrays:
            self.in_specs.append(pl.BlockSpec((self.seqs, *a.shape[1:]), lambda i, b: (i, 0, 0)))
            self.args.append(a)
        return self

    def own(self, *arrays):
        step = self.count // self.seqs
        for a in arrays:
            self.in_specs.append(
                pl.BlockSpec((self.seqs, *a.shape[1:]), lambda i, b: (b[0] * step + i, 0, 0))
            )
            self.args.append(a)
        return self

    def halo(self, *arrays):
        for a in arrays:
            self.in_specs.append(
                pl.BlockSpec((2, self.seqs, *a.shape[2:]), lambda i, b: (0, i, 0, 0))
            )
            self.args.append(a)
        return self

    def whole(self, *arrays):
        for a in arrays:
            zeros = (0,) * a.ndim
            self.in_specs.append(
                pl.BlockSpec(a.shape, lambda i, b, zeros=zeros: zeros, pipeline_mode=pl.Buffered(1))
            )
            self.args.append(a)
        return self

    def block(self, index, *arrays):
        for a in arrays:
            spot = (index,) + (0,) * (a.ndim - 1)
            self.in_specs.append(
                pl.BlockSpec(
                    (1, *a.shape[1:]), lambda i, b, spot=spot: spot, pipeline_mode=pl.Buffered(1)
                )
            )
            self.args.append(a)
        return self

    def out_seq(self, *shapes):
        for shape, dtype in shapes:
            self.out_specs.append(pl.BlockSpec((self.seqs, *shape), lambda i, b: (i, 0, 0)))
            self.outs.append(jax.ShapeDtypeStruct((self.count, *shape), dtype))
        return self

    def out_edge(self, width):
        self.out_specs.append(
            pl.BlockSpec((2, self.seqs, REACH, width), lambda i, b: (0, i, 0, 0))
        )
        self.outs.append(jax.ShapeDtypeStruct((2, self.count, REACH, width), bf16))
        return self

    def out_sum(self, *shapes):
        for shape in shapes:
            self.out_specs.append(pl.BlockSpec(shape, lambda i, b: (0, 0)))
            self.outs.append(jax.ShapeDtypeStruct(shape, f32))
        return self

    def pads(self, number, rows, width):
        for _ in range(number):
            self.scratch.append(pltpu.VMEM((self.seqs, rows + 2 * REACH, width), f32))
        return self

    def __call__(self, kernel):
        return pl.pallas_call(
            kernel,
            grid_spec=pltpu.PrefetchScalarGridSpec(
                num_scalar_prefetch=1,
                grid=(self.count // self.seqs,),
                in_specs=self.in_specs,
                out_specs=self.out_specs,
                scratch_shapes=self.scratch,
            ),
            out_shape=self.outs,
            compiler_params=pltpu.CompilerParams(vmem_limit_bytes=VMEM_LIMIT),
            name=self.name,
        )(self.base, *self.args)


def without_base(function, *static):
    def kernel(base_ref, *refs):
        del base_ref
        function(*static, *refs)

    return kernel


def spread(edges):
    count = lax.axis_size("seq")
    up = [(i, i + 1) for i in range(count - 1)]
    down = [(b, a) for a, b in up]
    low = lax.ppermute(edges[1], "seq", up)
    high = lax.ppermute(edges[0], "seq", down)
    return jnp.stack([low, high])


def swap(values):
    return lax.ppermute(values, "pipe", [(0, 1), (1, 0)])


def both(values):
    return lax.all_gather(values, "pipe", axis=0, tiled=True)


def shards(
    inputs,
    cotangent,
    mask_flags,
    residue_types,
    predicted,
    outer_params,
    narrow,
    dilated,
    restore,
    inner_params,
):
    core = lax.axis_index("pipe")
    base = core.astype(jnp.int32)[None]
    chip_seqs, rows, width = inputs.shape
    inner = narrow.shape[-1]
    count = chip_seqs // 2
    half = width // 2
    type_ids = jnp.arange(TYPES, dtype=jnp.int32)
    matches = residue_types[:, :, None] == type_ids
    right_flags = mask_flags * (predicted == residue_types).astype(jnp.int32)
    right_counts = jnp.sum(jnp.where(matches, right_flags[:, :, None], 0), axis=(0, 1))
    masked_counts = jnp.sum(jnp.where(matches, mask_flags[:, :, None], 0), axis=(0, 1))
    accuracy = lax.psum(jnp.stack([right_counts, masked_counts]), ("dp", "seq"))
    masked_count = jnp.sum(accuracy[1])
    factor = f32(chip_seqs * lax.axis_size("dp") * LENGTH) / masked_count.astype(f32)
    flags = (mask_flags.astype(f32) * factor)[:, None, :]

    outer2, narrow2, dilated2, restore2, inner2 = (
        both(v) for v in (outer_params, narrow, dilated, restore, inner_params)
    )

    def caller(name, seqs):
        return Caller(name, seqs, count, base)

    seqs = 1
    hidden0, second0, edge = (
        caller("first_half", seqs)
        .own(inputs)
        .block(0, outer2, inner2, narrow2)
        .out_seq(((rows, inner), f32), ((rows, inner), bf16))
        .out_edge(inner)
    )(without_base(first_half, seqs))
    halo0 = spread(edge)

    mixed0, middle, hidden1, second1, edge = (
        caller("middle_half", seqs)
        .own(inputs)
        .seq(second0)
        .halo(halo0)
        .block(0, outer2, inner2, dilated2, restore2)
        .block(1, outer2, inner2, narrow2)
        .out_seq(
            ((rows, inner), f32), ((rows, width), f32), ((rows, inner), f32), ((rows, inner), bf16)
        )
        .out_edge(inner)
        .pads(1, rows, inner)
    )(without_base(middle_half, seqs, FIRST_DILATION))
    halo1 = spread(edge)

    out_own, out_other, gm1, edge, restore_sum1, bias_sum1, upper_sum1 = (
        caller("turn", seqs)
        .seq(middle, second1)
        .halo(halo1)
        .own(cotangent, flags)
        .block(1, outer2, inner2, dilated2, restore2)
        .out_seq(((rows, half), bf16), ((rows, half), bf16), ((rows, inner), bf16))
        .out_edge(inner)
        .out_sum((inner, width), (8, width), (24, inner))
        .pads(1, rows, inner)
    )(without_base(turn, seqs, SECOND_DILATION))
    gm_halo1 = spread(edge)

    (
        gx1,
        gm0,
        edge,
        narrow_sum1,
        dilated_sum1,
        wide_sum1,
        small_sum1,
        restore_sum0,
        bias_sum0,
        upper_sum0,
    ) = (
        caller("between", seqs)
        .seq(middle)
        .own(cotangent, flags)
        .seq(hidden1, second1)
        .halo(halo1)
        .seq(gm1)
        .halo(gm_halo1)
        .block(1, outer2, inner2, narrow2, dilated2)
        .seq(mixed0)
        .block(0, inner2, restore2)
        .out_seq(((rows, width), f32), ((rows, inner), bf16))
        .out_edge(inner)
        .out_sum(
            (width, inner),
            (KERNEL * inner, inner),
            (16, width),
            (24, inner),
            (inner, width),
            (8, width),
            (24, inner),
        )
        .pads(2, rows, inner)
    )(without_base(between, seqs, SECOND_DILATION))
    gm_halo0 = spread(edge)

    in_own, in_other, narrow_sum0, dilated_sum0, wide_sum0, small_sum0 = (
        caller("last_half", seqs)
        .own(inputs)
        .seq(gx1, hidden0, second0)
        .halo(halo0)
        .seq(gm0)
        .halo(gm_halo0)
        .block(0, outer2, inner2, narrow2, dilated2)
        .out_seq(((rows, half), bf16), ((rows, half), bf16))
        .out_sum((width, inner), (KERNEL * inner, inner), (16, width), (24, inner))
        .pads(2, rows, inner)
    )(without_base(last_half, seqs, FIRST_DILATION))

    def small(bias_sum, upper_sum, wide_sum, small_sum):
        def total(v):
            return jnp.sum(v.reshape(-1, 8, v.shape[-1]), axis=1)

        outer_grad = jnp.concatenate([total(wide_sum), total(bias_sum)])
        upper_rows, lower_rows = total(upper_sum), total(small_sum)
        inner_grad = jnp.stack(
            [
                lower_rows[0],
                upper_rows[0],
                lower_rows[1],
                lower_rows[2],
                upper_rows[1],
                upper_rows[2],
            ]
        )
        return outer_grad, inner_grad

    smalls = [
        small(bias_sum0, upper_sum0, wide_sum0, small_sum0),
        small(bias_sum1, upper_sum1, wide_sum1, small_sum1),
    ]
    parts = (
        (smalls[0][0], narrow_sum0, dilated_sum0, restore_sum0, smalls[0][1]),
        (smalls[1][0], narrow_sum1, dilated_sum1, restore_sum1, smalls[1][1]),
    )
    mine = jax.tree.map(lambda a, b: jnp.where(core == 0, a, b), *parts)
    theirs = jax.tree.map(lambda a, b: jnp.where(core == 0, b, a).astype(bf16), *parts)
    mine = jax.tree.map(lambda a, b: a + swap(b).astype(f32), mine, theirs)
    totals = lax.psum(mine, ("dp", "seq"))

    def assembled(own, other):
        arrived = swap(other)
        return jnp.where(
            core == 0,
            jnp.concatenate([own, arrived]),
            jnp.concatenate([arrived, own]),
        )

    return (
        assembled(out_own, out_other),
        assembled(in_own, in_other),
        totals[0][None],
        totals[1][None],
        totals[2].reshape(1, KERNEL, inner, inner),
        totals[3][None],
        totals[4][None],
        accuracy,
    )


def solution(mesh):
    in_specs = (
        P("dp", "seq", None),
        P("dp", "seq", None),
        P("dp", "seq"),
        P("dp", "seq"),
        P("dp", "seq"),
        P("pipe", None, None),
        P("pipe", None, None),
        P("pipe", None, None, None),
        P("pipe", None, None),
        P("pipe", None, None),
    )
    out_specs = (
        P("dp", "seq", "pipe"),
        P("dp", "seq", "pipe"),
        P("pipe", None, None),
        P("pipe", None, None),
        P("pipe", None, None, None),
        P("pipe", None, None),
        P("pipe", None, None),
        P(),
    )
    return jax.shard_map(shards, mesh=mesh, in_specs=in_specs, out_specs=out_specs, check_vma=False)
```

time: 2770 us -> 577 us (0.21); the launches traced: 2730 us -> 576 us
  other arithmetic: 833 us -> 31.8 us
  matrix products: 726 us -> 0 us
  local copies, waits for them, and re-layouts: 451 us -> 16.3 us
  starting transfers between devices: 395 us -> 20.4 us
  Pallas kernels: 0 us -> 183 us
  loops' own time: 29.2 us -> 0 us
    dot_general x225 -> x0, matrix products: 726 us -> none  [the longest x25 130 us: block_backward(): jnp.dot(hidden_low, narrow_w.T, preferred_element_type=jnp.float32)]
    ppermute x151 -> x15, starting transfers between devices: 395 us -> 20.3 us  [the longest x4 12.8 us: spread(): low = lax.ppermute(edges[1], 'seq', up)]
    reduce_sum x350 -> x8, other arithmetic: 341 us -> 0.82 us  [the longest x1 0.63 us: shards(): masked_count = jnp.sum(accuracy[1])]
    dynamic_update_slice x125 -> x0, other arithmetic: 248 us -> none  [place(): return lax.dynamic_update_index_in_dim(buffer, chosen, slot_index, 0)]
    pallas_call x0 -> x5, Pallas kernels: none -> 183 us  [__call__(): pl.pallas_call(kernel, grid_spec=pltpu.PrefetchScalarGridSpec(num_scalar_...]
    while x1075 -> x0, local copies, waits for them, and re-layouts: 174 us -> none
    dynamic_slice x100 -> x0, local copies, waits for them, and re-layouts: 153 us -> none  [place(): previous = lax.dynamic_index_in_dim(buffer, slot_index, 0, keepdims=False)]
    convert_element_type x100 -> x5, other arithmetic: 82.7 us -> 4.7 us  [shards(): jnp.where(core == 0, b, a).astype(bf16)]
  transfers between devices with their start and end apart: 152 -> 19, of which waited for: 26 -> 10; matrix products, arithmetic and copies ran while one was open for 25% -> 4% of each run, Pallas kernels for 0% -> 3%
where the time goes in v1:
time: 577 us; the launch traced here: 576 us
  waiting for transfers between devices  212 us (37%)
  Pallas kernels  183 us (32%)
  blocking collectives  97.2 us (17%)
  other arithmetic  31.8 us (6%)
  starting transfers between devices  20.4 us (4%)
  local copies, waits for them, and re-layouts  16.3 us (3%)
  between operations  15.1 us (3%)
    psum x1, waiting for transfers between devices, shards(): totals = lax.psum(mine, ('dp', 'seq'))  184 us
    pallas_call x5, Pallas kernels, __call__(): pl.pallas_call(kernel, grid_spec=pltpu.PrefetchScalarGridSpec(num_scalar_...  183 us
    psum x1, blocking collectives, shards(): totals = lax.psum(mine, ('dp', 'seq'))  77.1 us
    ppermute x4, waiting for transfers between devices, spread(): high = lax.ppermute(edges[0], 'seq', down)  16.8 us
    psum x1, blocking collectives, shards(): accuracy = lax.psum(jnp.stack([right_counts, masked_counts]), ('dp', 'seq'))  16.2 us
    select_n x2, other arithmetic, assembled(): jnp.where(core == 0, jnp.concatenate([own, arrived]), jnp.concatenate([ar...  14.5 us
    ppermute x4, starting transfers between devices, spread(): low = lax.ppermute(edges[1], 'seq', up)  12.8 us
    unnamed x55, local copies, waits for them, and re-layouts  11.7 us
  transfers between devices with their start and end apart: 19, of which 10 were waited for; matrix products, arithmetic and copies ran while one was open for 4% of the time, Pallas kernels for 3%

profile of v1, /device:TPU:0, one launch (start us, length us, event | category | flops | bytes accessed | tf_op | source)
XLA Modules:
  0.0 576.2 jit_solution(12511270662534566003)
XLA Ops:
  10.8 16.2 %psum.42 = s32[2,30]{1,0:T(2,128)S(1)} all-reduce(s32[2,30]{1,0:T(2,128)S(1)} %pad_add_fusion), channel_id=1, replica_groups=mesh['pipe'=2,'dp'=4,'seq'=4] {'dp','seq'}, use_global_device_ids=true, to_apply=%region_2.3 | all-reduce | flops 60 | bytes 480 | tf_op jit(solution)/shard_map/psum | solution.py:537
  30.9 15.1 %first_half.1 = (f32[12,256,512]{2,1,0:T(8,128)}, bf16[12,256,512]{2,1,0:T(8,128)(2,1)}, bf16[2,12,8,512]{3,2,1,0:T(8,128)(2,1)}) custom-call(s32[1]{0:T(128)} %bitcast.base_ref, bf16[24,256,1024]{2,1,0:T(8,128)(2,1)} %refs_0_.5, f32[2,3,1024]{2,1,0:T(4,128)} %all_gather.15.refs_1_.refs_3_.refs_7_.refs_5_.refs_8_, ...), custom_call_target="tpu_custom_call" | custom-call | tf_op jit(solution)/shard_map/first_half/pallas_call | solution.py:474
  47.0 3.5 collective-permute-start
  53.1 3.9 collective-permute-done.1
  57.7 32.0 %middle_half.1 = (f32[12,256,512]{2,1,0:T(8,128)}, f32[12,256,1024]{2,1,0:T(8,128)}, f32[12,256,512]{2,1,0:T(8,128)}, bf16[12,256,512]{2,1,0:T(8,128)(2,1)}, bf16[2,12,8,512]{3,2,1,0:T(8,128)(2,1)}) custom-call(s32[1]{0:T(128)} %bitcast.base_ref, bf16[24,256,1024]{2,1,0:T(8,128)(2,1)} %refs_0_.5, bf16[12,256,512]{2,1,0:T(8,128)(2,1)} %get-tuple-element.39.refs_1_.refs_3_, ...), custom_call_target="tpu_custom_call" | custom-call | tf_op jit(solution)/shard_map/middle_half/pallas_call | solution.py:474
  90.6 3.1 collective-permute-start.2
  96.0 4.3 collective-permute-done.3
  101.0 31.4 %turn.1 = (bf16[12,256,512]{2,1,0:T(8,128)(2,1)}, bf16[12,256,512]{2,1,0:T(8,128)(2,1)}, bf16[12,256,512]{2,1,0:T(8,128)(2,1)}, bf16[2,12,8,512]{3,2,1,0:T(8,128...) custom-call(s32[1]{0:T(128)} %bitcast.base_ref, f32[12,256,1024]{2,1,0:T(8,128)} %get-tuple-element.41.refs_0_, ...), custom_call_target="tpu_custom_call" | custom-call | tf_op jit(solution)/shard_map/turn/pallas_call | solution.py:474
  133.3 3.4 collective-permute-start.5
  138.9 4.3 collective-permute-done.6
  143.9 59.4 %between.1 = (f32[12,256,1024]{2,1,0:T(8,128)}, bf16[12,256,512]{2,1,0:T(8,128)(2,1)}, bf16[2,12,8,512]{3,2,1,0:T(8,128)(2,1)}, f32[1024,512]{1,0:T(8,128)}, f32...) custom-call(s32[1]{0:T(128)} %bitcast.base_ref, ...), custom_call_target="tpu_custom_call" | custom-call | tf_op jit(solution)/shard_map/between/pallas_call | solution.py:474
  204.3 2.8 collective-permute-start.7
  209.3 4.3 collective-permute-done.8
  214.4 45.5 %last_half.1 = (bf16[12,256,512]{2,1,0:T(8,128)(2,1)}, bf16[12,256,512]{2,1,0:T(8,128)(2,1)}, f32[1024,512]{1,0:T(8,128)}, f32[2560,512]{1,0:T(8,128)}, f32[16,1024]{1,0:T(8,128)}, /*index=5*/f32[24,512]{1,0:T(8,128)}) custom-call(s32[1]{0:T(128)} %bitcast.base_ref, bf16[24,256,1024]{2,1,0:T(8,128)(2,1)} %refs_0_.5, ...), custom_call_target="tpu_custom_call" | custom-call | tf_op jit(solution)/shard_map/last_half/pallas_call | solution.py:474
  259.9 3.6 select_convert_fusion
  266.5 3.6 collective-permute-done.13
  274.0 3.8 convert_add_fusion
  279.7 4.0 collective-permute-done.10
  283.7 77.1 %all-reduce = (f32[1,3,1024]{2,0,1:T(1,128)}, f32[1,6,512]{2,0,1:T(1,128)}) all-reduce(f32[1,3,1024]{2,0,1:T(1,128)S(1)} %broadcast_in_dim.45, f32[1,6,512]{2,0,1:T(1,128)S(1)} %broadcast_in_dim.48), channel_id=1, replica_groups=mesh['pipe'=2,'dp'=4,'seq'=4] {'dp','seq'}, use_global_device_ids=true, to_apply=%region_8.9 | all-reduce | flops 6144 | bytes 49152 | tf_op jit(solution)/shard_map/psum | solution.py:666
  360.8 7.1 %maximum_select_fusion = bf16[24,256,512]{2,1,0:T(8,128)(2,1)} fusion(bf16[12,256,512]{2,1,0:T(8,128)(2,1)} %collective-permute-done.4, bf16[12,256,512]{2,1,0:T(8,128)(2,1)S(1)} %copy-done.4, pred[]{:T(512)S(6)} %eq.10), kind=kLoop, calls=%fused_computation | loop fusion | flops 9437184 | bytes 12582913 | tf_op jit(solution)/shard_map/jit(_where)/select_n | solution.py:670
  367.9 7.5 %maximum_select_fusion.1 = bf16[24,256,512]{2,1,0:T(8,128)(2,1)} fusion(bf16[12,256,512]{2,1,0:T(8,128)(2,1)} %collective-permute-done.9, bf16[12,256,512]{2,1,0:T(8,128)(2,1)S(1)} %copy-done.5, pred[]{:T(512)S(6)} %eq.10), kind=kLoop, calls=%fused_computation.1 | loop fusion | flops 9437184 | bytes 12582913 | tf_op jit(solution)/shard_map/jit(_where)/select_n | solution.py:670
  375.4 184.0 %all-reduce.4.cloned.1.call-done = (f32[1,1024,512]{2,1,0:T(8,128)}, f32[1,5,512,512]{3,2,1,0:T(8,128)}, f32[1,512,1024]{2,1,0:T(8,128)}) async-done(((f32[1,1024,512]{2,1,0:T(8,128)}, f32[1,5,512,512]{3,2,1,0:T(8,128)}, f32[1,512,1024]{2,1,0:T(8,128)}), (f32[1,1024,512]{2,1,0:T(8,128)}, f32[1,5,512,512]{3,2,1,0:T(8,128)}, f32[1,512,1024]{2,1,0:T(8,128)})) %all-reduce.4.cloned.1.call-update) | async-done | bytes 9437200 | tf_op jit(solution)/shard_map/psum | solution.py:666
  559.3 3.1 copy.27
  562.4 6.0 %copy.28 = f32[1,5,512,512]{3,2,1,0:T(8,128)} copy(f32[1,5,512,512]{3,2,1,0:T(8,128)} %get-tuple-element.91) | data formatting | bytes 10485760
  (127 shorter events, 32.3 us)
Async XLA Ops:
  7.2 23.6 %all-gather.4.cloned.1.call-start = ((), (), s32[]{:S(2)}) async-start(), calls=%async_computation | async-start | bytes 3145728 | tf_op jit(solution)/shard_map/all_gather | solution.py:511
  8.0 49.7 %all-gather.8.cloned.1.call-start = ((), (), s32[]{:S(2)}) async-start(), calls=%async_computation.2 | async-start | bytes 3145728 | tf_op jit(solution)/shard_map/all_gather | solution.py:511
  8.7 49.0 %all-gather.6.cloned.1.call-start = ((), (), s32[]{:S(2)}) async-start(), calls=%async_computation.1 | async-start | bytes 7864320 | tf_op jit(solution)/shard_map/all_gather | solution.py:511
  9.4 549.9 %all-reduce.4.cloned.1.call-start = ((), (), s32[]{:S(2)}) async-start(), calls=%async_computation.3 | async-start | bytes 18874368 | tf_op jit(solution)/shard_map/psum | solution.py:666
  27.0 24.8 %copy-start.20 = (s32[2,30]{1,0:T(2,128)}, s32[2,30]{1,0:T(2,128)S(1)}, u32[]{:S(2)}) copy-start(s32[2,30]{1,0:T(2,128)S(1)} %psum.42) | copy-start | bytes 724
  47.0 6.1 %collective-permute-start = (bf16[12,8,512]{2,1,0:T(8,128)(2,1)S(1)}, bf16[12,8,512]{2,1,0:T(8,128)(2,1)S(1)}, u32[]{:S(2)}, u32[]{:S(2)}) collective-permute-start(bf16[12,8,512]{2,1,0:T(8,128)(2,1)S(1)} %get-tuple-element.83), channel_id=1, source_target_pairs={{0,1},{1,2},{2,3},{4,5},{5,6},{6,7},{8,9},{9,10},{10,11},{12,13},{... | collective-permute-start | bytes 294920 | tf_op jit(solution)/shard_map/ppermute | solution.py:501
  50.5 6.5 %collective-permute-start.1 = (bf16[12,8,512]{2,1,0:T(8,128)(2,1)S(1)}, bf16[12,8,512]{2,1,0:T(8,128)(2,1)S(1)}, u32[]{:S(2)}, u32[]{:S(2)}) collective-permute-start(bf16[12,8,512]{2,1,0:T(8,128)(2,1)S(1)} %get-tuple-element.84), channel_id=1, source_target_pairs={{1,0},{2,1},{3,2},{5,4},{6,5},{7,6},{9,8},{10,9},{11,10},{13,12},{... | collective-permute-start | bytes 294920 | tf_op jit(solution)/shard_map/ppermute | solution.py:502
  90.6 5.3 collective-permute-start.2
  93.8 6.5 %collective-permute-start.3 = (bf16[12,8,512]{2,1,0:T(8,128)(2,1)S(1)}, bf16[12,8,512]{2,1,0:T(8,128)(2,1)S(1)}, u32[]{:S(2)}, u32[]{:S(2)}) collective-permute-start(bf16[12,8,512]{2,1,0:T(8,128)(2,1)S(1)} %get-tuple-element.82), channel_id=1, source_target_pairs={{1,0},{2,1},{3,2},{5,4},{6,5},{7,6},{9,8},{10,9},{11,10},{13,12},{... | collective-permute-start | bytes 294920 | tf_op jit(solution)/shard_map/ppermute | solution.py:502
  133.3 5.6 collective-permute-start.5
  136.7 6.5 %collective-permute-start.6 = (bf16[12,8,512]{2,1,0:T(8,128)(2,1)S(1)}, bf16[12,8,512]{2,1,0:T(8,128)(2,1)S(1)}, u32[]{:S(2)}, u32[]{:S(2)}) collective-permute-start(bf16[12,8,512]{2,1,0:T(8,128)(2,1)S(1)} %get-tuple-element.80), channel_id=1, source_target_pairs={{1,0},{2,1},{3,2},{5,4},{6,5},{7,6},{9,8},{10,9},{11,10},{13,12},{... | collective-permute-start | bytes 294920 | tf_op jit(solution)/shard_map/ppermute | solution.py:502
  204.3 5.0 collective-permute-start.7
  207.1 6.5 %collective-permute-start.8 = (bf16[12,8,512]{2,1,0:T(8,128)(2,1)S(1)}, bf16[12,8,512]{2,1,0:T(8,128)(2,1)S(1)}, u32[]{:S(2)}, u32[]{:S(2)}) collective-permute-start(bf16[12,8,512]{2,1,0:T(8,128)(2,1)S(1)} %get-tuple-element.78), channel_id=1, source_target_pairs={{1,0},{2,1},{3,2},{5,4},{6,5},{7,6},{9,8},{10,9},{11,10},{13,12},{... | collective-permute-start | bytes 294920 | tf_op jit(solution)/shard_map/ppermute | solution.py:502
  263.6 10.4 %collective-permute-start.12 = (bf16[2560,512]{1,0:T(8,128)(2,1)S(1)}, bf16[2560,512]{1,0:T(8,128)(2,1)S(1)}, u32[]{:S(2)}, u32[]{:S(2)}) collective-permute-start(bf16[2560,512]{1,0:T(8,128)(2,1)S(1)} %select_convert_fusion), channel_id=1, source_target_pairs={{0,16},{16,0},{1,17},{17,1},{2,18},{18,2},{3,19},{19,3},{4,20},{20... | collective-permute-start | bytes 7864328 | tf_op jit(solution)/shard_map/ppermute | solution.py:507
  264.2 5.8 %collective-permute-start.13 = (bf16[512,1024]{1,0:T(8,128)(2,1)S(1)}, bf16[512,1024]{1,0:T(8,128)(2,1)S(1)}, u32[]{:S(2)}, u32[]{:S(2)}) collective-permute-start(bf16[512,1024]{1,0:T(8,128)(2,1)S(1)} %select_convert_fusion.1), channel_id=1, source_target_pairs={{0,16},{16,0},{1,17},{17,1},{2,18},{18,2},{3,19},{19,3},{4,20},{20... | collective-permute-start | bytes 3145736 | tf_op jit(solution)/shard_map/ppermute | solution.py:507
  265.8 8.1 %slice-start = ((s8[5242880]{0:T(1024)(128)(4,1)}), s8[4194304]{0:T(1024)(128)(4,1)S(1)}, s32[]{:S(2)}) async-start(s8[5242880]{0:T(1024)(128)(4,1)} %bitcast.46), calls=%async_computation.4 | async-start | bytes 8388608
  265.8 8.1 %slice-start.2 = ((s8[5242880]{0:T(1024)(128)(4,1)}), s8[4194304]{0:T(1024)(128)(4,1)S(1)}, s32[]{:S(2)}) async-start(s8[5242880]{0:T(1024)(128)(4,1)} %bitcast.48), calls=%async_computation.6 | async-start | bytes 8388608
  266.4 7.6 %slice-start.1 = ((s8[5242880]{0:T(1024)(128)(4,1)}), s8[1048576]{0:T(1024)(128)(4,1)S(1)}, s32[]{:S(2)}) async-start(s8[5242880]{0:T(1024)(128)(4,1)} %bitcast.46), calls=%async_computation.5 | async-start | bytes 2097152
  266.4 5.6 collective-permute-start.11
  277.9 83.0 %copy-start.4 = (bf16[12,256,512]{2,1,0:T(8,128)(2,1)S(1)}, bf16[12,256,512]{2,1,0:T(8,128)(2,1)}, u32[]{:S(2)}) copy-start(bf16[12,256,512]{2,1,0:T(8,128)(2,1)} %get-tuple-element.44) | copy-start | bytes 9437188
  277.9 82.9 %collective-permute-start.4 = (bf16[12,256,512]{2,1,0:T(8,128)(2,1)}, bf16[12,256,512]{2,1,0:T(8,128)(2,1)}, u32[]{:S(2)}, u32[]{:S(2)}) collective-permute-start(bf16[12,256,512]{2,1,0:T(8,128)(2,1)} %get-tuple-element.45), channel_id=1, source_target_pairs={{0,16},{16,0},{1,17},{17,1},{2,18},{18,2},{3,19},{19,3},{4,20},{20... | collective-permute-start | bytes 9437192 | tf_op jit(solution)/shard_map/ppermute | solution.py:507
  278.1 89.8 %collective-permute-start.9 = (bf16[12,256,512]{2,1,0:T(8,128)(2,1)}, bf16[12,256,512]{2,1,0:T(8,128)(2,1)}, u32[]{:S(2)}, u32[]{:S(2)}) collective-permute-start(bf16[12,256,512]{2,1,0:T(8,128)(2,1)} %get-tuple-element.55), channel_id=1, source_target_pairs={{0,16},{16,0},{1,17},{17,1},{2,18},{18,2},{3,19},{19,3},{4,20},{20... | collective-permute-start | bytes 9437192 | tf_op jit(solution)/shard_map/ppermute | solution.py:507
  279.0 4.6 collective-permute-start.10
  279.2 4.5 collective-permute-start.14
  (20 other events, 51.2 us)
Sparse Core Ops, SparseCore 0:
  9.6 13.2 all-gather.3
  24.5 11.7 all-gather.7
  37.8 16.3 all-gather.5
  278.0 281.2 all-reduce.3

commit v2 on v1

--- a/solution.py
+++ b/solution.py
@@ -149,6 +149,22 @@
         edge_ref[1, i] = second[rows - REACH :]
 
 
+def last_step():
+    return pl.program_id(0) == pl.num_programs(0) - 1
+
+
+def write_restore(out, total):
+    inner, width = total.shape
+    for j in range(width // inner):
+        out[j * inner : (j + 1) * inner, :] = total[:, j * inner : (j + 1) * inner].astype(bf16)
+
+
+def write_joined(out, narrow_sum, dilated_sum):
+    cut = narrow_sum.shape[0]
+    out[:cut, :] = narrow_sum[...].astype(bf16)
+    out[cut:, :] = dilated_sum[...].astype(bf16)
+
+
 def start_sums(refs):
     @pl.when(pl.program_id(0) == 0)
     def _():
@@ -181,10 +197,11 @@
     other_ref,
     gm_ref,
     edge_ref,
-    restore_sum,
+    restore_out,
     wide_sum,
     small_sum,
     pads,
+    restore_sum,
 ):
     rows = middle_ref.shape[1]
     inner = inner_ref.shape[-1]
@@ -207,6 +224,10 @@
         gm_ref[i] = gm
         edge_ref[0, i] = gm[:REACH]
         edge_ref[1, i] = gm[rows - REACH :]
+
+    @pl.when(last_step())
+    def _():
+        write_restore(restore_out, restore_sum)
 
 
 def block_out_back(back, grad_low, restore_ref, restore_sum, wide_sum, small_sum):
@@ -285,15 +306,17 @@
     gx_ref,
     lower_gm_ref,
     edge_ref,
-    narrow_sum,
-    dilated_sum,
+    joined_out,
     wide_sum,
     small_sum,
-    lower_restore_sum,
+    lower_restore_out,
     lower_wide_sum,
     lower_small_sum,
     pads,
     gm_pads,
+    narrow_sum,
+    dilated_sum,
+    lower_restore_sum,
 ):
     rows = middle_ref.shape[1]
     start_sums(
@@ -343,6 +366,11 @@
         edge_ref[0, i] = gm[:REACH]
         edge_ref[1, i] = gm[rows - REACH :]
 
+    @pl.when(last_step())
+    def _():
+        write_joined(joined_out, narrow_sum, dilated_sum)
+        write_restore(lower_restore_out, lower_restore_sum)
+
 
 def last_half(
     seqs,
@@ -360,12 +388,13 @@
     dilated_ref,
     own_ref,
     other_ref,
-    narrow_sum,
-    dilated_sum,
+    joined_out,
     wide_sum,
     small_sum,
     pads,
     gm_pads,
+    narrow_sum,
+    dilated_sum,
 ):
     half = own_ref.shape[-1]
     core = lax.axis_index("pipe")
@@ -397,6 +426,342 @@
         own_ref[i] = jnp.where(core == 0, left, right)
         other_ref[i] = jnp.where(core == 0, right, left)
 
+    @pl.when(last_step())
+    def _():
+        write_joined(joined_out, narrow_sum, dilated_sum)
+
+
+MESH = pl.DeviceIdType.MESH
+UNIT = 16
+
+
+def bits_of(count):
+    return count.bit_length() - 1
+
+
+def mixed_by(core, first, second):
+    return first + core * (second - first)
+
+
+class Place:
+    def __init__(self):
+        self.core = lax.axis_index("pipe")
+        self.seq = lax.axis_index("seq")
+        self.dp = lax.axis_index("dp")
+        seq_bits = bits_of(lax.axis_size("seq"))
+        dp_bits = bits_of(lax.axis_size("dp"))
+        order = list(range(seq_bits))
+        cut = seq_bits // 2
+        turned = order[cut:] + order[:cut]
+        self.stages = [("seq", a, b) for a, b in zip(order, turned)]
+        self.stages += [("dp", a, a) for a in range(dp_bits)]
+
+    def bit(self, stage):
+        axis, a, b = self.stages[stage]
+        spot = self.seq if axis == "seq" else self.dp
+        return mixed_by(self.core, (spot // (1 << a)) % 2, (spot // (1 << b)) % 2)
+
+    def peer(self, stage):
+        axis, a, b = self.stages[stage]
+        spot = self.seq if axis == "seq" else self.dp
+        hop = mixed_by(self.core, 1 << a, 1 << b) * (1 - 2 * self.bit(stage))
+        return {axis: spot + hop}
+
+    def other_core(self):
+        return {"pipe": 1 - self.core}
+
+    def greet(self):
+        barrier = pltpu.get_barrier_semaphore()
+        friends = [self.other_core()] + [self.peer(s) for s in range(len(self.stages))]
+        for friend in friends:
+            pl.semaphore_signal(barrier, inc=1, device_id=friend, device_id_type=MESH)
+        pl.semaphore_wait(barrier, len(friends))
+
+
+def remote(src, dst, send_sem, recv_sem, device):
+    return pltpu.make_async_remote_copy(
+        src_ref=src,
+        dst_ref=dst,
+        send_sem=send_sem,
+        recv_sem=recv_sem,
+        device_id=device,
+        device_id_type=MESH,
+    )
+
+
+def group_sizes(inner, width):
+    upper = KERNEL * inner // 2
+    return [upper - upper // 5 * 2, upper // 5 * 2, width // 2, width // 2]
+
+
+class BlockSum:
+    def __init__(self, place, block, sizes, joined, restore, out, room, sems):
+        self.place, self.block, self.sizes = place, block, sizes
+        self.joined, self.restore, self.out = joined, restore, out
+        self.own, self.theirs, self.acc, self.sbuf, self.rbuf, self.res = room
+        self.core_sems, self.load_sems, self.send_sems, self.recv_sems, self.out_sems = sems
+        self.levels = len(place.stages)
+        self.starts = [sum(sizes[:g]) for g in range(len(sizes))]
+        self.half = sum(sizes)
+
+    @staticmethod
+    def scratch(sizes, width, levels):
+        rows, groups = sum(sizes), len(sizes)
+        room = [
+            pltpu.VMEM((rows, width), bf16),
+            pltpu.VMEM((rows, width), bf16),
+            pltpu.VMEM((rows, width), f32),
+            pltpu.VMEM((groups, max(BlockSum.sent(n, levels) for n in sizes), width), bf16),
+            pltpu.VMEM((groups, max(BlockSum.sent(n, levels) for n in sizes), width), bf16),
+            pltpu.VMEM((rows, width), bf16),
+        ]
+        dma = pltpu.SemaphoreType.DMA
+        sems = [
+            dma((groups, 2)),
+            dma((groups,)),
+            dma((groups, 2 * levels)),
+            dma((groups, 2 * levels)),
+            dma((groups, 3)),
+        ]
+        return room, sems
+
+    @staticmethod
+    def lengths(rows, levels):
+        out = [rows]
+        for _ in range(levels):
+            last = out[-1]
+            out.append(last // 2 if last % (2 * UNIT) == 0 else last)
+        return out
+
+    @staticmethod
+    def sent(rows, levels):
+        return sum(BlockSum.lengths(rows, levels)[1:])
+
+    def spots(self, g):
+        lengths = self.lengths(self.sizes[g], self.levels)
+        start, out = self.starts[g], []
+        for s in range(self.levels):
+            out.append((start, lengths[s]))
+            if lengths[s + 1] < lengths[s]:
+                start = start + self.place.bit(s) * lengths[s + 1]
+        out.append((start, lengths[-1]))
+        return out
+
+    def source(self, g, half):
+        n, at = self.sizes[g], self.starts[g] + half * self.half
+        top = self.joined.shape[0]
+        if at < top:
+            return self.joined.at[pl.ds(at, n)]
+        return self.restore.at[pl.ds(at - top, n)]
+
+    def core_copy(self, g, half):
+        at = pl.ds(self.starts[g], self.sizes[g])
+        return remote(
+            self.source(g, half),
+            self.theirs.at[at],
+            self.core_sems.at[g, 0],
+            self.core_sems.at[g, 1],
+            self.place.other_core(),
+        )
+
+    def load(self, g, half):
+        at = pl.ds(self.starts[g], self.sizes[g])
+        return pltpu.make_async_copy(self.source(g, half), self.own.at[at], self.load_sems.at[g])
+
+    def down(self, g, s):
+        lengths = self.lengths(self.sizes[g], self.levels)
+        at = pl.ds(sum(lengths[1 : s + 1]), lengths[s + 1])
+        return remote(
+            self.sbuf.at[g, at],
+            self.rbuf.at[g, at],
+            self.send_sems.at[g, s],
+            self.recv_sems.at[g, s],
+            self.place.peer(s),
+        )
+
+    def start_down(self, g, s):
+        lengths = self.lengths(self.sizes[g], self.levels)
+        start, rows = self.spots(g)[s]
+        to, n = sum(lengths[1 : s + 1]), lengths[s + 1]
+        if n < rows:
+            start = start + (1 - self.place.bit(s)) * n
+        start = pl.multiple_of(start, UNIT)
+        self.sbuf[g, to : to + n, :] = self.acc[pl.ds(start, n), :].astype(bf16)
+        self.down(g, s).start()
+
+    def end_down(self, g, s):
+        lengths = self.lengths(self.sizes[g], self.levels)
+        at, n = sum(lengths[1 : s + 1]), lengths[s + 1]
+        start = pl.multiple_of(self.spots(g)[s + 1][0], UNIT)
+        self.down(g, s).wait()
+        kept = self.acc[pl.ds(start, n), :]
+        if n == lengths[s]:
+            kept = kept.astype(bf16).astype(f32)
+        self.acc[pl.ds(start, n), :] = kept + self.rbuf[g, at : at + n, :].astype(f32)
+
+    def up(self, g, s):
+        lengths = self.lengths(self.sizes[g], self.levels)
+        if lengths[s] == lengths[s + 1]:
+            return None
+        start, n = self.spots(g)[s + 1]
+        at = pl.ds(pl.multiple_of(start, UNIT), n)
+        return remote(
+            self.res.at[at],
+            self.res.at[at],
+            self.send_sems.at[g, self.levels + s],
+            self.recv_sems.at[g, self.levels + s],
+            self.place.peer(s),
+        )
+
+    def keep(self, g, half):
+        at = pl.ds(self.starts[g], self.sizes[g])
+        to = pl.ds(self.starts[g] + half * self.half, self.sizes[g])
+        return pltpu.make_async_copy(self.res.at[at], self.out.at[to], self.out_sems.at[g, 0])
+
+    def give(self, g, half):
+        at = pl.ds(self.starts[g], self.sizes[g])
+        to = pl.ds(self.starts[g] + half * self.half, self.sizes[g])
+        return remote(
+            self.res.at[at],
+            self.out.at[to],
+            self.out_sems.at[g, 1],
+            self.out_sems.at[g, 2],
+            self.place.other_core(),
+        )
+
+    def steps(self):
+        return 2 * self.levels + 3
+
+    def step(self, g, t):
+        core, levels = self.place.core, self.levels
+        if t == 0:
+            for half in (0, 1):
+
+                @pl.when(core == half)
+                def _():
+                    self.core_copy(g, 1 - half).start()
+                    self.load(g, half).start()
+
+        if t == 1:
+            for half in (0, 1):
+
+                @pl.when(core == half)
+                def _():
+                    self.load(g, half).wait()
+                    self.core_copy(g, 1 - half).wait()
+
+            at = slice(self.starts[g], self.starts[g] + self.sizes[g])
+            self.acc[at, :] = self.own[at, :].astype(f32) + self.theirs[at, :].astype(f32)
+        if 2 <= t < 2 + levels:
+            self.end_down(g, t - 2)
+        if 1 <= t < 1 + levels:
+            self.start_down(g, t - 1)
+        if t == 1 + levels:
+            start, n = self.spots(g)[levels]
+            at = pl.ds(pl.multiple_of(start, UNIT), n)
+            self.res[at, :] = self.acc[at, :].astype(bf16)
+        if 2 + levels <= t < 2 + 2 * levels:
+            copy = self.up(g, 2 * levels + 1 - t)
+            if copy is not None:
+                copy.wait()
+        if 1 + levels <= t < 1 + 2 * levels:
+            copy = self.up(g, 2 * levels - t)
+            if copy is not None:
+                copy.start()
+        if t == 1 + 2 * levels:
+            for half in (0, 1):
+
+                @pl.when(core == half)
+                def _():
+                    if half == self.block:
+                        self.keep(g, half).start()
+                    else:
+                        self.give(g, half).start()
+
+        if t == 2 + 2 * levels:
+            for half in (0, 1):
+
+                @pl.when(core == half)
+                def _():
+                    if half == self.block:
+                        self.keep(g, half).wait()
+                        self.give(g, 1 - half).wait_recv()
+                    else:
+                        self.give(g, half).wait_send()
+
+
+class SmallSum:
+    def __init__(self, place, total, arrived, sems):
+        self.place, self.total, self.arrived, self.sems = place, total, arrived, sems
+        self.stages = len(place.stages) + 1
+
+    @staticmethod
+    def scratch(rows, width, levels):
+        return [
+            pltpu.VMEM((levels + 2, rows, width), f32),
+            pltpu.VMEM((levels + 1, rows, width), f32),
+            pltpu.SemaphoreType.DMA((levels + 1, 2)),
+        ]
+
+    def copy(self, s):
+        device = self.place.other_core() if s == 0 else self.place.peer(s - 1)
+        return remote(
+            self.total.at[s], self.arrived.at[s], self.sems.at[s, 0], self.sems.at[s, 1], device
+        )
+
+    def start(self, s):
+        self.copy(s).start()
+
+    def end(self, s):
+        self.copy(s).wait()
+        self.total[s + 1] = self.total[s] + self.arrived[s]
+
+
+def gather_small(total, block, bias_ref, upper_ref, wide_ref, small_ref):
+    half = total.shape[-1]
+    rows = []
+    for ref in (wide_ref, bias_ref):
+        for k in range(ref.shape[0] // 8):
+            for lane in range(0, ref.shape[1], half):
+                rows.append((ref, k, lane))
+    for ref, k in ((small_ref, 0), (upper_ref, 0), (small_ref, 1), (small_ref, 2), (upper_ref, 1), (upper_ref, 2)):
+        rows.append((ref, k, 0))
+    for j, (ref, k, lane) in enumerate(rows):
+        piece = ref[8 * k : 8 * k + 8, lane : lane + half]
+        total[0, 16 * block + j : 16 * block + j + 1, :] = jnp.sum(piece, axis=0, keepdims=True)
+
+
+def sum_all(
+    sizes,
+    joined0,
+    restore0,
+    joined1,
+    restore1,
+    *refs,
+):
+    smalls, (out, small_out), scratch = refs[:8], refs[8:10], refs[10:]
+    place = Place()
+    place.greet()
+    levels = len(place.stages)
+    sets = [
+        BlockSum(place, 1, sizes, joined1, restore1, out, scratch[0:6], scratch[6:11]),
+        BlockSum(place, 0, sizes, joined0, restore0, out, scratch[11:17], scratch[17:22]),
+    ]
+    small = SmallSum(place, *scratch[22:])
+    small.total[0] = jnp.zeros_like(small.total[0])
+    for block in (0, 1):
+        gather_small(small.total, block, *smalls[4 * block : 4 * block + 4])
+    work = [(each, g) for each in sets for g in range(len(sizes))]
+    for t in range(len(work) + sets[0].steps() - 1):
+        if 0 < t <= small.stages:
+            small.end(t - 1)
+        if t < small.stages:
+            small.start(t)
+        for i, (each, g) in enumerate(work):
+            if 0 <= t - i < each.steps():
+                each.step(g, t - i)
+    small_out[...] = small.total[small.stages]
+
 
 class Caller:
     def __init__(self, name, seqs, count, base):
@@ -459,10 +824,14 @@
         self.outs.append(jax.ShapeDtypeStruct((2, self.count, REACH, width), bf16))
         return self
 
-    def out_sum(self, *shapes):
+    def out_sum(self, *shapes, dtype=f32):
         for shape in shapes:
             self.out_specs.append(pl.BlockSpec(shape, lambda i, b: (0, 0)))
-            self.outs.append(jax.ShapeDtypeStruct(shape, f32))
+            self.outs.append(jax.ShapeDtypeStruct(shape, dtype))
+        return self
+
+    def sums(self, *shapes):
+        self.scratch += [pltpu.VMEM(shape, f32) for shape in shapes]
         return self
 
     def pads(self, number, rows, width):
@@ -571,6 +940,8 @@
     )(without_base(middle_half, seqs, FIRST_DILATION))
     halo1 = spread(edge)
 
+    joined_rows = (width + KERNEL * inner, inner)
+    restore_rows = (width, inner)
     out_own, out_other, gm1, edge, restore_sum1, bias_sum1, upper_sum1 = (
         caller("turn", seqs)
         .seq(middle, second1)
@@ -579,8 +950,10 @@
         .block(1, outer2, inner2, dilated2, restore2)
         .out_seq(((rows, half), bf16), ((rows, half), bf16), ((rows, inner), bf16))
         .out_edge(inner)
-        .out_sum((inner, width), (8, width), (24, inner))
+        .out_sum(restore_rows, dtype=bf16)
+        .out_sum((8, width), (24, inner))
         .pads(1, rows, inner)
+        .sums((inner, width))
     )(without_base(turn, seqs, SECOND_DILATION))
     gm_halo1 = spread(edge)
 
@@ -588,8 +961,7 @@
         gx1,
         gm0,
         edge,
-        narrow_sum1,
-        dilated_sum1,
+        joined1,
         wide_sum1,
         small_sum1,
         restore_sum0,
@@ -608,20 +980,16 @@
         .block(0, inner2, restore2)
         .out_seq(((rows, width), f32), ((rows, inner), bf16))
         .out_edge(inner)
-        .out_sum(
-            (width, inner),
-            (KERNEL * inner, inner),
-            (16, width),
-            (24, inner),
-            (inner, width),
-            (8, width),
-            (24, inner),
-        )
+        .out_sum(joined_rows, dtype=bf16)
+        .out_sum((16, width), (24, inner))
+        .out_sum(restore_rows, dtype=bf16)
+        .out_sum((8, width), (24, inner))
         .pads(2, rows, inner)
+        .sums((width, inner), (KERNEL * inner, inner), (inner, width))
     )(without_base(between, seqs, SECOND_DILATION))
     gm_halo0 = spread(edge)
 
-    in_own, in_other, narrow_sum0, dilated_sum0, wide_sum0, small_sum0 = (
+    in_own, in_other, joined0, wide_sum0, small_sum0 = (
         caller("last_half", seqs)
         .own(inputs)
         .seq(gx1, hidden0, second0)
@@ -630,40 +998,49 @@
         .halo(gm_halo0)
         .block(0, outer2, inner2, narrow2, dilated2)
         .out_seq(((rows, half), bf16), ((rows, half), bf16))
-        .out_sum((width, inner), (KERNEL * inner, inner), (16, width), (24, inner))
+        .out_sum(joined_rows, dtype=bf16)
+        .out_sum((16, width), (24, inner))
         .pads(2, rows, inner)
+        .sums((width, inner), (KERNEL * inner, inner))
     )(without_base(last_half, seqs, FIRST_DILATION))
 
-    def small(bias_sum, upper_sum, wide_sum, small_sum):
-        def total(v):
-            return jnp.sum(v.reshape(-1, 8, v.shape[-1]), axis=1)
-
-        outer_grad = jnp.concatenate([total(wide_sum), total(bias_sum)])
-        upper_rows, lower_rows = total(upper_sum), total(small_sum)
-        inner_grad = jnp.stack(
-            [
-                lower_rows[0],
-                upper_rows[0],
-                lower_rows[1],
-                lower_rows[2],
-                upper_rows[1],
-                upper_rows[2],
-            ]
-        )
-        return outer_grad, inner_grad
-
-    smalls = [
-        small(bias_sum0, upper_sum0, wide_sum0, small_sum0),
-        small(bias_sum1, upper_sum1, wide_sum1, small_sum1),
-    ]
-    parts = (
-        (smalls[0][0], narrow_sum0, dilated_sum0, restore_sum0, smalls[0][1]),
-        (smalls[1][0], narrow_sum1, dilated_sum1, restore_sum1, smalls[1][1]),
+    sizes = group_sizes(inner, width)
+    levels = bits_of(lax.axis_size("seq")) + bits_of(lax.axis_size("dp"))
+    rooms = []
+    for _ in range(2):
+        room, sems = BlockSum.scratch(sizes, inner, levels)
+        rooms += room + sems
+    rooms += SmallSum.scratch(32, inner, levels)
+    anywhere, vmem = pl.BlockSpec(memory_space=pl.ANY), pl.BlockSpec(memory_space=pltpu.VMEM)
+    totals, smalls = pl.pallas_call(
+        functools.partial(sum_all, sizes),
+        out_shape=[
+            jax.ShapeDtypeStruct((2 * sum(sizes), inner), bf16),
+            jax.ShapeDtypeStruct((32, inner), f32),
+        ],
+        in_specs=[anywhere] * 4 + [vmem] * 8,
+        out_specs=[anywhere, vmem],
+        scratch_shapes=rooms,
+        compiler_params=pltpu.CompilerParams(
+            vmem_limit_bytes=VMEM_LIMIT, collective_id=0, has_side_effects=True
+        ),
+        name="sum_all",
+    )(
+        joined0,
+        restore_sum0,
+        joined1,
+        restore_sum1,
+        *(bias_sum0, upper_sum0, wide_sum0, small_sum0),
+        *(bias_sum1, upper_sum1, wide_sum1, small_sum1),
     )
-    mine = jax.tree.map(lambda a, b: jnp.where(core == 0, a, b), *parts)
-    theirs = jax.tree.map(lambda a, b: jnp.where(core == 0, b, a).astype(bf16), *parts)
-    mine = jax.tree.map(lambda a, b: a + swap(b).astype(f32), mine, theirs)
-    totals = lax.psum(mine, ("dp", "seq"))
+    totals = totals.astype(f32)
+    smalls = lax.dynamic_slice_in_dim(smalls, core * 16, 16, 0)
+    narrow_total = totals[:width]
+    dilated_total = totals[width : width + KERNEL * inner]
+    restore_total = totals[width + KERNEL * inner :].reshape(width // inner, inner, inner)
+    restore_total = jnp.concatenate(list(restore_total), axis=1)
+    outer_total = smalls[: 3 * width // inner].reshape(3, width)
+    inner_total = smalls[3 * width // inner :][:6]
 
     def assembled(own, other):
         arrived = swap(other)
@@ -676,11 +1053,11 @@
     return (
         assembled(out_own, out_other),
         assembled(in_own, in_other),
-        totals[0][None],
-        totals[1][None],
-        totals[2].reshape(1, KERNEL, inner, inner),
-        totals[3][None],
-        totals[4][None],
+        outer_total[None],
+        narrow_total[None],
+        dilated_total.reshape(1, KERNEL, inner, inner),
+        restore_total[None],
+        inner_total[None],
         accuracy,
     )
 

time: 577 us -> 411 us (0.71)
  waiting for transfers between devices: 212 us -> 20.5 us
  Pallas kernels: 183 us -> 298 us
  blocking collectives: 97.2 us -> 20.1 us
  other arithmetic: 31.8 us -> 23.9 us
    psum x1 -> x0, waiting for transfers between devices: 184 us -> none  [shards(): totals = lax.psum(mine, ('dp', 'seq'))]
    pallas_call x0 -> x1, Pallas kernels: none -> 112 us  [shards(): pl.pallas_call(functools.partial(sum_all, sizes), out_shape=[jax.ShapeDty...]
    psum x1 -> x0, blocking collectives: 77.1 us -> none  [shards(): totals = lax.psum(mine, ('dp', 'seq'))]
    unnamed x55 -> x23, local copies, waits for them, and re-layouts: 11.7 us -> 0.66 us
    ppermute x7 -> x2, waiting for transfers between devices: 7.56 us -> 0.01 us  [swap(): return lax.ppermute(values, 'pipe', [(0, 1), (1, 0)])]
  transfers between devices with their start and end apart: 19 -> 13, of which waited for: 10 -> 7; matrix products, arithmetic and copies ran while one was open for 4% -> 7% of each run, Pallas kernels for 3% -> 57%
where the time goes in v2:
time: 411 us; the launch traced here: 410 us
  Pallas kernels  298 us (73%)
  other arithmetic  23.9 us (6%)
  waiting for transfers between devices  20.5 us (5%)
  blocking collectives  20.1 us (5%)
  starting transfers between devices  18.7 us (5%)
  between operations  14.8 us (4%)
  local copies, waits for them, and re-layouts  13.7 us (3%)
    pallas_call x5, Pallas kernels, __call__(): pl.pallas_call(kernel, grid_spec=pltpu.PrefetchScalarGridSpec(num_scalar_...  186 us
    pallas_call x1, Pallas kernels, shards(): pl.pallas_call(functools.partial(sum_all, sizes), out_shape=[jax.ShapeDty...  112 us
    ppermute x4, waiting for transfers between devices, spread(): high = lax.ppermute(edges[0], 'seq', down)  16.8 us
    psum x1, blocking collectives, shards(): accuracy = lax.psum(jnp.stack([right_counts, masked_counts]), ('dp', 'seq'))  16.2 us
    ppermute x4, starting transfers between devices, spread(): low = lax.ppermute(edges[1], 'seq', up)  12.9 us
    select_n x2, other arithmetic, assembled(): jnp.where(core == 0, jnp.concatenate([own, arrived]), jnp.concatenate([ar...  10.3 us
  transfers between devices with their start and end apart: 13, of which 7 were waited for; matrix products, arithmetic and copies ran while one was open for 7% of the time, Pallas kernels for 57%

profile of v2, /device:TPU:0, one launch (start us, length us, event | category | flops | bytes accessed | tf_op | source)
XLA Modules:
  0.0 409.6 jit_solution(13491261716030600357)
XLA Ops:
  10.7 16.2 %psum.7 = s32[2,30]{1,0:T(2,128)S(1)} all-reduce(s32[2,30]{1,0:T(2,128)S(1)} %pad_add_fusion), channel_id=1, replica_groups=mesh['pipe'=2,'dp'=4,'seq'=4] {'dp','seq'}, use_global_device_ids=true, to_apply=%region_2.3 | all-reduce | flops 60 | bytes 480 | tf_op jit(solution)/shard_map/psum | solution.py:906
  26.9 2.0 all_gather.15.refs_1_.refs_3_.refs_7_.refs_5_.refs_8_
  28.9 2.0 all_gather.16.refs_2_.refs_4_.refs_8_.refs_6_.refs_9_.refs_13_
  30.8 15.1 %first_half.1 = (f32[12,256,512]{2,1,0:T(8,128)}, bf16[12,256,512]{2,1,0:T(8,128)(2,1)}, bf16[2,12,8,512]{3,2,1,0:T(8,128)(2,1)}) custom-call(s32[1]{0:T(128)} %bitcast.base_ref, bf16[24,256,1024]{2,1,0:T(8,128)(2,1)} %refs_0_.5, f32[2,3,1024]{2,1,0:T(4,128)} %all_gather.15.refs_1_.refs_3_.refs_7_.refs_5_.refs_8_, ...), custom_call_target="tpu_custom_call" | custom-call | tf_op jit(solution)/shard_map/first_half/pallas_call | solution.py:843
  46.9 3.5 collective-permute-start
  53.1 3.9 collective-permute-done.1
  57.7 32.0 %middle_half.1 = (f32[12,256,512]{2,1,0:T(8,128)}, f32[12,256,1024]{2,1,0:T(8,128)}, f32[12,256,512]{2,1,0:T(8,128)}, bf16[12,256,512]{2,1,0:T(8,128)(2,1)}, bf16[2,12,8,512]{3,2,1,0:T(8,128)(2,1)}) custom-call(s32[1]{0:T(128)} %bitcast.base_ref, bf16[24,256,1024]{2,1,0:T(8,128)(2,1)} %refs_0_.5, bf16[12,256,512]{2,1,0:T(8,128)(2,1)} %get-tuple-element.39.refs_1_.refs_3_, ...), custom_call_target="tpu_custom_call" | custom-call | tf_op jit(solution)/shard_map/middle_half/pallas_call | solution.py:843
  90.6 3.2 collective-permute-start.2
  96.0 4.3 %collective-permute-done.3 = bf16[12,8,512]{2,1,0:T(8,128)(2,1)S(1)} collective-permute-done((bf16[12,8,512]{2,1,0:T(8,128)(2,1)S(1)}, bf16[12,8,512]{2,1,0:T(8,128)(2,1)S(1)}, u32[]{:S(2)}, u32[]{:S(2)}) %collective-permute-start.3) | collective-permute-done | bytes 98336 | tf_op jit(solution)/shard_map/ppermute | solution.py:871
  101.0 32.5 %turn.1 = (bf16[12,256,512]{2,1,0:T(8,128)(2,1)}, bf16[12,256,512]{2,1,0:T(8,128)(2,1)}, bf16[12,256,512]{2,1,0:T(8,128)(2,1)}, bf16[2,12,8,512]{3,2,1,0:T(8,128...) custom-call(s32[1]{0:T(128)} %bitcast.base_ref, ...), custom_call_target="tpu_custom_call" | custom-call | tf_op jit(solution)/shard_map/turn/pallas_call | solution.py:843
  134.4 3.4 collective-permute-start.5
  140.0 4.3 %collective-permute-done.6 = bf16[12,8,512]{2,1,0:T(8,128)(2,1)S(1)} collective-permute-done((bf16[12,8,512]{2,1,0:T(8,128)(2,1)S(1)}, bf16[12,8,512]{2,1,0:T(8,128)(2,1)S(1)}, u32[]{:S(2)}, u32[]{:S(2)}) %collective-permute-start.6) | collective-permute-done | bytes 98336 | tf_op jit(solution)/shard_map/ppermute | solution.py:871
  145.0 60.2 %between.1 = (f32[12,256,1024]{2,1,0:T(8,128)}, bf16[12,256,512]{2,1,0:T(8,128)(2,1)}, bf16[2,12,8,512]{3,2,1,0:T(8,128)(2,1)}, bf16[3584,512]{1,0:T(8,128)(2,1)...) custom-call(s32[1]{0:T(128)} %bitcast.base_ref, ...), custom_call_target="tpu_custom_call" | custom-call | tf_op jit(solution)/shard_map/between/pallas_call | solution.py:843
  206.2 2.8 collective-permute-start.7
  209.0 1.5 collective-permute-start.8
  211.2 4.3 %collective-permute-done.8 = bf16[12,8,512]{2,1,0:T(8,128)(2,1)S(1)} collective-permute-done((bf16[12,8,512]{2,1,0:T(8,128)(2,1)S(1)}, bf16[12,8,512]{2,1,0:T(8,128)(2,1)S(1)}, u32[]{:S(2)}, u32[]{:S(2)}) %collective-permute-start.8) | collective-permute-done | bytes 98336 | tf_op jit(solution)/shard_map/ppermute | solution.py:871
  216.2 45.9 %last_half.1 = (bf16[12,256,512]{2,1,0:T(8,128)(2,1)}, bf16[12,256,512]{2,1,0:T(8,128)(2,1)}, bf16[3584,512]{1,0:T(8,128)(2,1)}, f32[16,1024]{1,0:T(8,128)}, f32[24,512]{1,0:T(8,128)}) custom-call(s32[1]{0:T(128)} %bitcast.base_ref, bf16[24,256,1024]{2,1,0:T(8,128)(2,1)} %refs_0_.5, f32[12,256,1024]{2,1,0:T(8,128)} %get-tuple-element.50.refs_1_, ...), custom_call_target="tpu_custom_call" | custom-call | tf_op jit(solution)/shard_map/last_half/pallas_call | solution.py:843
  262.3 112.4 %sum_all.1 = (bf16[4608,512]{1,0:T(8,128)(2,1)}, f32[32,512]{1,0:T(8,128)}) custom-call(bf16[3584,512]{1,0:T(8,128)(2,1)} %get-tuple-element.56.joined0, bf16[1024,512]{1,0:T(8,128)(2,1)} %get-tuple-element.57.restore0, bf16[3584,512]{1,0:T(8,128)(2,1)} %get-tuple-element.58.joined1, bf16[1024,512]{1,0:T(8,128)(2,1)} %get-tuple-element.59.restore1, ...), custom_call_target="tpu_custom_call" | custom-call | tf_op jit(solution)/shard_map/sum_all/pallas_call | solution.py:1015
  374.7 7.5 %convert_element_type.12 = f32[4608,512]{1,0:T(8,128)} convert(bf16[4608,512]{1,0:T(8,128)(2,1)} %get-tuple-element.69) | non-fusion elementwise | flops 2359296 | bytes 14155776 | tf_op jit(solution)/shard_map/convert_element_type | solution.py:1036
  382.2 3.1 slice.60
  386.5 1.5 fusion
  389.5 3.3 slice_bitcast_fusion
  392.8 3.5 maximum_select_fusion
  396.3 6.8 %maximum_select_fusion.1 = bf16[24,256,512]{2,1,0:T(8,128)(2,1)} fusion(bf16[12,256,512]{2,1,0:T(8,128)(2,1)} %collective-permute-done.9, bf16[12,256,512]{2,1,0:T(8,128)(2,1)S(1)} %copy-done.2, pred[]{:T(512)S(6)} %eq.20), kind=kLoop, calls=%fused_computation.1 | loop fusion | flops 9437184 | bytes 12582913 | tf_op jit(solution)/shard_map/jit(_where)/select_n | solution.py:1047
  (60 shorter events, 19.8 us)
Async XLA Ops:
  7.2 2.3 copy-start.7
  7.2 2.3 copy-start.8
  7.2 2.3 copy-start.3
  7.2 2.3 copy-start.4
  7.2 2.3 copy-start.5
  7.2 23.6 %all-gather.4.cloned.1.call-start = ((), (), s32[]{:S(2)}) async-start(), calls=%async_computation | async-start | bytes 3145728 | tf_op jit(solution)/shard_map/all_gather | solution.py:880
  8.0 49.7 %all-gather.8.cloned.1.call-start = ((), (), s32[]{:S(2)}) async-start(), calls=%async_computation.2 | async-start | bytes 3145728 | tf_op jit(solution)/shard_map/all_gather | solution.py:880
  8.7 49.0 %all-gather.6.cloned.1.call-start = ((), (), s32[]{:S(2)}) async-start(), calls=%async_computation.1 | async-start | bytes 7864320 | tf_op jit(solution)/shard_map/all_gather | solution.py:880
  26.9 24.8 %copy-start.9 = (s32[2,30]{1,0:T(2,128)}, s32[2,30]{1,0:T(2,128)S(1)}, u32[]{:S(2)}) copy-start(s32[2,30]{1,0:T(2,128)S(1)} %psum.7) | copy-start | bytes 724
  46.9 6.1 %collective-permute-start = (bf16[12,8,512]{2,1,0:T(8,128)(2,1)S(1)}, bf16[12,8,512]{2,1,0:T(8,128)(2,1)S(1)}, u32[]{:S(2)}, u32[]{:S(2)}) collective-permute-start(bf16[12,8,512]{2,1,0:T(8,128)(2,1)S(1)} %get-tuple-element.112), channel_id=1, source_target_pairs={{0,1},{1,2},{2,3},{4,5},{5,6},{6,7},{8,9},{9,10},{10,11},{12,13},{... | collective-permute-start | bytes 294920 | tf_op jit(solution)/shard_map/ppermute | solution.py:870
  50.4 6.5 %collective-permute-start.1 = (bf16[12,8,512]{2,1,0:T(8,128)(2,1)S(1)}, bf16[12,8,512]{2,1,0:T(8,128)(2,1)S(1)}, u32[]{:S(2)}, u32[]{:S(2)}) collective-permute-start(bf16[12,8,512]{2,1,0:T(8,128)(2,1)S(1)} %get-tuple-element.113), channel_id=1, source_target_pairs={{1,0},{2,1},{3,2},{5,4},{6,5},{7,6},{9,8},{10,9},{11,10},{13,12},{... | collective-permute-start | bytes 294920 | tf_op jit(solution)/shard_map/ppermute | solution.py:871
  90.6 5.4 %collective-permute-start.2 = (bf16[12,8,512]{2,1,0:T(8,128)(2,1)S(1)}, bf16[12,8,512]{2,1,0:T(8,128)(2,1)S(1)}, u32[]{:S(2)}, u32[]{:S(2)}) collective-permute-start(bf16[12,8,512]{2,1,0:T(8,128)(2,1)S(1)} %get-tuple-element.110), channel_id=1, source_target_pairs={{0,1},{1,2},{2,3},{4,5},{5,6},{6,7},{8,9},{9,10},{10,11},{12,13},{... | collective-permute-start | bytes 294920 | tf_op jit(solution)/shard_map/ppermute | solution.py:870
  93.8 6.5 %collective-permute-start.3 = (bf16[12,8,512]{2,1,0:T(8,128)(2,1)S(1)}, bf16[12,8,512]{2,1,0:T(8,128)(2,1)S(1)}, u32[]{:S(2)}, u32[]{:S(2)}) collective-permute-start(bf16[12,8,512]{2,1,0:T(8,128)(2,1)S(1)} %get-tuple-element.111), channel_id=1, source_target_pairs={{1,0},{2,1},{3,2},{5,4},{6,5},{7,6},{9,8},{10,9},{11,10},{13,12},{... | collective-permute-start | bytes 294920 | tf_op jit(solution)/shard_map/ppermute | solution.py:871
  134.4 5.6 %collective-permute-start.5 = (bf16[12,8,512]{2,1,0:T(8,128)(2,1)S(1)}, bf16[12,8,512]{2,1,0:T(8,128)(2,1)S(1)}, u32[]{:S(2)}, u32[]{:S(2)}) collective-permute-start(bf16[12,8,512]{2,1,0:T(8,128)(2,1)S(1)} %get-tuple-element.108), channel_id=1, source_target_pairs={{0,1},{1,2},{2,3},{4,5},{5,6},{6,7},{8,9},{9,10},{10,11},{12,13},{... | collective-permute-start | bytes 294920 | tf_op jit(solution)/shard_map/ppermute | solution.py:870
  137.8 6.5 %collective-permute-start.6 = (bf16[12,8,512]{2,1,0:T(8,128)(2,1)S(1)}, bf16[12,8,512]{2,1,0:T(8,128)(2,1)S(1)}, u32[]{:S(2)}, u32[]{:S(2)}) collective-permute-start(bf16[12,8,512]{2,1,0:T(8,128)(2,1)S(1)} %get-tuple-element.109), channel_id=1, source_target_pairs={{1,0},{2,1},{3,2},{5,4},{6,5},{7,6},{9,8},{10,9},{11,10},{13,12},{... | collective-permute-start | bytes 294920 | tf_op jit(solution)/shard_map/ppermute | solution.py:871
  139.3 253.5 %collective-permute-start.4 = (bf16[12,256,512]{2,1,0:T(8,128)(2,1)}, bf16[12,256,512]{2,1,0:T(8,128)(2,1)S(1)}, u32[]{:S(2)}, u32[]{:S(2)}) collective-permute-start(bf16[12,256,512]{2,1,0:T(8,128)(2,1)} %get-tuple-element.45), channel_id=1, source_target_pairs={{0,16},{16,0},{1,17},{17,1},{2,18},{18,2},{3,19},{19,3},{4,20},{20... | collective-permute-start | bytes 9437192 | tf_op jit(solution)/shard_map/ppermute | solution.py:876
  206.2 5.0 %collective-permute-start.7 = (bf16[12,8,512]{2,1,0:T(8,128)(2,1)S(1)}, bf16[12,8,512]{2,1,0:T(8,128)(2,1)S(1)}, u32[]{:S(2)}, u32[]{:S(2)}) collective-permute-start(bf16[12,8,512]{2,1,0:T(8,128)(2,1)S(1)} %get-tuple-element.106), channel_id=1, source_target_pairs={{0,1},{1,2},{2,3},{4,5},{5,6},{6,7},{8,9},{9,10},{10,11},{12,13},{... | collective-permute-start | bytes 294920 | tf_op jit(solution)/shard_map/ppermute | solution.py:870
  209.0 6.5 %collective-permute-start.8 = (bf16[12,8,512]{2,1,0:T(8,128)(2,1)S(1)}, bf16[12,8,512]{2,1,0:T(8,128)(2,1)S(1)}, u32[]{:S(2)}, u32[]{:S(2)}) collective-permute-start(bf16[12,8,512]{2,1,0:T(8,128)(2,1)S(1)} %get-tuple-element.107), channel_id=1, source_target_pairs={{1,0},{2,1},{3,2},{5,4},{6,5},{7,6},{9,8},{10,9},{11,10},{13,12},{... | collective-permute-start | bytes 294920 | tf_op jit(solution)/shard_map/ppermute | solution.py:871
  262.2 134.1 %collective-permute-start.9 = (bf16[12,256,512]{2,1,0:T(8,128)(2,1)}, bf16[12,256,512]{2,1,0:T(8,128)(2,1)}, u32[]{:S(2)}, u32[]{:S(2)}) collective-permute-start(bf16[12,256,512]{2,1,0:T(8,128)(2,1)} %get-tuple-element.55), channel_id=1, source_target_pairs={{0,16},{16,0},{1,17},{17,1},{2,18},{18,2},{3,19},{19,3},{4,20},{20... | collective-permute-start | bytes 9437192 | tf_op jit(solution)/shard_map/ppermute | solution.py:876
  374.7 7.5 %copy-start = (bf16[4608,512]{1,0:T(8,128)(2,1)S(1)}, bf16[4608,512]{1,0:T(8,128)(2,1)}, u32[]{:S(2)}) copy-start(bf16[4608,512]{1,0:T(8,128)(2,1)} %get-tuple-element.69) | copy-start | bytes 14155780
  382.2 3.1 copy-start.6
  388.0 4.8 %copy-start.1 = (bf16[12,256,512]{2,1,0:T(8,128)(2,1)S(1)}, bf16[12,256,512]{2,1,0:T(8,128)(2,1)}, u32[]{:S(2)}) copy-start(bf16[12,256,512]{2,1,0:T(8,128)(2,1)} %get-tuple-element.44) | copy-start | bytes 9437188
  392.8 3.5 copy-start.2
Sparse Core Ops, SparseCore 0:
  9.6 13.2 all-gather.3
  24.4 11.7 all-gather.7
  37.8 16.3 all-gather.5

commit v3 on v2

--- a/solution.py
+++ b/solution.py
@@ -97,20 +97,139 @@
     return ref[0, i : i + 1, :]
 
 
-def first_half(seqs, x_ref, outer_ref, inner_ref, narrow_ref, hidden_ref, second_ref, edge_ref):
-    rows = x_ref.shape[1]
+def step_of(seqs, i):
+    return pl.program_id(0) * seqs + i
+
+
+def first_half(
+    seqs,
+    count,
+    x_ref,
+    counts_ref,
+    outer,
+    inner,
+    narrow,
+    dilated,
+    restore,
+    hidden_ref,
+    second_ref,
+    total_ref,
+    halo_out,
+    outer2,
+    inner2,
+    narrow2,
+    dilated2,
+    restore2,
+    outer_s,
+    inner_s,
+    narrow_s,
+    outer_p,
+    inner_p,
+    narrow_p,
+    restore_s,
+    dilated_s,
+    param_sems,
+    edges,
+    zeros,
+    halo_sems,
+    zero_sems,
+    *sum_room,
+):
+    place = Place()
+    halo = Halo(place, count, edges, zeros, halo_out, halo_sems, zero_sems)
+    small = SmallSum(place, *sum_room)
+    step = pl.program_id(0)
+    params = ((outer, outer2), (inner, inner2), (narrow, narrow2), (restore, restore2), (dilated, dilated2))
+    shadows = (outer_s, inner_s, narrow_s)
+
+    through = (outer_p, inner_p, narrow_p, restore_s, dilated_s)
+
+    def local(k, passing):
+        dst = params[k][1].at[pl.ds(place.core, 1)]
+        return pltpu.make_async_copy(passing, dst, param_sems.at[0, k])
+
+    def away(k):
+        src, dst = params[k]
+        return remote(
+            src,
+            dst.at[pl.ds(place.core, 1)],
+            param_sems.at[1, k],
+            param_sems.at[2, k],
+            place.other_core(),
+        )
+
+    @pl.when(step == 0)
+    def _():
+        place.greet(place.line() + place.partners())
+        for k in range(len(params)):
+            away(k).start()
+        for k, shadow in enumerate(shadows):
+            load = param_sems.at[3, k]
+
+            @pl.when(place.core == 0)
+            def _():
+                pltpu.make_async_copy(params[k][0], shadow, load).start()
+
+        for k, shadow in enumerate(shadows):
+            load = param_sems.at[3, k]
+
+            @pl.when(place.core == 1)
+            def _():
+                away(k).wait_recv()
+                pltpu.make_async_copy(params[k][1].at[0:1], shadow, load).start()
+
+        for k in range(len(params)):
+            pltpu.make_async_copy(params[k][0], through[k], param_sems.at[0, k]).start()
+        for k, shadow in enumerate(shadows):
+            pltpu.make_async_copy(params[k][0], shadow, param_sems.at[3, k]).wait()
+        small.total[1] = counts_ref[...]
+        halo.begin()
+
+    @pl.when(step == 2)
+    def _():
+        for k in range(len(params)):
+            pltpu.make_async_copy(params[k][0], through[k], param_sems.at[0, k]).wait()
+            local(k, through[k]).start()
+
+    for k in range(1, small.stages):
+
+        @pl.when(step == k - 1)
+        def _():
+            if k > 1:
+                small.end(k - 1)
+            small.start(k)
+
     for i in range(seqs):
-        act = norm_act(x_ref[i].astype(f32), row(outer_ref, 0), row(outer_ref, 1))
-        hidden = dot(act, narrow_ref[0]) + row(inner_ref, 0)
+        at = step_of(seqs, i)
+        act = norm_act(x_ref[i].astype(f32), row(outer_s, 0), row(outer_s, 1))
+        hidden = dot(act, narrow_s[0]) + row(inner_s, 0)
         hidden_ref[i] = hidden
-        second = norm_act(hidden, row(inner_ref, 2), row(inner_ref, 3))
+        second = norm_act(hidden, row(inner_s, 2), row(inner_s, 3))
         second_ref[i] = second
-        edge_ref[0, i] = second[:REACH]
-        edge_ref[1, i] = second[rows - REACH :]
+        halo.send(at, second)
+
+    @pl.when(last_step())
+    def _():
+        small.end(small.stages - 1)
+        total_ref[...] = small.total[small.stages]
+        for k in range(len(params)):
+            local(k, through[k]).wait()
+            away(k).wait_send()
+
+            if k < len(shadows):
+
+                @pl.when(place.core == 0)
+                def _():
+                    away(k).wait_recv()
+            else:
+                away(k).wait_recv()
+
+        halo.end()
 
 
 def middle_half(
     seqs,
+    count,
     d,
     x_ref,
     second_ref,
@@ -126,11 +245,13 @@
     middle_ref,
     hidden_ref,
     next_second_ref,
-    edge_ref,
+    halo_out,
     pads,
+    *halo_room,
 ):
     rows = x_ref.shape[1]
     inner = inner_ref.shape[-1]
+    halo = halo_of(count, halo_out, halo_room)
     for i in range(seqs):
         pad = pads.at[i]
         fill(pad, halo_ref[0, i], second_ref.at[i], halo_ref[1, i])
@@ -145,8 +266,8 @@
         hidden_ref[i] = hidden
         second = norm_act(hidden, row(next_inner_ref, 2), row(next_inner_ref, 3))
         next_second_ref[i] = second
-        edge_ref[0, i] = second[:REACH]
-        edge_ref[1, i] = second[rows - REACH :]
+        halo.send(step_of(seqs, i), second)
+    halo.end_last()
 
 
 def last_step():
@@ -183,6 +304,7 @@
 
 def turn(
     seqs,
+    count,
     d,
     middle_ref,
     second_ref,
@@ -193,21 +315,21 @@
     inner_ref,
     dilated_ref,
     restore_ref,
-    own_ref,
-    other_ref,
     gm_ref,
-    edge_ref,
     restore_out,
     wide_sum,
     small_sum,
+    halo_out,
+    final_out,
     pads,
     restore_sum,
+    *rooms,
 ):
     rows = middle_ref.shape[1]
     inner = inner_ref.shape[-1]
-    half = own_ref.shape[-1]
-    core = lax.axis_index("pipe")
     start_sums((restore_sum, wide_sum, small_sum))
+    halo = halo_of(count, halo_out, rooms[:4], ahead=True)
+    halves = Halves(halo.place, count, final_out, *rooms[4:])
     for i in range(seqs):
         pad = pads.at[i]
         fill(pad, halo_ref[0, i], second_ref.at[i], halo_ref[1, i])
@@ -215,19 +337,18 @@
         mixed = dot(windows, dilated_ref[0].reshape(KERNEL * inner, inner)) + row(inner_ref, 1)
         back = Back(mixed, row(inner_ref, 4), row(inner_ref, 5))
         y = middle_ref[i] + (dot(back.act, restore_ref[0]) + row(outer_ref, 2))
-        y = y.astype(bf16)
-        left, right = y[:, :half], y[:, half:]
-        own_ref[i] = jnp.where(core == 0, left, right)
-        other_ref[i] = jnp.where(core == 0, right, left)
+        halves.send(step_of(seqs, i), y.astype(bf16))
         grad_low = seeded(cot_ref[i], flags_ref[i]).astype(bf16)
         gm = block_out_back(back, grad_low, restore_ref, restore_sum, wide_sum, small_sum)
         gm_ref[i] = gm
-        edge_ref[0, i] = gm[:REACH]
-        edge_ref[1, i] = gm[rows - REACH :]
+        halo.send(step_of(seqs, i), gm)
 
     @pl.when(last_step())
     def _():
         write_restore(restore_out, restore_sum)
+        halves.end()
+
+    halo.end_last()
 
 
 def block_out_back(back, grad_low, restore_ref, restore_sum, wide_sum, small_sum):
@@ -287,6 +408,7 @@
 
 def between(
     seqs,
+    count,
     d,
     middle_ref,
     cot_ref,
@@ -305,20 +427,21 @@
     lower_restore_ref,
     gx_ref,
     lower_gm_ref,
-    edge_ref,
     joined_out,
     wide_sum,
     small_sum,
     lower_restore_out,
     lower_wide_sum,
     lower_small_sum,
+    halo_out,
     pads,
     gm_pads,
     narrow_sum,
     dilated_sum,
     lower_restore_sum,
+    *halo_room,
 ):
-    rows = middle_ref.shape[1]
+    halo = halo_of(count, halo_out, halo_room)
     start_sums(
         (
             narrow_sum,
@@ -363,17 +486,19 @@
             lower_small_sum,
         )
         lower_gm_ref[i] = gm
-        edge_ref[0, i] = gm[:REACH]
-        edge_ref[1, i] = gm[rows - REACH :]
+        halo.send(step_of(seqs, i), gm)
 
     @pl.when(last_step())
     def _():
         write_joined(joined_out, narrow_sum, dilated_sum)
         write_restore(lower_restore_out, lower_restore_sum)
 
+    halo.end_last()
+
 
 def last_half(
     seqs,
+    count,
     d,
     x_ref,
     gx_ref,
@@ -386,18 +511,23 @@
     inner_ref,
     narrow_ref,
     dilated_ref,
-    own_ref,
-    other_ref,
     joined_out,
     wide_sum,
     small_sum,
+    final_out,
     pads,
     gm_pads,
     narrow_sum,
     dilated_sum,
+    *room,
 ):
-    half = own_ref.shape[-1]
-    core = lax.axis_index("pipe")
+    place = Place()
+    halves = Halves(place, count, final_out, *room)
+
+    @pl.when(pl.program_id(0) == 0)
+    def _():
+        place.greet([place.other_core()])
+
     start_sums((narrow_sum, dilated_sum, wide_sum, small_sum))
     for i in range(seqs):
         gx = block_in_back(
@@ -421,14 +551,12 @@
             pads.at[i],
             gm_pads.at[i],
         )
-        gx = gx.astype(bf16)
-        left, right = gx[:, :half], gx[:, half:]
-        own_ref[i] = jnp.where(core == 0, left, right)
-        other_ref[i] = jnp.where(core == 0, right, left)
+        halves.send(step_of(seqs, i), gx.astype(bf16))
 
     @pl.when(last_step())
     def _():
         write_joined(joined_out, narrow_sum, dilated_sum)
+        halves.end()
 
 
 MESH = pl.DeviceIdType.MESH
@@ -470,9 +598,15 @@
     def other_core(self):
         return {"pipe": 1 - self.core}
 
-    def greet(self):
+    def partners(self):
+        return [self.other_core()] + [self.peer(s) for s in range(len(self.stages))]
+
+    def line(self):
+        n = lax.axis_size("seq")
+        return [{"seq": (self.seq + 1) % n}, {"seq": (self.seq + n - 1) % n}]
+
+    def greet(self, friends):
         barrier = pltpu.get_barrier_semaphore()
-        friends = [self.other_core()] + [self.peer(s) for s in range(len(self.stages))]
         for friend in friends:
             pl.semaphore_signal(barrier, inc=1, device_id=friend, device_id_type=MESH)
         pl.semaphore_wait(barrier, len(friends))
@@ -487,6 +621,161 @@
         device_id=device,
         device_id_type=MESH,
     )
+
+
+class Halo:
+    def __init__(self, place, count, edges, zeros, halo, sems, zero_sems):
+        self.place, self.count, self.edges, self.zeros = place, count, edges, zeros
+        self.halo, self.sems, self.zero_sems = halo, sems, zero_sems
+        self.has_low = place.seq > 0
+        self.has_high = place.seq < lax.axis_size("seq") - 1
+
+    @staticmethod
+    def scratch(count, width):
+        return [
+            pltpu.VMEM((2, count, REACH, width), bf16),
+            pltpu.VMEM((count, REACH, width), bf16),
+            pltpu.SemaphoreType.DMA((4, count)),
+            pltpu.SemaphoreType.DMA((2,)),
+        ]
+
+    def up(self, i):
+        device = {"seq": self.place.seq + 1}
+        sems = self.sems
+        return remote(self.edges.at[1, i], self.halo.at[0, i], sems.at[0, i], sems.at[1, i], device)
+
+    def down(self, i):
+        device = {"seq": self.place.seq - 1}
+        sems = self.sems
+        return remote(self.edges.at[0, i], self.halo.at[1, i], sems.at[2, i], sems.at[3, i], device)
+
+    def blank(self, side):
+        return pltpu.make_async_copy(self.zeros, self.halo.at[side], self.zero_sems.at[side])
+
+    def begin(self):
+        self.zeros[...] = jnp.zeros_like(self.zeros)
+
+        @pl.when(jnp.logical_not(self.has_low))
+        def _():
+            self.blank(0).start()
+
+        @pl.when(jnp.logical_not(self.has_high))
+        def _():
+            self.blank(1).start()
+
+    def send(self, i, values):
+        self.edges[0, i] = values[:REACH]
+        self.edges[1, i] = values[values.shape[0] - REACH :]
+
+        @pl.when(self.has_high)
+        def _():
+            self.up(i).start()
+
+        @pl.when(self.has_low)
+        def _():
+            self.down(i).start()
+
+    def end(self):
+        @pl.when(jnp.logical_not(self.has_low))
+        def _():
+            self.blank(0).wait()
+
+        @pl.when(jnp.logical_not(self.has_high))
+        def _():
+            self.blank(1).wait()
+
+        @pl.when(self.has_high)
+        def _():
+            def body(i, carry):
+                self.up(i).wait_send()
+                self.down(i).wait_recv()
+                return carry
+
+            lax.fori_loop(0, self.count, body, 0)
+
+        @pl.when(self.has_low)
+        def _():
+            def body(i, carry):
+                self.down(i).wait_send()
+                self.up(i).wait_recv()
+                return carry
+
+            lax.fori_loop(0, self.count, body, 0)
+
+    def end_last(self):
+        @pl.when(last_step())
+        def _():
+            self.end()
+
+
+def halo_of(count, halo_out, room, ahead=False):
+    place = Place()
+    halo = Halo(place, count, room[0], room[1], halo_out, room[2], room[3])
+
+    @pl.when(pl.program_id(0) == 0)
+    def _():
+        place.greet(place.line() + ([place.other_core()] if ahead else []))
+        halo.begin()
+
+    return halo
+
+
+class Halves:
+    def __init__(self, place, count, out, own, other, sems, arrivals):
+        self.place, self.count, self.out = place, count, out
+        self.own, self.other, self.sems, self.arrivals = own, other, sems, arrivals
+
+    @staticmethod
+    def scratch(count, rows, half):
+        return [
+            pltpu.VMEM((2, rows, half), bf16),
+            pltpu.VMEM((2, rows, half), bf16),
+            pltpu.SemaphoreType.DMA((2, 2)),
+            pltpu.SemaphoreType.DMA((count,)),
+        ]
+
+    def local(self, i, slot):
+        to = self.place.core * self.count + i
+        return pltpu.make_async_copy(self.own.at[slot], self.out.at[to], self.sems.at[0, slot])
+
+    def away(self, i, slot):
+        to = self.place.core * self.count + i
+        return remote(
+            self.other.at[slot],
+            self.out.at[to],
+            self.sems.at[1, slot],
+            self.arrivals.at[i],
+            self.place.other_core(),
+        )
+
+    def release(self, i, slot):
+        self.local(i, slot).wait()
+        self.away(i, slot).wait_send()
+
+    def send(self, i, values):
+        slot = i % 2
+        half = values.shape[1] // 2
+        left, right = values[:, :half], values[:, half:]
+
+        @pl.when(i >= 2)
+        def _():
+            self.release(i - 2, slot)
+
+        first = self.place.core == 0
+        self.own[slot] = jnp.where(first, left, right)
+        self.other[slot] = jnp.where(first, right, left)
+        self.local(i, slot).start()
+        self.away(i, slot).start()
+
+    def end(self):
+        for i in range(max(0, self.count - 2), self.count):
+            self.release(i, i % 2)
+
+        def body(i, carry):
+            self.away(i, 0).wait_recv()
+            return carry
+
+        lax.fori_loop(0, self.count, body, 0)
 
 
 def group_sizes(inner, width):
@@ -613,17 +902,23 @@
             self.place.peer(s),
         )
 
+    def target(self, g, half):
+        n, at = self.sizes[g], self.starts[g] + half * self.half
+        joined, restore = self.out
+        top = joined.shape[0]
+        if at < top:
+            return joined.at[pl.ds(at, n)]
+        return restore.at[:, pl.ds(at - top, n)]
+
     def keep(self, g, half):
         at = pl.ds(self.starts[g], self.sizes[g])
-        to = pl.ds(self.starts[g] + half * self.half, self.sizes[g])
-        return pltpu.make_async_copy(self.res.at[at], self.out.at[to], self.out_sems.at[g, 0])
+        return pltpu.make_async_copy(self.res.at[at], self.target(g, half), self.out_sems.at[g, 0])
 
     def give(self, g, half):
         at = pl.ds(self.starts[g], self.sizes[g])
-        to = pl.ds(self.starts[g] + half * self.half, self.sizes[g])
         return remote(
             self.res.at[at],
-            self.out.at[to],
+            self.target(g, half),
             self.out_sems.at[g, 1],
             self.out_sems.at[g, 2],
             self.place.other_core(),
@@ -739,9 +1034,9 @@
     restore1,
     *refs,
 ):
-    smalls, (out, small_out), scratch = refs[:8], refs[8:10], refs[10:]
+    smalls, out, small_out, scratch = refs[:8], refs[8:10], refs[10], refs[11:]
     place = Place()
-    place.greet()
+    place.greet(place.partners())
     levels = len(place.stages)
     sets = [
         BlockSum(place, 1, sizes, joined1, restore1, out, scratch[0:6], scratch[6:11]),
@@ -764,21 +1059,24 @@
 
 
 class Caller:
-    def __init__(self, name, seqs, count, base):
-        self.name, self.seqs, self.count, self.base = name, seqs, count, base
+    def __init__(self, name, collective, seqs, count):
+        self.name, self.collective, self.seqs, self.count = name, collective, seqs, count
         self.in_specs, self.args, self.out_specs, self.outs, self.scratch = [], [], [], [], []
 
     def seq(self, *arrays):
         for a in arrays:
-            self.in_specs.append(pl.BlockSpec((self.seqs, *a.shape[1:]), lambda i, b: (i, 0, 0)))
+            self.in_specs.append(pl.BlockSpec((self.seqs, *a.shape[1:]), lambda i: (i, 0, 0)))
             self.args.append(a)
         return self
 
     def own(self, *arrays):
-        step = self.count // self.seqs
+        steps = self.count // self.seqs
         for a in arrays:
             self.in_specs.append(
-                pl.BlockSpec((self.seqs, *a.shape[1:]), lambda i, b: (b[0] * step + i, 0, 0))
+                pl.BlockSpec(
+                    (self.seqs, *a.shape[1:]),
+                    lambda i: (lax.axis_index("pipe") * steps + i, 0, 0),
+                )
             )
             self.args.append(a)
         return self
@@ -786,7 +1084,7 @@
     def halo(self, *arrays):
         for a in arrays:
             self.in_specs.append(
-                pl.BlockSpec((2, self.seqs, *a.shape[2:]), lambda i, b: (0, i, 0, 0))
+                pl.BlockSpec((2, self.seqs, *a.shape[2:]), lambda i: (0, i, 0, 0))
             )
             self.args.append(a)
         return self
@@ -794,9 +1092,13 @@
     def whole(self, *arrays):
         for a in arrays:
             zeros = (0,) * a.ndim
-            self.in_specs.append(
-                pl.BlockSpec(a.shape, lambda i, b, zeros=zeros: zeros, pipeline_mode=pl.Buffered(1))
-            )
+            self.in_specs.append(pl.BlockSpec(a.shape, lambda i, zeros=zeros: zeros))
+            self.args.append(a)
+        return self
+
+    def anywhere(self, *arrays):
+        for a in arrays:
+            self.in_specs.append(pl.BlockSpec(memory_space=pl.ANY))
             self.args.append(a)
         return self
 
@@ -805,7 +1107,7 @@
             spot = (index,) + (0,) * (a.ndim - 1)
             self.in_specs.append(
                 pl.BlockSpec(
-                    (1, *a.shape[1:]), lambda i, b, spot=spot: spot, pipeline_mode=pl.Buffered(1)
+                    (1, *a.shape[1:]), lambda i, spot=spot: spot, pipeline_mode=pl.Buffered(1)
                 )
             )
             self.args.append(a)
@@ -813,71 +1115,45 @@
 
     def out_seq(self, *shapes):
         for shape, dtype in shapes:
-            self.out_specs.append(pl.BlockSpec((self.seqs, *shape), lambda i, b: (i, 0, 0)))
+            self.out_specs.append(pl.BlockSpec((self.seqs, *shape), lambda i: (i, 0, 0)))
             self.outs.append(jax.ShapeDtypeStruct((self.count, *shape), dtype))
         return self
 
-    def out_edge(self, width):
-        self.out_specs.append(
-            pl.BlockSpec((2, self.seqs, REACH, width), lambda i, b: (0, i, 0, 0))
-        )
-        self.outs.append(jax.ShapeDtypeStruct((2, self.count, REACH, width), bf16))
+    def out_any(self, *shapes):
+        for shape, dtype in shapes:
+            self.out_specs.append(pl.BlockSpec(memory_space=pl.ANY))
+            self.outs.append(jax.ShapeDtypeStruct(shape, dtype))
         return self
 
     def out_sum(self, *shapes, dtype=f32):
         for shape in shapes:
-            self.out_specs.append(pl.BlockSpec(shape, lambda i, b: (0, 0)))
+            self.out_specs.append(pl.BlockSpec(shape, lambda i: (0, 0)))
             self.outs.append(jax.ShapeDtypeStruct(shape, dtype))
         return self
 
+    def room(self, scratch):
+        self.scratch += scratch
+        return self
+
     def sums(self, *shapes):
-        self.scratch += [pltpu.VMEM(shape, f32) for shape in shapes]
-        return self
+        return self.room([pltpu.VMEM(shape, f32) for shape in shapes])
 
     def pads(self, number, rows, width):
-        for _ in range(number):
-            self.scratch.append(pltpu.VMEM((self.seqs, rows + 2 * REACH, width), f32))
-        return self
+        return self.sums(*[(self.seqs, rows + 2 * REACH, width)] * number)
 
     def __call__(self, kernel):
         return pl.pallas_call(
             kernel,
-            grid_spec=pltpu.PrefetchScalarGridSpec(
-                num_scalar_prefetch=1,
-                grid=(self.count // self.seqs,),
-                in_specs=self.in_specs,
-                out_specs=self.out_specs,
-                scratch_shapes=self.scratch,
+            grid=(self.count // self.seqs,),
+            in_specs=self.in_specs,
+            out_specs=self.out_specs,
+            scratch_shapes=self.scratch,
+            out_shape=self.outs,
+            compiler_params=pltpu.CompilerParams(
+                vmem_limit_bytes=VMEM_LIMIT, collective_id=self.collective, has_side_effects=True
             ),
-            out_shape=self.outs,
-            compiler_params=pltpu.CompilerParams(vmem_limit_bytes=VMEM_LIMIT),
             name=self.name,
-        )(self.base, *self.args)
-
-
-def without_base(function, *static):
-    def kernel(base_ref, *refs):
-        del base_ref
-        function(*static, *refs)
-
-    return kernel
-
-
-def spread(edges):
-    count = lax.axis_size("seq")
-    up = [(i, i + 1) for i in range(count - 1)]
-    down = [(b, a) for a, b in up]
-    low = lax.ppermute(edges[1], "seq", up)
-    high = lax.ppermute(edges[0], "seq", down)
-    return jnp.stack([low, high])
-
-
-def swap(values):
-    return lax.ppermute(values, "pipe", [(0, 1), (1, 0)])
-
-
-def both(values):
-    return lax.all_gather(values, "pipe", axis=0, tiled=True)
+        )(*self.args)
 
 
 def shards(
@@ -893,40 +1169,50 @@
     inner_params,
 ):
     core = lax.axis_index("pipe")
-    base = core.astype(jnp.int32)[None]
     chip_seqs, rows, width = inputs.shape
     inner = narrow.shape[-1]
     count = chip_seqs // 2
     half = width // 2
+    levels = bits_of(lax.axis_size("seq")) + bits_of(lax.axis_size("dp"))
     type_ids = jnp.arange(TYPES, dtype=jnp.int32)
     matches = residue_types[:, :, None] == type_ids
     right_flags = mask_flags * (predicted == residue_types).astype(jnp.int32)
     right_counts = jnp.sum(jnp.where(matches, right_flags[:, :, None], 0), axis=(0, 1))
     masked_counts = jnp.sum(jnp.where(matches, mask_flags[:, :, None], 0), axis=(0, 1))
-    accuracy = lax.psum(jnp.stack([right_counts, masked_counts]), ("dp", "seq"))
+    counts = jnp.stack([right_counts, masked_counts]).astype(f32)
+    counts = jnp.pad(counts, ((0, 8 - 2), (0, 128 - TYPES)))
+
+    def caller(name, collective, seqs):
+        return Caller(name, collective, seqs, count)
+
+    def twice(a):
+        return ((2, *a.shape[1:]), a.dtype)
+
+    seqs = 1
+    halo_shape = ((2, count, REACH, inner), bf16)
+    halo_room = Halo.scratch(count, inner)
+    halves_room = Halves.scratch(count, rows, half)
+    hidden0, second0, counts, halo0, outer2, inner2, narrow2, dilated2, restore2 = (
+        caller("first_half", 1, seqs)
+        .own(inputs)
+        .whole(counts)
+        .anywhere(outer_params, inner_params, narrow, dilated, restore)
+        .out_seq(((rows, inner), f32), ((rows, inner), bf16))
+        .out_sum((8, 128))
+        .out_any(halo_shape, *map(twice, (outer_params, inner_params, narrow, dilated, restore)))
+        .room([pltpu.VMEM(a.shape, a.dtype) for a in (outer_params, inner_params, narrow) * 2])
+        .room([pltpu.VMEM(a.shape, a.dtype) for a in (restore, dilated)])
+        .room([pltpu.SemaphoreType.DMA((4, 5))])
+        .room(halo_room)
+        .room(SmallSum.scratch(8, 128, levels))
+    )(functools.partial(first_half, seqs, count))
+    accuracy = counts[:2, :TYPES].astype(jnp.int32)
     masked_count = jnp.sum(accuracy[1])
     factor = f32(chip_seqs * lax.axis_size("dp") * LENGTH) / masked_count.astype(f32)
     flags = (mask_flags.astype(f32) * factor)[:, None, :]
 
-    outer2, narrow2, dilated2, restore2, inner2 = (
-        both(v) for v in (outer_params, narrow, dilated, restore, inner_params)
-    )
-
-    def caller(name, seqs):
-        return Caller(name, seqs, count, base)
-
-    seqs = 1
-    hidden0, second0, edge = (
-        caller("first_half", seqs)
-        .own(inputs)
-        .block(0, outer2, inner2, narrow2)
-        .out_seq(((rows, inner), f32), ((rows, inner), bf16))
-        .out_edge(inner)
-    )(without_base(first_half, seqs))
-    halo0 = spread(edge)
-
-    mixed0, middle, hidden1, second1, edge = (
-        caller("middle_half", seqs)
+    mixed0, middle, hidden1, second1, halo1 = (
+        caller("middle_half", 2, seqs)
         .own(inputs)
         .seq(second0)
         .halo(halo0)
@@ -935,40 +1221,41 @@
         .out_seq(
             ((rows, inner), f32), ((rows, width), f32), ((rows, inner), f32), ((rows, inner), bf16)
         )
-        .out_edge(inner)
+        .out_any(halo_shape)
         .pads(1, rows, inner)
-    )(without_base(middle_half, seqs, FIRST_DILATION))
-    halo1 = spread(edge)
+        .room(halo_room)
+    )(functools.partial(middle_half, seqs, count, FIRST_DILATION))
 
     joined_rows = (width + KERNEL * inner, inner)
     restore_rows = (width, inner)
-    out_own, out_other, gm1, edge, restore_sum1, bias_sum1, upper_sum1 = (
-        caller("turn", seqs)
+    final_shape = ((chip_seqs, rows, half), bf16)
+    gm1, restore_sum1, bias_sum1, upper_sum1, gm_halo1, block_output = (
+        caller("turn", 3, seqs)
         .seq(middle, second1)
         .halo(halo1)
         .own(cotangent, flags)
         .block(1, outer2, inner2, dilated2, restore2)
-        .out_seq(((rows, half), bf16), ((rows, half), bf16), ((rows, inner), bf16))
-        .out_edge(inner)
+        .out_seq(((rows, inner), bf16))
         .out_sum(restore_rows, dtype=bf16)
         .out_sum((8, width), (24, inner))
+        .out_any(halo_shape, final_shape)
         .pads(1, rows, inner)
         .sums((inner, width))
-    )(without_base(turn, seqs, SECOND_DILATION))
-    gm_halo1 = spread(edge)
+        .room(halo_room + halves_room)
+    )(functools.partial(turn, seqs, count, SECOND_DILATION))
 
     (
         gx1,
         gm0,
-        edge,
         joined1,
         wide_sum1,
         small_sum1,
         restore_sum0,
         bias_sum0,
         upper_sum0,
+        gm_halo0,
     ) = (
-        caller("between", seqs)
+        caller("between", 4, seqs)
         .seq(middle)
         .own(cotangent, flags)
         .seq(hidden1, second1)
@@ -979,47 +1266,48 @@
         .seq(mixed0)
         .block(0, inner2, restore2)
         .out_seq(((rows, width), f32), ((rows, inner), bf16))
-        .out_edge(inner)
         .out_sum(joined_rows, dtype=bf16)
         .out_sum((16, width), (24, inner))
         .out_sum(restore_rows, dtype=bf16)
         .out_sum((8, width), (24, inner))
+        .out_any(halo_shape)
         .pads(2, rows, inner)
         .sums((width, inner), (KERNEL * inner, inner), (inner, width))
-    )(without_base(between, seqs, SECOND_DILATION))
-    gm_halo0 = spread(edge)
-
-    in_own, in_other, joined0, wide_sum0, small_sum0 = (
-        caller("last_half", seqs)
+        .room(halo_room)
+    )(functools.partial(between, seqs, count, SECOND_DILATION))
+
+    joined0, wide_sum0, small_sum0, input_grad = (
+        caller("last_half", 5, seqs)
         .own(inputs)
         .seq(gx1, hidden0, second0)
         .halo(halo0)
         .seq(gm0)
         .halo(gm_halo0)
         .block(0, outer2, inner2, narrow2, dilated2)
-        .out_seq(((rows, half), bf16), ((rows, half), bf16))
         .out_sum(joined_rows, dtype=bf16)
         .out_sum((16, width), (24, inner))
+        .out_any(final_shape)
         .pads(2, rows, inner)
         .sums((width, inner), (KERNEL * inner, inner))
-    )(without_base(last_half, seqs, FIRST_DILATION))
+        .room(halves_room)
+    )(functools.partial(last_half, seqs, count, FIRST_DILATION))
 
     sizes = group_sizes(inner, width)
-    levels = bits_of(lax.axis_size("seq")) + bits_of(lax.axis_size("dp"))
     rooms = []
     for _ in range(2):
         room, sems = BlockSum.scratch(sizes, inner, levels)
         rooms += room + sems
     rooms += SmallSum.scratch(32, inner, levels)
     anywhere, vmem = pl.BlockSpec(memory_space=pl.ANY), pl.BlockSpec(memory_space=pltpu.VMEM)
-    totals, smalls = pl.pallas_call(
+    joined_total, restore_total, smalls = pl.pallas_call(
         functools.partial(sum_all, sizes),
         out_shape=[
-            jax.ShapeDtypeStruct((2 * sum(sizes), inner), bf16),
+            jax.ShapeDtypeStruct(joined_rows, bf16),
+            jax.ShapeDtypeStruct((inner, width), bf16),
             jax.ShapeDtypeStruct((32, inner), f32),
         ],
         in_specs=[anywhere] * 4 + [vmem] * 8,
-        out_specs=[anywhere, vmem],
+        out_specs=[anywhere, anywhere, vmem],
         scratch_shapes=rooms,
         compiler_params=pltpu.CompilerParams(
             vmem_limit_bytes=VMEM_LIMIT, collective_id=0, has_side_effects=True
@@ -1033,26 +1321,16 @@
         *(bias_sum0, upper_sum0, wide_sum0, small_sum0),
         *(bias_sum1, upper_sum1, wide_sum1, small_sum1),
     )
-    totals = totals.astype(f32)
     smalls = lax.dynamic_slice_in_dim(smalls, core * 16, 16, 0)
-    narrow_total = totals[:width]
-    dilated_total = totals[width : width + KERNEL * inner]
-    restore_total = totals[width + KERNEL * inner :].reshape(width // inner, inner, inner)
-    restore_total = jnp.concatenate(list(restore_total), axis=1)
+    narrow_total = joined_total[:width].astype(f32)
+    dilated_total = joined_total[width:].astype(f32)
+    restore_total = restore_total.astype(f32)
     outer_total = smalls[: 3 * width // inner].reshape(3, width)
     inner_total = smalls[3 * width // inner :][:6]
 
-    def assembled(own, other):
-        arrived = swap(other)
-        return jnp.where(
-            core == 0,
-            jnp.concatenate([own, arrived]),
-            jnp.concatenate([arrived, own]),
-        )
-
     return (
-        assembled(out_own, out_other),
-        assembled(in_own, in_other),
+        block_output,
+        input_grad,
         outer_total[None],
         narrow_total[None],
         dilated_total.reshape(1, KERNEL, inner, inner),

time: 411 us -> 365 us (0.89)
  Pallas kernels: 298 us -> 335 us
  waiting for transfers between devices: 20.5 us -> 0 us
  blocking collectives: 20.1 us -> 0 us
  starting transfers between devices: 18.7 us -> 0 us
  between operations: 14.8 us -> 1.43 us
  other arithmetic: 23.9 us -> 11.5 us
    pallas_call x5, Pallas kernels: 186 us -> 224 us  [__call__(): pl.pallas_call(kernel, grid=(self.count // self.seqs,), in_specs=self.in_...]
    ppermute x10 -> x0, starting transfers between devices: 18.6 us -> none  [the longest x4 12.9 us: spread(): low = lax.ppermute(edges[1], 'seq', up)]
    ppermute x10 -> x0, waiting for transfers between devices: 18.4 us -> none  [the longest x4 16.8 us: spread(): high = lax.ppermute(edges[0], 'seq', down)]
    psum x1 -> x0, blocking collectives: 16.2 us -> none  [shards(): accuracy = lax.psum(jnp.stack([right_counts, masked_counts]), ('dp', 'seq'))]
    unnamed x23 -> x17, local copies, waits for them, and re-layouts: 0.66 us -> 12.2 us
    select_n x2 -> x0, other arithmetic: 10.3 us -> none  [assembled(): jnp.where(core == 0, jnp.concatenate([own, arrived]), jnp.concatenate([ar...]
    convert_element_type x1 -> x2, other arithmetic: 7.5 us -> 0.7 us  [the longest x1 0.68 us: shards(): accuracy = counts[:2, :TYPES].astype(jnp.int32)]
  transfers between devices with their start and end apart: 13 -> 0, of which waited for: 7 -> 0; matrix products, arithmetic and copies ran while one was open for 7% -> 0% of each run, Pallas kernels for 57% -> 0%
where the time goes in v3:
time: 365 us; the launch traced here: 364 us
  Pallas kernels  335 us (92%)
  local copies, waits for them, and re-layouts  16 us (4%)
  other arithmetic  11.5 us (3%)
    pallas_call x5, Pallas kernels, __call__(): pl.pallas_call(kernel, grid=(self.count // self.seqs,), in_specs=self.in_...  224 us
    pallas_call x1, Pallas kernels, shards(): pl.pallas_call(functools.partial(sum_all, sizes), out_shape=[jax.ShapeDty...  111 us
    unnamed x17, local copies, waits for them, and re-layouts  12.2 us

profile of v3, /device:TPU:0, one launch (start us, length us, event | category | flops | bytes accessed | tf_op | source)
XLA Modules:
  0.0 364.1 jit_solution(3267798896592817826)
XLA Ops:
  0.6 0.8 compare_select_fusion
  1.4 1.9 select_reduce_fusion.1
  3.3 0.6 pad.4.counts_ref
  4.0 1.3 copy.26.outer
  5.3 1.3 copy.27.inner
  6.6 30.2 %first_half.1 = (f32[12,256,512]{2,1,0:T(8,128)}, bf16[12,256,512]{2,1,0:T(8,128)(2,1)}, f32[8,128]{1,0:T(8,128)}, bf16[2,12,8,512]{3,2,1,0:T(8,128)(2,1)}, f32[...) custom-call(bf16[24,256,1024]{2,1,0:T(8,128)(2,1)} %x_ref.5, ...), custom_call_target="tpu_custom_call" | custom-call | tf_op jit(solution)/shard_map/first_half/pallas_call | solution.py:1145
  36.8 0.0 copy-start.1
  36.8 38.5 %middle_half.1 = (f32[12,256,512]{2,1,0:T(8,128)}, f32[12,256,1024]{2,1,0:T(8,128)}, f32[12,256,512]{2,1,0:T(8,128)}, bf16[12,256,512]{2,1,0:T(8,128)(2,1)}, bf16[2,12,8,512]{3,2,1,0:T(8,128)(2,1)}) custom-call(bf16[24,256,1024]{2,1,0:T(8,128)(2,1)} %x_ref.5, bf16[12,256,512]{2,1,0:T(8,128)(2,1)} %get-tuple-element.44.second_ref, ...), custom_call_target="tpu_custom_call" | custom-call | tf_op jit(solution)/shard_map/middle_half/pallas_call | solution.py:1145
  75.2 0.7 slice_convert_fusion
  75.9 0.6 slice_reduce_fusion
  77.3 0.6 broadcast_in_dim.43.flags_ref
  77.9 42.3 %turn.1 = (bf16[12,256,512]{2,1,0:T(8,128)(2,1)}, bf16[1024,512]{1,0:T(8,128)(2,1)}, f32[8,1024]{1,0:T(8,128)}, f32[24,512]{1,0:T(8,128)}, bf16[2,12,8,512]{3,2,...) custom-call(f32[12,256,1024]{2,1,0:T(8,128)} %get-tuple-element.51.middle_ref, ...), custom_call_target="tpu_custom_call" | custom-call | tf_op jit(solution)/shard_map/turn/pallas_call | solution.py:1145
  120.2 0.0 copy-done.3
  120.2 65.4 %between.1 = (f32[12,256,1024]{2,1,0:T(8,128)}, bf16[12,256,512]{2,1,0:T(8,128)(2,1)}, bf16[3584,512]{1,0:T(8,128)(2,1)}, f32[16,1024]{1,0:T(8,128)}, f32[24,512...) custom-call(f32[12,256,1024]{2,1,0:T(8,128)} %get-tuple-element.51.m, ...), custom_call_target="tpu_custom_call" | custom-call | tf_op jit(solution)/shard_map/between/pallas_call | solution.py:1145
  185.6 47.8 %last_half.1 = (bf16[3584,512]{1,0:T(8,128)(2,1)}, f32[16,1024]{1,0:T(8,128)}, f32[24,512]{1,0:T(8,128)}, bf16[24,256,512]{2,1,0:T(8,128)(2,1)}) custom-call(bf16[24,256,1024]{2,1,0:T(8,128)(2,1)} %x_ref.5, f32[12,256,1024]{2,1,0:T(8,128)} %get-tuple-element.60.gx_ref, f32[12,256,512]{2,1,0:T(8,128)} %get-tuple-element.61.hidden_ref, ...), custom_call_target="tpu_custom_call" | custom-call | tf_op jit(solution)/shard_map/last_half/pallas_call | solution.py:1145
  233.4 111.1 %sum_all.1 = (bf16[3584,512]{1,0:T(8,128)(2,1)}, bf16[512,1024]{1,0:T(8,128)(2,1)}, f32[32,512]{1,0:T(8,128)}) custom-call(bf16[3584,512]{1,0:T(8,128)(2,1)} %get-tuple-element.65.joined0, bf16[1024,512]{1,0:T(8,128)(2,1)} %get-tuple-element.66.restore0, bf16[3584,512]{1,0:T(8,128)(2,1)} %get-tuple-element.67.joined1, ...), custom_call_target="tpu_custom_call" | custom-call | tf_op jit(solution)/shard_map/sum_all/pallas_call | solution.py:1302
  344.4 1.9 slice.24
  346.3 3.1 convert.4
  349.4 1.6 bitcast_convert_fusion
  351.0 2.8 bitcast_convert_fusion.1
  353.9 0.6 broadcast_in_dim_reshape.4
  354.5 0.6 copy.29
  355.1 6.2 %copy.32 = bf16[24,256,512]{2,1,0:T(8,128)(2,1)} copy(bf16[24,256,512]{2,1,0:T(8,128)(2,1)} %get-tuple-element.116) | data formatting | bytes 12582912
  361.4 2.7 copy.33
  (14 shorter events, 0.0 us)
Async XLA Ops:
  36.8 40.5 %copy-start.1 = (s32[24,256]{1,0:T(8,128)S(1)}, s32[24,256]{1,0:T(8,128)}, u32[]{:S(2)}) copy-start(s32[24,256]{1,0:T(8,128)} %param.12) | copy-start | bytes 73732
  75.9 44.2 %copy-start.3 = (s32[2,30]{1,0:T(2,128)}, s32[2,30]{1,0:T(2,128)S(1)}, u32[]{:S(2)}) copy-start(s32[2,30]{1,0:T(2,128)S(1)} %slice_convert_fusion) | copy-start | bytes 724
  346.3 3.1 copy-start
  349.4 4.4 %copy-start.2 = (f32[32,512]{1,0:T(8,128)S(1)}, f32[32,512]{1,0:T(8,128)}, u32[]{:S(2)}) copy-start(f32[32,512]{1,0:T(8,128)} %get-tuple-element.77) | copy-start | bytes 196612
  355.1 6.2 %slice-start = ((s8[6291456]{0:T(1024)(128)(4,1)}), s8[4194304]{0:T(1024)(128)(4,1)S(1)}, s32[]{:S(2)}) async-start(s8[6291456]{0:T(1024)(128)(4,1)} %bitcast.13), calls=%async_computation | async-start | bytes 8388608
  355.1 6.3 %slice-start.1 = ((s8[6291456]{0:T(1024)(128)(4,1)}), s8[2097152]{0:T(1024)(128)(4,1)S(1)}, s32[]{:S(2)}) async-start(s8[6291456]{0:T(1024)(128)(4,1)} %bitcast.13), calls=%async_computation.1 | async-start | bytes 4194304

commit v4 on v0

v4 whole, which is shorter than its diff:
```python
import functools

import jax
import jax.numpy as jnp
from jax import lax
from jax.experimental import pallas as pl
from jax.experimental.pallas import tpu as pltpu
from jax.sharding import PartitionSpec as P

KERNEL = 5
FIRST_DILATION = 2
SECOND_DILATION = 4
TYPES = 30
LENGTH = 1024
REACH = 8
EPSILON = 1e-05
VMEM_LIMIT = 63 << 20

f32 = jnp.float32
bf16 = jnp.bfloat16
KEPT = bf16

ROOT_HALF = 0.7071067811865476
INV_ROOT_2PI = 0.3989422804014327
EXP2_SCALE = -0.5 * 1.4426950408889634


def normalized(v):
    scale = 1.0 / v.shape[-1]
    centered = v - jnp.sum(v, axis=-1, keepdims=True) * scale
    spread = jnp.sum(centered * centered, axis=-1, keepdims=True) * scale
    r = lax.rsqrt(spread + EPSILON)
    return centered * r, r


def upper(u):
    return 0.5 * lax.erf(u * ROOT_HALF) + 0.5


def norm_act(v, g, s):
    n, _ = normalized(v)
    u = n * g + s
    return (u * upper(u)).astype(bf16)


def fold(v):
    rows, width = v.shape
    return jnp.sum(v.reshape(rows // 8, 8, width), axis=0)


class Back:
    def __init__(self, v, g, s):
        self.n, self.r = normalized(v)
        self.g = g
        u = self.n * g + s
        phi = upper(u)
        self.act = (u * phi).astype(bf16)
        self.slope = phi + u * (INV_ROOT_2PI * jnp.exp2(u * u * EXP2_SCALE))

    def grad(self, e):
        p = e * self.slope
        pn = p * self.n
        scale = 1.0 / p.shape[-1]
        pg = p * self.g
        a = jnp.sum(pg, axis=-1, keepdims=True) * scale
        b = jnp.sum(pn * self.g, axis=-1, keepdims=True) * scale
        return self.r * (pg - a - self.n * b), fold(pn), fold(p)


def dot(a, b):
    return jnp.dot(a, b, preferred_element_type=f32)


def dot_nt(a, b):
    return lax.dot_general(a, b, (((1,), (1,)), ((), ())), preferred_element_type=f32)


def dot_tn(a, b):
    return lax.dot_general(a, b, (((0,), (0,)), ((), ())), preferred_element_type=f32)


def fill(pad, low, values, high):
    rows = values.shape[0]
    pad[0:REACH, :] = low.astype(f32)
    pad[REACH : REACH + rows, :] = values.astype(f32)
    pad[REACH + rows :, :] = high.astype(f32)


def taps(pad, rows, d, direction):
    pieces = []
    for k in range(KERNEL):
        start = REACH + direction * (k - KERNEL // 2) * d
        pieces.append(pad[start : start + rows, :].astype(bf16))
    return pieces


def row(ref, i):
    return ref[i : i + 1, :]


def column(flags):
    return jnp.transpose(jnp.broadcast_to(flags, (128, flags.shape[1])))


def seeded(cot, flags):
    col = column(flags)
    return cot.astype(f32) * jnp.concatenate([col] * (cot.shape[1] // 128), axis=1)


MESH = pl.DeviceIdType.MESH
UNIT = 16


def bits_of(count):
    return count.bit_length() - 1


def mixed_by(core, first, second):
    return first + core * (second - first)


class Place:
    def __init__(self):
        self.core = lax.axis_index("pipe")
        self.seq = lax.axis_index("seq")
        self.dp = lax.axis_index("dp")
        seq_bits = bits_of(lax.axis_size("seq"))
        dp_bits = bits_of(lax.axis_size("dp"))
        order = list(range(seq_bits))
        cut = seq_bits // 2
        turned = order[cut:] + order[:cut]
        self.stages = [("seq", a, b) for a, b in zip(order, turned)]
        self.stages += [("dp", a, a) for a in range(dp_bits)]

    def bit(self, stage):
        axis, a, b = self.stages[stage]
        spot = self.seq if axis == "seq" else self.dp
        return mixed_by(self.core, (spot // (1 << a)) % 2, (spot // (1 << b)) % 2)

    def peer(self, stage):
        axis, a, b = self.stages[stage]
        spot = self.seq if axis == "seq" else self.dp
        hop = mixed_by(self.core, 1 << a, 1 << b) * (1 - 2 * self.bit(stage))
        return {axis: spot + hop}

    def other_core(self):
        return {"pipe": 1 - self.core}

    def partners(self):
        return [self.other_core()] + [self.peer(s) for s in range(len(self.stages))]

    def line(self):
        n = lax.axis_size("seq")
        return [{"seq": (self.seq + 1) % n}, {"seq": (self.seq + n - 1) % n}]

    def greet(self, friends):
        barrier = pltpu.get_barrier_semaphore()
        for friend in friends:
            pl.semaphore_signal(barrier, inc=1, device_id=friend, device_id_type=MESH)
        pl.semaphore_wait(barrier, len(friends))


def remote(src, dst, send_sem, recv_sem, device):
    return pltpu.make_async_remote_copy(
        src_ref=src,
        dst_ref=dst,
        send_sem=send_sem,
        recv_sem=recv_sem,
        device_id=device,
        device_id_type=MESH,
    )


class Halo:
    def __init__(self, place, edges, halo, sems):
        self.place, self.edges, self.halo, self.sems = place, edges, halo, sems
        self.has_low = place.seq > 0
        self.has_high = place.seq < lax.axis_size("seq") - 1

    @staticmethod
    def scratch(count, width):
        return [
            pltpu.VMEM((2, count, REACH, width), bf16),
            pltpu.VMEM((2, count, REACH, width), bf16),
            pltpu.SemaphoreType.DMA((4, count)),
        ]

    def up(self, i):
        device = {"seq": self.place.seq + 1}
        sems = self.sems
        return remote(self.edges.at[1, i], self.halo.at[0, i], sems.at[0, i], sems.at[1, i], device)

    def down(self, i):
        device = {"seq": self.place.seq - 1}
        sems = self.sems
        return remote(self.edges.at[0, i], self.halo.at[1, i], sems.at[2, i], sems.at[3, i], device)

    def begin(self):
        @pl.when(jnp.logical_not(self.has_low))
        def _():
            self.halo[0] = jnp.zeros_like(self.halo[0])

        @pl.when(jnp.logical_not(self.has_high))
        def _():
            self.halo[1] = jnp.zeros_like(self.halo[1])

    def send(self, i, values):
        self.edges[0, i] = values[:REACH]
        self.edges[1, i] = values[values.shape[0] - REACH :]

        @pl.when(self.has_high)
        def _():
            self.up(i).start()

        @pl.when(self.has_low)
        def _():
            self.down(i).start()

    def take(self, i):
        @pl.when(self.has_low)
        def _():
            self.down(i).wait_send()
            self.up(i).wait_recv()

        @pl.when(self.has_high)
        def _():
            self.up(i).wait_send()
            self.down(i).wait_recv()

    def around(self, pad, i, values):
        fill(pad, self.halo[0, i], values, self.halo[1, i])


class Halves:
    def __init__(self, place, count, out, own, other, sems, arrivals):
        self.place, self.count, self.out = place, count, out
        self.own, self.other, self.sems, self.arrivals = own, other, sems, arrivals

    @staticmethod
    def scratch(count, rows, half):
        return [
            pltpu.VMEM((2, rows, half), bf16),
            pltpu.VMEM((2, rows, half), bf16),
            pltpu.SemaphoreType.DMA((2, 2)),
            pltpu.SemaphoreType.DMA((count,)),
        ]

    def local(self, i, slot):
        to = self.place.core * self.count + i
        return pltpu.make_async_copy(self.own.at[slot], self.out.at[to], self.sems.at[0, slot])

    def away(self, i, slot):
        to = self.place.core * self.count + i
        return remote(
            self.other.at[slot],
            self.out.at[to],
            self.sems.at[1, slot],
            self.arrivals.at[i],
            self.place.other_core(),
        )

    def release(self, i, slot):
        self.local(i, slot).wait()
        self.away(i, slot).wait_send()

    def send(self, i, values):
        slot = i % 2
        half = values.shape[1] // 2
        left, right = values[:, :half], values[:, half:]

        @pl.when(i >= 2)
        def _():
            self.release(i - 2, slot)

        first = self.place.core == 0
        self.own[slot] = jnp.where(first, left, right)
        self.other[slot] = jnp.where(first, right, left)
        self.local(i, slot).start()
        self.away(i, slot).start()

    def end(self):
        for i in range(max(0, self.count - 2), self.count):
            self.release(i, i % 2)

        def body(i, carry):
            self.away(i, 0).wait_recv()
            return carry

        lax.fori_loop(0, self.count, body, 0)


def group_sizes(inner, width):
    upper = KERNEL * inner // 2
    return [upper - upper // 5 * 2, upper // 5 * 2, width // 2, width // 2]


class BlockSum:
    def __init__(self, place, block, sizes, part, out, room):
        self.place, self.block, self.sizes, self.part, self.out = place, block, sizes, part, out
        self.theirs, self.sbuf, self.rbuf, self.res = room[:4]
        self.core_sems, self.send_sems, self.recv_sems, self.out_sems = room[4:]
        self.levels = len(place.stages)
        self.starts = [sum(sizes[:g]) for g in range(len(sizes))]
        self.half = sum(sizes)
        sent = [sum(self.lengths(n, self.levels)[1:]) for n in sizes]
        self.bases = [sum(sent[:g]) for g in range(len(sizes))]

    @staticmethod
    def lengths(rows, levels):
        out = [rows]
        for _ in range(levels):
            last = out[-1]
            out.append(last // 2 if last % (2 * UNIT) == 0 else last)
        return out

    @staticmethod
    def scratch(sizes, width, levels):
        rows, groups = sum(sizes), len(sizes)
        sent = sum(sum(BlockSum.lengths(n, levels)[1:]) for n in sizes)
        dma = pltpu.SemaphoreType.DMA
        return [
            pltpu.VMEM((rows, width), bf16),
            pltpu.VMEM((sent, width), bf16),
            pltpu.VMEM((sent, width), bf16),
            pltpu.VMEM((rows, width), bf16),
            dma((groups, 2)),
            dma((groups, 2 * levels)),
            dma((groups, 2 * levels)),
            dma((groups, 3)),
        ]

    def spots(self, g):
        lengths = self.lengths(self.sizes[g], self.levels)
        start, out = self.starts[g], []
        for s in range(self.levels):
            out.append((start, lengths[s]))
            if lengths[s + 1] < lengths[s]:
                start = start + self.place.bit(s) * lengths[s + 1]
        out.append((start, lengths[-1]))
        return out

    def base(self, g, s):
        return self.bases[g] + sum(self.lengths(self.sizes[g], self.levels)[1 : s + 1])

    def value(self, g, s, start, n):
        lengths, spots = self.lengths(self.sizes[g], self.levels), self.spots(g)
        terms = [(self.part, self.place.core * self.half + start), (self.theirs, start)]
        for k in range(s):
            at = self.base(g, k) + (start - spots[k + 1][0])
            if lengths[k + 1] == lengths[k]:
                terms = [(self.sbuf, at)]
            terms.append((self.rbuf, at))
        total = None
        for ref, at in terms:
            term = ref[pl.ds(pl.multiple_of(at, UNIT), n), :].astype(f32)
            total = term if total is None else total + term
        return total

    def core_copy(self, g):
        n = self.sizes[g]
        source = pl.multiple_of((1 - self.place.core) * self.half + self.starts[g], UNIT)
        return remote(
            self.part.at[pl.ds(source, n)],
            self.theirs.at[pl.ds(self.starts[g], n)],
            self.core_sems.at[g, 0],
            self.core_sems.at[g, 1],
            self.place.other_core(),
        )

    def down(self, g, s):
        n = self.lengths(self.sizes[g], self.levels)[s + 1]
        at = pl.ds(self.base(g, s), n)
        return remote(
            self.sbuf.at[at],
            self.rbuf.at[at],
            self.send_sems.at[g, s],
            self.recv_sems.at[g, s],
            self.place.peer(s),
        )

    def start_down(self, g, s):
        start, rows = self.spots(g)[s]
        n = self.lengths(self.sizes[g], self.levels)[s + 1]
        if n < rows:
            start = start + (1 - self.place.bit(s)) * n
        base = self.base(g, s)
        self.sbuf[base : base + n, :] = self.value(g, s, start, n).astype(bf16)
        self.down(g, s).start()

    def up(self, g, s):
        lengths = self.lengths(self.sizes[g], self.levels)
        if lengths[s] == lengths[s + 1]:
            return None
        start, n = self.spots(g)[s + 1]
        at = pl.ds(pl.multiple_of(start, UNIT), n)
        return remote(
            self.res.at[at],
            self.res.at[at],
            self.send_sems.at[g, self.levels + s],
            self.recv_sems.at[g, self.levels + s],
            self.place.peer(s),
        )

    def target(self, g, half):
        n, at = self.sizes[g], self.starts[g] + half * self.half
        joined, restore = self.out
        top = joined.shape[0]
        if at < top:
            return joined.at[pl.ds(at, n)]
        return restore.at[:, pl.ds(at - top, n)]

    def keep(self, g, half):
        at = pl.ds(self.starts[g], self.sizes[g])
        return pltpu.make_async_copy(self.res.at[at], self.target(g, half), self.out_sems.at[g, 0])

    def give(self, g, half):
        at = pl.ds(self.starts[g], self.sizes[g])
        return remote(
            self.res.at[at],
            self.target(g, half),
            self.out_sems.at[g, 1],
            self.out_sems.at[g, 2],
            self.place.other_core(),
        )

    def steps(self):
        return 2 * self.levels + 3

    def step(self, g, t):
        core, levels = self.place.core, self.levels
        if t == 0:
            self.core_copy(g).start()
        if t == 1:
            self.core_copy(g).wait()
        if 2 <= t < 2 + levels:
            self.down(g, t - 2).wait()
        if 1 <= t < 1 + levels:
            self.start_down(g, t - 1)
        if t == 1 + levels:
            start, n = self.spots(g)[levels]
            at = pl.ds(pl.multiple_of(start, UNIT), n)
            self.res[at, :] = self.value(g, levels, start, n).astype(bf16)
        if 2 + levels <= t < 2 + 2 * levels:
            copy = self.up(g, 2 * levels + 1 - t)
            if copy is not None:
                copy.wait()
        if 1 + levels <= t < 1 + 2 * levels:
            copy = self.up(g, 2 * levels - t)
            if copy is not None:
                copy.start()
        if t == 1 + 2 * levels:
            for half in (0, 1):

                @pl.when(core == half)
                def _():
                    if half == self.block:
                        self.keep(g, half).start()
                    else:
                        self.give(g, half).start()

        if t == 2 + 2 * levels:
            for half in (0, 1):

                @pl.when(core == half)
                def _():
                    if half == self.block:
                        self.keep(g, half).wait()
                        self.give(g, 1 - half).wait_recv()
                    else:
                        self.give(g, half).wait_send()


class SmallSum:
    def __init__(self, place, total, arrived, sems):
        self.place, self.total, self.arrived, self.sems = place, total, arrived, sems
        self.stages = len(place.stages) + 1

    @staticmethod
    def scratch(rows, width, levels):
        return [
            pltpu.VMEM((levels + 2, rows, width), f32),
            pltpu.VMEM((levels + 1, rows, width), f32),
            pltpu.SemaphoreType.DMA((levels + 1, 2)),
        ]

    def copy(self, s):
        device = self.place.other_core() if s == 0 else self.place.peer(s - 1)
        return remote(
            self.total.at[s], self.arrived.at[s], self.sems.at[s, 0], self.sems.at[s, 1], device
        )

    def start(self, s):
        self.copy(s).start()

    def end(self, s):
        self.copy(s).wait()
        self.total[s + 1] = self.total[s] + self.arrived[s]


def gather_small(total, block, bias_ref, upper_ref, wide_ref, small_ref):
    half = total.shape[-1]
    rows = []
    for ref in (wide_ref, bias_ref):
        for k in range(ref.shape[0] // 8):
            for lane in range(0, ref.shape[1], half):
                rows.append((ref, k, lane))
    for ref, k in ((small_ref, 0), (upper_ref, 0), (small_ref, 1), (small_ref, 2), (upper_ref, 1), (upper_ref, 2)):
        rows.append((ref, k, 0))
    for j, (ref, k, lane) in enumerate(rows):
        piece = ref[8 * k : 8 * k + 8, lane : lane + half]
        total[0, 16 * block + j : 16 * block + j + 1, :] = jnp.sum(piece, axis=0, keepdims=True)


def block_out_back(back, grad_low, restore, restore_sum, bias_sum, upper_sum):
    restore_sum[...] += dot_tn(back.act, grad_low)
    bias_sum[...] += fold(grad_low.astype(f32))
    gv, gain, shift = back.grad(dot_nt(grad_low, restore[...]))
    gm = gv.astype(bf16)
    upper_sum[0:8] += fold(gm.astype(f32))
    upper_sum[8:16] += gain
    upper_sum[16:24] += shift
    return gm


def block_in_back(
    d, stream, grad_out, hidden, gm, outer, inner, narrow, dilated, narrow_sum, dilated_sum, wide_sum, small_sum, pad, gm_pad
):
    rows = stream.shape[0]
    grad_second = None
    for k, piece in enumerate(taps(gm_pad, rows, d, -1)):
        term = dot_nt(piece, dilated[k])
        grad_second = term if grad_second is None else grad_second + term
    windows = jnp.concatenate(taps(pad, rows, d, 1), axis=1)
    dilated_sum[...] += dot_tn(windows, gm)
    back = Back(hidden, row(inner, 2), row(inner, 3))
    gv, gain, shift = back.grad(grad_second)
    gh = gv.astype(bf16)
    small_sum[0:8] += fold(gh.astype(f32))
    small_sum[8:16] += gain
    small_sum[16:24] += shift
    first = Back(stream, row(outer, 0), row(outer, 1))
    narrow_sum[...] += dot_tn(first.act, gh)
    gx, gain, shift = first.grad(dot_nt(gh, narrow[...]))
    wide_sum[0:8] += gain
    wide_sum[8:16] += shift
    return grad_out + gx


def clear(*refs):
    for ref in refs:
        ref[...] = jnp.zeros_like(ref)


class Refs:
    def __init__(self, names, refs):
        for name, ref in zip(names, refs, strict=True):
            setattr(self, name, ref)


def whole(names, count, sizes, residues, *refs):
    r = Refs(names, refs)
    place = Place()
    core = place.core
    rows, width = r.inputs.shape[1:]
    inner = r.narrow.shape[2]
    taps_rows = KERNEL * inner
    small_counts = SmallSum(place, *r.count_room)
    halos = [Halo(place, *room) for room in r.halo_rooms]
    outputs = Halves(place, count, r.block_output, *r.halves_room)
    grads = Halves(place, count, r.input_grad, *r.halves_room[:3], r.grad_arrivals)
    outer, inner_p, narrow, dilated, restore = r.outer_v, r.inner_v, r.narrow_v, r.dilated_v, r.restore_v
    params = ((r.outer, outer), (r.inner, inner_p), (r.narrow, narrow), (r.dilated, dilated), (r.restore, restore))
    sets = [
        BlockSum(place, block, sizes, r.parts[block], (r.joined_total, r.restore_total), r.sum_rooms[block])
        for block in (0, 1)
    ]

    def local(k):
        src, dst = params[k]
        return pltpu.make_async_copy(src, dst.at[pl.ds(core, 1)], r.param_sems.at[0, k])

    def away(k):
        src, dst = params[k]
        to = dst.at[pl.ds(core, 1)]
        return remote(src, to, r.param_sems.at[1, k], r.param_sems.at[2, k], place.other_core())

    def arrive(k, block):
        @pl.when(core == block)
        def _():
            local(k).wait()

        @pl.when(core != block)
        def _():
            away(k).wait_recv()

    def over(body, ins, outs):
        def spec(a, own):
            shape = (1, *a.shape[1:])
            if own:
                return pl.BlockSpec(shape, lambda i: (core * count + i, 0, 0))
            return pl.BlockSpec(shape, lambda i: (i, 0, 0))

        in_specs = [spec(a, a is r.inputs or a is r.cotangent) for a in ins]
        out_specs = [spec(a, False) for a in outs]
        pipe = pltpu.emit_pipeline(
            lambda *blocks: body(pl.program_id(0), *blocks),
            grid=(count,),
            in_specs=in_specs,
            out_specs=out_specs,
        )
        pipe(*ins, *outs)

    def flags_of(i):
        masked = jnp.sum(small_counts.total[small_counts.stages][1:2, :], axis=1, keepdims=True)
        return r.flags[core * count + i] * (residues / masked)

    place.greet(place.line() + place.partners())
    for k in range(len(params)):
        local(k).start()
        away(k).start()
    small_counts.total[1] = r.counts[...]
    for halo in halos:
        halo.begin()
    clear(r.narrow_sum, r.dilated_sum, r.restore_sum)
    clear(*r.wide_sums, *r.bias_sums, *r.upper_sums, *r.small_sums)
    for k in range(3):
        arrive(k, 0)

    def first(i, x, hidden_out, second_out):
        for k in range(1, small_counts.stages):

            @pl.when(i == k)
            def _():
                if k > 1:
                    small_counts.end(k - 1)
                small_counts.start(k)

        act = norm_act(x[0].astype(f32), row(outer.at[0], 0), row(outer.at[0], 1))
        hidden = dot(act, narrow[0]) + row(inner_p.at[0], 0)
        hidden_out[0] = hidden
        second = norm_act(hidden, row(inner_p.at[0], 2), row(inner_p.at[0], 3))
        second_out[0] = second
        halos[0].send(i, second)

    over(first, [r.inputs], [r.hidden0, r.second0])
    small_counts.end(small_counts.stages - 1)
    r.counts_out[...] = small_counts.total[small_counts.stages]
    for k in range(len(params)):
        away(k).wait_send()
        arrive(k, 1)
        if k >= 3:
            arrive(k, 0)

    def second(i, x, second_in, mixed_out, middle_out, hidden_out, second_out):
        halos[0].take(i)
        halos[0].around(r.pads.at[0], i, second_in[0])
        windows = jnp.concatenate(taps(r.pads.at[0], rows, FIRST_DILATION, 1), axis=1)
        mixed = dot(windows, dilated[0].reshape(taps_rows, inner)) + row(inner_p.at[0], 1)
        mixed_out[0] = mixed
        third = norm_act(mixed, row(inner_p.at[0], 4), row(inner_p.at[0], 5))
        y = x[0].astype(f32) + (dot(third, restore[0]) + row(outer.at[0], 2))
        middle_out[0] = y.astype(middle_out.dtype)
        act = norm_act(y, row(outer.at[1], 0), row(outer.at[1], 1))
        hidden = dot(act, narrow[1]) + row(inner_p.at[1], 0)
        hidden_out[0] = hidden
        second = norm_act(hidden, row(inner_p.at[1], 2), row(inner_p.at[1], 3))
        second_out[0] = second
        halos[1].send(i, second)

    over(second, [r.inputs, r.second0], [r.mixed0, r.middle, r.hidden1, r.second1])

    def turn(i, middle, second_in, cot, gm_out):
        halos[1].take(i)
        halos[1].around(r.pads.at[0], i, second_in[0])
        windows = jnp.concatenate(taps(r.pads.at[0], rows, SECOND_DILATION, 1), axis=1)
        mixed = dot(windows, dilated[1].reshape(taps_rows, inner)) + row(inner_p.at[1], 1)
        back = Back(mixed, row(inner_p.at[1], 4), row(inner_p.at[1], 5))
        y = middle[0].astype(f32) + (dot(back.act, restore[1]) + row(outer.at[1], 2))
        outputs.send(i, y.astype(bf16))
        grad_low = seeded(cot[0], flags_of(i)).astype(bf16)
        gm = block_out_back(back, grad_low, restore.at[1], r.restore_sum, r.bias_sums[1], r.upper_sums[1])
        gm_out[0] = gm
        halos[2].send(i, gm)

    over(turn, [r.middle, r.second1, r.cotangent], [r.gm1])
    outputs.end()
    write_restore(r.parts[1], r.restore_sum)
    clear(r.restore_sum)

    def between(i, middle, cot, hidden, second_in, gm, mixed, gx_out, gm_out):
        halos[2].take(i)
        halos[2].around(r.pads.at[1], i, gm[0])
        halos[1].around(r.pads.at[0], i, second_in[0])
        gx = block_in_back(
            SECOND_DILATION,
            middle[0].astype(f32),
            seeded(cot[0], flags_of(i)),
            hidden[0],
            gm[0],
            outer.at[1],
            inner_p.at[1],
            narrow.at[1],
            dilated.at[1],
            r.narrow_sum,
            r.dilated_sum,
            r.wide_sums[1],
            r.small_sums[1],
            r.pads.at[0],
            r.pads.at[1],
        )
        gx_out[0] = gx.astype(gx_out.dtype)
        back = Back(mixed[0], row(inner_p.at[0], 4), row(inner_p.at[0], 5))
        gm = block_out_back(back, gx.astype(bf16), restore.at[0], r.restore_sum, r.bias_sums[0], r.upper_sums[0])
        gm_out[0] = gm
        halos[3].send(i, gm)

    over(between, [r.middle, r.cotangent, r.hidden1, r.second1, r.gm1, r.mixed0], [r.gx1, r.gm0])
    write_joined(r.parts[1], r.narrow_sum, r.dilated_sum)
    write_restore(r.parts[0], r.restore_sum)
    clear(r.narrow_sum, r.dilated_sum)

    groups = range(len(sizes))
    steps = sets[0].steps()
    lag = [g // 2 for g in groups]

    def beside(t):
        for g in groups:
            if 0 <= t - lag[g] < steps:
                sets[1].step(g, t - lag[g])

    ticks = steps + max(lag)

    def last(i, x, gx_in, hidden, second_in, gm):
        for t in range(min(ticks, count)):

            @pl.when(i == t)
            def _():
                beside(t)

        halos[3].take(i)
        halos[3].around(r.pads.at[1], i, gm[0])
        halos[0].around(r.pads.at[0], i, second_in[0])
        gx = block_in_back(
            FIRST_DILATION,
            x[0].astype(f32),
            gx_in[0].astype(f32),
            hidden[0],
            gm[0],
            outer.at[0],
            inner_p.at[0],
            narrow.at[0],
            dilated.at[0],
            r.narrow_sum,
            r.dilated_sum,
            r.wide_sums[0],
            r.small_sums[0],
            r.pads.at[0],
            r.pads.at[1],
        )
        grads.send(i, gx.astype(bf16))

    over(last, [r.inputs, r.gx1, r.hidden0, r.second0, r.gm0], [])
    write_joined(r.parts[0], r.narrow_sum, r.dilated_sum)

    small = SmallSum(place, *r.small_room)
    small.total[0] = jnp.zeros_like(small.total[0])
    for b in (0, 1):
        gather_small(small.total, b, r.bias_sums[b], r.upper_sums[b], r.wide_sums[b], r.small_sums[b])
    for t in range(max(steps + len(sizes) - 1, small.stages + 1, ticks - count)):
        if count + t < ticks:
            beside(count + t)
        for g in groups:
            if 0 <= t - g < steps:
                sets[0].step(g, t - g)
        if 0 < t <= small.stages:
            small.end(t - 1)
        if t < small.stages:
            small.start(t)
    r.small_out[...] = small.total[small.stages]
    grads.end()


def write_restore(part, total):
    inner, wide = total.shape
    top = part.shape[0] - wide
    for j in range(wide // inner):
        at = top + j * inner
        part[at : at + inner, :] = total[:, j * inner : (j + 1) * inner].astype(bf16)


def write_joined(part, narrow_sum, dilated_sum):
    cut, deep = narrow_sum.shape[0], dilated_sum.shape[0]
    part[:cut, :] = narrow_sum[...].astype(bf16)
    part[cut : cut + deep, :] = dilated_sum[...].astype(bf16)


def shards(
    inputs,
    cotangent,
    mask_flags,
    residue_types,
    predicted,
    outer_params,
    narrow,
    dilated,
    restore,
    inner_params,
):
    core = lax.axis_index("pipe")
    chip_seqs, rows, width = inputs.shape
    inner = narrow.shape[-1]
    count = chip_seqs // 2
    half = width // 2
    levels = bits_of(lax.axis_size("seq")) + bits_of(lax.axis_size("dp"))
    type_ids = jnp.arange(TYPES, dtype=jnp.int32)
    matches = residue_types[:, :, None] == type_ids
    right_flags = mask_flags * (predicted == residue_types).astype(jnp.int32)
    right_counts = jnp.sum(jnp.where(matches, right_flags[:, :, None], 0), axis=(0, 1))
    masked_counts = jnp.sum(jnp.where(matches, mask_flags[:, :, None], 0), axis=(0, 1))
    counts = jnp.stack([right_counts, masked_counts]).astype(f32)
    counts = jnp.pad(counts, ((0, 8 - 2), (0, 128 - TYPES)))

    flags = mask_flags.astype(f32)[:, None, :]
    sizes = group_sizes(inner, width)
    residues = float(chip_seqs * lax.axis_size("dp") * LENGTH)
    deep = KERNEL * inner
    any_space, vmem = pl.BlockSpec(memory_space=pl.ANY), pl.BlockSpec(memory_space=pltpu.VMEM)
    args = [
        ("inputs", inputs, any_space),
        ("cotangent", cotangent, any_space),
        ("flags", flags, vmem),
        ("counts", counts, vmem),
        ("outer", outer_params, any_space),
        ("inner", inner_params, any_space),
        ("narrow", narrow, any_space),
        ("dilated", dilated, any_space),
        ("restore", restore, any_space),
    ]
    results = [
        ("block_output", (chip_seqs, rows, half), bf16, any_space),
        ("input_grad", (chip_seqs, rows, half), bf16, any_space),
        ("joined_total", (width + deep, inner), bf16, any_space),
        ("restore_total", (inner, width), bf16, any_space),
        ("small_out", (32, inner), f32, vmem),
        ("counts_out", (8, 128), f32, vmem),
        ("hidden0", (count, rows, inner), f32, any_space),
        ("hidden1", (count, rows, inner), f32, any_space),
        ("mixed0", (count, rows, inner), f32, any_space),
        ("middle", (count, rows, width), f32, any_space),
        ("gx1", (count, rows, width), KEPT, any_space),
        ("second0", (count, rows, inner), bf16, any_space),
        ("second1", (count, rows, inner), bf16, any_space),
        ("gm0", (count, rows, inner), bf16, any_space),
        ("gm1", (count, rows, inner), bf16, any_space),
    ]

    def twice(a):
        return pltpu.VMEM((2, *a.shape[1:]), a.dtype)

    def sums(*shape):
        return pltpu.VMEM(shape, f32)

    scratch = [
        ("outer_v", twice(outer_params)),
        ("inner_v", twice(inner_params)),
        ("narrow_v", twice(narrow)),
        ("dilated_v", twice(dilated)),
        ("restore_v", twice(restore)),
        ("param_sems", pltpu.SemaphoreType.DMA((3, 5))),
        ("count_room", SmallSum.scratch(8, 128, levels)),
        ("small_room", SmallSum.scratch(32, inner, levels)),
        ("halo_rooms", [Halo.scratch(count, inner) for _ in range(4)]),
        ("halves_room", Halves.scratch(count, rows, half)),
        ("grad_arrivals", pltpu.SemaphoreType.DMA((count,))),
        ("pads", sums(2, rows + 2 * REACH, inner)),
        ("narrow_sum", sums(width, inner)),
        ("dilated_sum", sums(deep, inner)),
        ("restore_sum", sums(inner, width)),
        ("wide_sums", [sums(16, width)] * 2),
        ("bias_sums", [sums(8, width)] * 2),
        ("upper_sums", [sums(24, inner)] * 2),
        ("small_sums", [sums(24, inner)] * 2),
        ("parts", [pltpu.VMEM((2 * width + deep, inner), bf16)] * 2),
        ("sum_rooms", [BlockSum.scratch(sizes, inner, levels) for _ in range(2)]),
    ]
    names = [a[0] for a in args] + [a[0] for a in results] + [a[0] for a in scratch]
    outs = pl.pallas_call(
        functools.partial(whole, names, count, sizes, residues),
        out_shape=[jax.ShapeDtypeStruct(shape, dtype) for _, shape, dtype, _ in results],
        in_specs=[a[2] for a in args],
        out_specs=[a[3] for a in results],
        scratch_shapes=[a[1] for a in scratch],
        compiler_params=pltpu.CompilerParams(
            vmem_limit_bytes=VMEM_LIMIT, collective_id=0, has_side_effects=True
        ),
        name="whole",
    )(*[a[1] for a in args])
    block_output, input_grad, joined_total, restore_total, smalls, counts = outs[:6]
    accuracy = counts[:2, :TYPES].astype(jnp.int32)
    smalls = lax.dynamic_slice_in_dim(smalls, core * 16, 16, 0)
    narrow_total = joined_total[:width].astype(f32)
    dilated_total = joined_total[width:].astype(f32)
    restore_total = restore_total.astype(f32)
    outer_total = smalls[: 3 * width // inner].reshape(3, width)
    inner_total = smalls[3 * width // inner :][:6]

    return (
        block_output,
        input_grad,
        outer_total[None],
        narrow_total[None],
        dilated_total.reshape(1, KERNEL, inner, inner),
        restore_total[None],
        inner_total[None],
        accuracy,
    )


def solution(mesh):
    in_specs = (
        P("dp", "seq", None),
        P("dp", "seq", None),
        P("dp", "seq"),
        P("dp", "seq"),
        P("dp", "seq"),
        P("pipe", None, None),
        P("pipe", None, None),
        P("pipe", None, None, None),
        P("pipe", None, None),
        P("pipe", None, None),
    )
    out_specs = (
        P("dp", "seq", "pipe"),
        P("dp", "seq", "pipe"),
        P("pipe", None, None),
        P("pipe", None, None),
        P("pipe", None, None, None),
        P("pipe", None, None),
        P("pipe", None, None),
        P(),
    )
    return jax.shard_map(shards, mesh=mesh, in_specs=in_specs, out_specs=out_specs, check_vma=False)
```

time: 2770 us -> 330 us (0.12); the launches traced: 2730 us -> 329 us
  other arithmetic: 833 us -> 12.9 us
  matrix products: 726 us -> 0 us
  local copies, waits for them, and re-layouts: 451 us -> 13.6 us
  starting transfers between devices: 395 us -> 0 us
  Pallas kernels: 0 us -> 302 us
  waiting for transfers between devices: 190 us -> 0 us
  blocking collectives: 95.9 us -> 0 us
  loops' own time: 29.2 us -> 0 us
    dot_general x225 -> x0, matrix products: 726 us -> none  [the longest x25 130 us: block_backward(): jnp.dot(hidden_low, narrow_w.T, preferred_element_type=jnp.float32)]
    ppermute x151 -> x0, starting transfers between devices: 395 us -> none  [the longest x50 265 us: extended(): lax.ppermute(lax.slice_in_dim(block, block.shape[dim] - width, None, axis...]
    reduce_sum x350 -> x0, other arithmetic: 341 us -> none  [the longest x125 78.6 us: norm_act(): spread = jnp.mean(centered * centered, axis=-1, keepdims=True)]
    pallas_call x0 -> x1, Pallas kernels: none -> 302 us  [shards(): pl.pallas_call(functools.partial(whole, names, count, sizes, residues), o...]
    dynamic_update_slice x125 -> x0, other arithmetic: 248 us -> none  [place(): return lax.dynamic_update_index_in_dim(buffer, chosen, slot_index, 0)]
    psum x1 -> x0, waiting for transfers between devices: 177 us -> none  [shards(): lax.psum((outer_sum, narrow_sum, dilated_sum, restore_sum, inner_sum), ('...]
    while x1075 -> x0, local copies, waits for them, and re-layouts: 174 us -> none
    dynamic_slice x100 -> x0, local copies, waits for them, and re-layouts: 153 us -> none  [place(): previous = lax.dynamic_index_in_dim(buffer, slot_index, 0, keepdims=False)]
  transfers between devices with their start and end apart: 152 -> 0, of which waited for: 26 -> 0; matrix products, arithmetic and copies ran while one was open for 25% -> 0% of each run, Pallas kernels for 0% -> 0%
where the time goes in v4:
time: 330 us; the launch traced here: 329 us
  Pallas kernels  302 us (92%)
  local copies, waits for them, and re-layouts  13.6 us (4%)
  other arithmetic  12.9 us (4%)
    pallas_call x1, Pallas kernels, shards(): pl.pallas_call(functools.partial(whole, names, count, sizes, residues), o...  302 us
    unnamed x15, local copies, waits for them, and re-layouts  9.06 us

profile of v4, /device:TPU:0, one launch (start us, length us, event | category | flops | bytes accessed | tf_op | source)
XLA Modules:
  0.0 329.0 jit_solution(6590937592052716743)
XLA Ops:
  0.6 0.8 compare_select_fusion
  1.5 1.9 select_reduce_fusion.1
  3.4 0.6 pad.4.refs_3_
  4.0 0.6 broadcast_in_dim.40.refs_2_
  4.6 1.3 copy.26.refs_4_
  5.9 1.3 copy.27.refs_5_
  7.3 301.8 %whole.1 = (bf16[24,256,512]{2,1,0:T(8,128)(2,1)}, bf16[24,256,512]{2,1,0:T(8,128)(2,1)}, bf16[3584,512]{1,0:T(8,128)(2,1)}, bf16[512,1024]{1,0:T(8,128)(2,1)}, ...) custom-call(bf16[24,256,1024]{2,1,0:T(8,128)(2,1)} %refs_0_.1, ...), custom_call_target="tpu_custom_call" | custom-call | tf_op jit(solution)/shard_map/whole/pallas_call | solution.py:887
  309.1 0.8 dynamic-slice_bitcast_fusion
  309.9 0.6 broadcast_in_dim_reshape.4
  310.5 0.6 copy.29
  311.1 1.9 slice.19
  313.1 0.0 slice-start.2
  313.1 0.0 copy-start
  313.1 0.0 slice-start.3
  313.1 3.4 %convert.4 = f32[1,5,512,512]{3,2,1,0:T(8,128)} convert(bf16[1,5,512,512]{3,2,1,0:T(8,128)(2,1)S(1)} %bitcast.12) | non-fusion elementwise | flops 1310720 | bytes 7864320 | tf_op jit(solution)/shard_map/reshape | solution.py:912
  316.5 3.5 %bitcast_convert_fusion.1 = f32[1,1024,512]{2,1,0:T(8,128)} fusion(bf16[3584,512]{1,0:T(8,128)(2,1)} %get-tuple-element.17), kind=kLoop, calls=%fused_computation.1 | loop fusion | flops 524288 | bytes 3145728 | tf_op jit(solution)/shard_map/broadcast_in_dim | solution.py:911
  320.0 0.0 copy-done
  320.0 1.6 bitcast_convert_fusion
  321.5 1.7 slice_convert_fusion
  323.2 0.0 slice-done.2
  323.2 0.0 slice-done.3
  323.2 2.8 copy.32
  326.1 0.3 slice-done.1
  326.3 2.7 copy.33
  (6 shorter events, 0.0 us)
Async XLA Ops:
  313.1 10.2 %slice-start.2 = ((s8[6291456]{0:T(1024)(128)(4,1)}), s8[4194304]{0:T(1024)(128)(4,1)S(1)}, s32[]{:S(2)}) async-start(s8[6291456]{0:T(1024)(128)(4,1)} %bitcast.15), calls=%async_computation.2 | async-start | bytes 8388608
  313.1 6.9 %copy-start = (bf16[512,1024]{1,0:T(8,128)(2,1)S(1)}, bf16[512,1024]{1,0:T(8,128)(2,1)}, u32[]{:S(2)}) copy-start(bf16[512,1024]{1,0:T(8,128)(2,1)} %get-tuple-element.18) | copy-start | bytes 3145732
  313.1 10.2 %slice-start.3 = ((s8[6291456]{0:T(1024)(128)(4,1)}), s8[2097152]{0:T(1024)(128)(4,1)S(1)}, s32[]{:S(2)}) async-start(s8[6291456]{0:T(1024)(128)(4,1)} %bitcast.15), calls=%async_computation.3 | async-start | bytes 4194304
  320.0 6.1 %slice-start = ((s8[6291456]{0:T(1024)(128)(4,1)}), s8[4194304]{0:T(1024)(128)(4,1)S(1)}, s32[]{:S(2)}) async-start(s8[6291456]{0:T(1024)(128)(4,1)} %bitcast.13), calls=%async_computation | async-start | bytes 8388608
  323.2 3.1 slice-start.1

commit v5 on v4

--- a/solution.py
+++ b/solution.py
@@ -289,19 +289,26 @@
         lax.fori_loop(0, self.count, body, 0)
 
 
-def group_sizes(inner, width):
-    upper = KERNEL * inner // 2
-    return [upper - upper // 5 * 2, upper // 5 * 2, width // 2, width // 2]
+def groups_of(inner, width):
+    joined = width + KERNEL * inner
+    half = joined // 2
+    out, at = [(width // 2, joined, width // 2)], 0
+    while at < half:
+        rows = min(width // 2, half - at)
+        out.append((rows, at, half))
+        at += rows
+    return out
 
 
 class BlockSum:
-    def __init__(self, place, block, sizes, part, out, room):
-        self.place, self.block, self.sizes, self.part, self.out = place, block, sizes, part, out
+    def __init__(self, place, block, groups, part, out, room):
+        self.place, self.block, self.part, self.out = place, block, part, out
+        self.groups, sizes = groups, [g[0] for g in groups]
+        self.sizes = sizes
         self.theirs, self.sbuf, self.rbuf, self.res = room[:4]
         self.core_sems, self.send_sems, self.recv_sems, self.out_sems = room[4:]
         self.levels = len(place.stages)
         self.starts = [sum(sizes[:g]) for g in range(len(sizes))]
-        self.half = sum(sizes)
         sent = [sum(self.lengths(n, self.levels)[1:]) for n in sizes]
         self.bases = [sum(sent[:g]) for g in range(len(sizes))]
 
@@ -314,7 +321,8 @@
         return out
 
     @staticmethod
-    def scratch(sizes, width, levels):
+    def scratch(groups, width, levels):
+        sizes = [g[0] for g in groups]
         rows, groups = sum(sizes), len(sizes)
         sent = sum(sum(BlockSum.lengths(n, levels)[1:]) for n in sizes)
         dma = pltpu.SemaphoreType.DMA
@@ -344,7 +352,10 @@
 
     def value(self, g, s, start, n):
         lengths, spots = self.lengths(self.sizes[g], self.levels), self.spots(g)
-        terms = [(self.part, self.place.core * self.half + start), (self.theirs, start)]
+        terms = [
+            (self.part, self.row(g, self.place.core) + (start - self.starts[g])),
+            (self.theirs, start),
+        ]
         for k in range(s):
             at = self.base(g, k) + (start - spots[k + 1][0])
             if lengths[k + 1] == lengths[k]:
@@ -356,9 +367,13 @@
             total = term if total is None else total + term
         return total
 
+    def row(self, g, half):
+        _, at, stride = self.groups[g]
+        return at + half * stride
+
     def core_copy(self, g):
         n = self.sizes[g]
-        source = pl.multiple_of((1 - self.place.core) * self.half + self.starts[g], UNIT)
+        source = pl.multiple_of(self.row(g, 1 - self.place.core), UNIT)
         return remote(
             self.part.at[pl.ds(source, n)],
             self.theirs.at[pl.ds(self.starts[g], n)],
@@ -402,12 +417,13 @@
         )
 
     def target(self, g, half):
-        n, at = self.sizes[g], self.starts[g] + half * self.half
-        joined, restore = self.out
-        top = joined.shape[0]
-        if at < top:
-            return joined.at[pl.ds(at, n)]
-        return restore.at[:, pl.ds(at - top, n)]
+        n, at = self.sizes[g], self.row(g, half)
+        narrow, dilated, restore = self.out
+        for ref in (narrow, dilated):
+            if at < ref.shape[0]:
+                return ref.at[pl.ds(at, n)]
+            at -= ref.shape[0]
+        return restore.at[:, pl.ds(at, n)]
 
     def keep(self, g, half):
         at = pl.ds(self.starts[g], self.sizes[g])
@@ -470,6 +486,50 @@
                         self.give(g, half).wait_send()
 
 
+STEP_TIMES = (5.0, 2.3, 2.9, 0.7)
+LATENCY = 2.5
+CHIP_RATE = 1.0e5
+CORE_RATE = 5.0e5
+
+
+def plan(place, groups, width, begins, count):
+    levels = len(place.stages)
+    times, now = [], 0.0
+    for k in range(3 * count + 400):
+        times.append(now)
+        now += STEP_TIMES[min(k // count, 3)]
+
+    def sent(g, t):
+        rows = groups[g][0]
+        lengths = BlockSum.lengths(rows, levels)
+        size = 2 * width
+        if t in (0, 2 * levels + 1):
+            return "pipe", rows * size / CORE_RATE
+        s = t - 1 if t <= levels else 2 * levels - t
+        axis, bit, _ = place.stages[s]
+        flows = 1 if axis == "seq" else 2 << bit
+        if t > levels and lengths[s] == lengths[s + 1]:
+            flows = 0
+        return axis, lengths[s + 1] * size * flows / CHIP_RATE
+
+    due, free = {}, {}
+    ready = {(block, g): times[at] for block, g, at in begins}
+    tick = dict.fromkeys(ready, 0)
+    for k, now in enumerate(times):
+        for key in [key for key in ready if ready[key] <= now]:
+            t = tick[key]
+            due.setdefault(k, []).append((*key, t))
+            tick[key] += 1
+            if t == 2 * levels + 2:
+                del ready[key]
+                continue
+            link, busy = sent(key[1], t)
+            free[link] = max(free.get(link, 0.0), now) + busy
+            ready[key] = free[link] + LATENCY
+    assert not ready
+    return due
+
+
 class SmallSum:
     def __init__(self, place, total, arrived, sems):
         self.place, self.total, self.arrived, self.sems = place, total, arrived, sems
@@ -522,10 +582,8 @@
     return gm
 
 
-def block_in_back(
-    d, stream, grad_out, hidden, gm, outer, inner, narrow, dilated, narrow_sum, dilated_sum, wide_sum, small_sum, pad, gm_pad
-):
-    rows = stream.shape[0]
+def convolution_back(d, hidden, gm, inner, dilated, dilated_sum, small_sum, pad, gm_pad):
+    rows = hidden.shape[0]
     grad_second = None
     for k, piece in enumerate(taps(gm_pad, rows, d, -1)):
         term = dot_nt(piece, dilated[k])
@@ -538,12 +596,14 @@
     small_sum[0:8] += fold(gh.astype(f32))
     small_sum[8:16] += gain
     small_sum[16:24] += shift
-    first = Back(stream, row(outer, 0), row(outer, 1))
-    narrow_sum[...] += dot_tn(first.act, gh)
+    return gh
+
+
+def stream_back(first, gh, narrow, wide_sum):
     gx, gain, shift = first.grad(dot_nt(gh, narrow[...]))
     wide_sum[0:8] += gain
     wide_sum[8:16] += shift
-    return grad_out + gx
+    return gx
 
 
 def clear(*refs):
@@ -557,7 +617,7 @@
             setattr(self, name, ref)
 
 
-def whole(names, count, sizes, residues, *refs):
+def whole(names, count, groups, residues, *refs):
     r = Refs(names, refs)
     place = Place()
     core = place.core
@@ -567,11 +627,11 @@
     small_counts = SmallSum(place, *r.count_room)
     halos = [Halo(place, *room) for room in r.halo_rooms]
     outputs = Halves(place, count, r.block_output, *r.halves_room)
-    grads = Halves(place, count, r.input_grad, *r.halves_room[:3], r.grad_arrivals)
+    grads = Halves(place, count, r.input_grad, *r.grads_room)
     outer, inner_p, narrow, dilated, restore = r.outer_v, r.inner_v, r.narrow_v, r.dilated_v, r.restore_v
     params = ((r.outer, outer), (r.inner, inner_p), (r.narrow, narrow), (r.dilated, dilated), (r.restore, restore))
     sets = [
-        BlockSum(place, block, sizes, r.parts[block], (r.joined_total, r.restore_total), r.sum_rooms[block])
+        BlockSum(place, block, groups, r.parts[block], (r.narrow_total, r.dilated_total, r.restore_total), r.sum_rooms[block])
         for block in (0, 1)
     ]
 
@@ -626,7 +686,7 @@
     for k in range(3):
         arrive(k, 0)
 
-    def first(i, x, hidden_out, second_out):
+    def first(i, x, act_out, hidden_out, second_out):
         for k in range(1, small_counts.stages):
 
             @pl.when(i == k)
@@ -636,13 +696,14 @@
                 small_counts.start(k)
 
         act = norm_act(x[0].astype(f32), row(outer.at[0], 0), row(outer.at[0], 1))
+        act_out[0] = act
         hidden = dot(act, narrow[0]) + row(inner_p.at[0], 0)
         hidden_out[0] = hidden
         second = norm_act(hidden, row(inner_p.at[0], 2), row(inner_p.at[0], 3))
         second_out[0] = second
         halos[0].send(i, second)
 
-    over(first, [r.inputs], [r.hidden0, r.second0])
+    over(first, [r.inputs], [r.first0, r.hidden0, r.second0])
     small_counts.end(small_counts.stages - 1)
     r.counts_out[...] = small_counts.total[small_counts.stages]
     for k in range(len(params)):
@@ -669,45 +730,56 @@
 
     over(second, [r.inputs, r.second0], [r.mixed0, r.middle, r.hidden1, r.second1])
 
-    def turn(i, middle, second_in, cot, gm_out):
+    def turn(i, second_in, cot, third_out, gm_out):
         halos[1].take(i)
         halos[1].around(r.pads.at[0], i, second_in[0])
         windows = jnp.concatenate(taps(r.pads.at[0], rows, SECOND_DILATION, 1), axis=1)
         mixed = dot(windows, dilated[1].reshape(taps_rows, inner)) + row(inner_p.at[1], 1)
         back = Back(mixed, row(inner_p.at[1], 4), row(inner_p.at[1], 5))
-        y = middle[0].astype(f32) + (dot(back.act, restore[1]) + row(outer.at[1], 2))
-        outputs.send(i, y.astype(bf16))
+        third_out[0] = back.act
         grad_low = seeded(cot[0], flags_of(i)).astype(bf16)
         gm = block_out_back(back, grad_low, restore.at[1], r.restore_sum, r.bias_sums[1], r.upper_sums[1])
         gm_out[0] = gm
         halos[2].send(i, gm)
 
-    over(turn, [r.middle, r.second1, r.cotangent], [r.gm1])
-    outputs.end()
+    over(turn, [r.second1, r.cotangent], [r.third1, r.gm1])
     write_restore(r.parts[1], r.restore_sum)
     clear(r.restore_sum)
 
+    begins = [(1, 0, 0)]
+    begins += [(1, g, count) for g in range(1, len(groups))]
+    begins += [(0, 0, count + 4)]
+    begins += [(0, g, 2 * count) for g in range(1, len(groups))]
+    due = plan(place, groups, inner, begins, count)
+
+    def beside(base, i):
+        for k in range(count):
+            if base + k in due:
+
+                @pl.when(i == k)
+                def _():
+                    for block, g, t in due[base + k]:
+                        sets[block].step(g, t)
+
     def between(i, middle, cot, hidden, second_in, gm, mixed, gx_out, gm_out):
+        beside(0, i)
         halos[2].take(i)
         halos[2].around(r.pads.at[1], i, gm[0])
         halos[1].around(r.pads.at[0], i, second_in[0])
-        gx = block_in_back(
+        gh = convolution_back(
             SECOND_DILATION,
-            middle[0].astype(f32),
-            seeded(cot[0], flags_of(i)),
             hidden[0],
             gm[0],
-            outer.at[1],
             inner_p.at[1],
-            narrow.at[1],
             dilated.at[1],
-            r.narrow_sum,
             r.dilated_sum,
-            r.wide_sums[1],
             r.small_sums[1],
             r.pads.at[0],
             r.pads.at[1],
         )
+        first = Back(middle[0].astype(f32), row(outer.at[1], 0), row(outer.at[1], 1))
+        r.narrow_sum[...] += dot_tn(first.act, gh)
+        gx = seeded(cot[0], flags_of(i)) + stream_back(first, gh, narrow.at[1], r.wide_sums[1])
         gx_out[0] = gx.astype(gx_out.dtype)
         back = Back(mixed[0], row(inner_p.at[0], 4), row(inner_p.at[0], 5))
         gm = block_out_back(back, gx.astype(bf16), restore.at[0], r.restore_sum, r.bias_sums[0], r.upper_sums[0])
@@ -719,64 +791,53 @@
     write_restore(r.parts[0], r.restore_sum)
     clear(r.narrow_sum, r.dilated_sum)
 
-    groups = range(len(sizes))
-    steps = sets[0].steps()
-    lag = [g // 2 for g in groups]
-
-    def beside(t):
-        for g in groups:
-            if 0 <= t - lag[g] < steps:
-                sets[1].step(g, t - lag[g])
-
-    ticks = steps + max(lag)
-
-    def last(i, x, gx_in, hidden, second_in, gm):
-        for t in range(min(ticks, count)):
-
-            @pl.when(i == t)
-            def _():
-                beside(t)
-
+    def inward(i, act, hidden, second_in, gm, gh_out):
+        beside(count, i)
         halos[3].take(i)
         halos[3].around(r.pads.at[1], i, gm[0])
         halos[0].around(r.pads.at[0], i, second_in[0])
-        gx = block_in_back(
+        gh = convolution_back(
             FIRST_DILATION,
-            x[0].astype(f32),
-            gx_in[0].astype(f32),
             hidden[0],
             gm[0],
-            outer.at[0],
             inner_p.at[0],
-            narrow.at[0],
             dilated.at[0],
-            r.narrow_sum,
             r.dilated_sum,
-            r.wide_sums[0],
             r.small_sums[0],
             r.pads.at[0],
             r.pads.at[1],
         )
+        r.narrow_sum[...] += dot_tn(act[0], gh)
+        gh_out[0] = gh
+
+    over(inward, [r.first0, r.hidden0, r.second0, r.gm0], [r.gh0])
+    write_joined(r.parts[0], r.narrow_sum, r.dilated_sum)
+
+    def last(i, x, gx_in, gh, middle, third):
+        beside(2 * count, i)
+        y = middle[0].astype(f32) + (dot(third[0], restore[1]) + row(outer.at[1], 2))
+        outputs.send(i, y.astype(bf16))
+        first = Back(x[0].astype(f32), row(outer.at[0], 0), row(outer.at[0], 1))
+        gx = gx_in[0].astype(f32) + stream_back(first, gh[0], narrow.at[0], r.wide_sums[0])
         grads.send(i, gx.astype(bf16))
 
-    over(last, [r.inputs, r.gx1, r.hidden0, r.second0, r.gm0], [])
-    write_joined(r.parts[0], r.narrow_sum, r.dilated_sum)
+    over(last, [r.inputs, r.gx1, r.gh0, r.middle, r.third1], [])
 
     small = SmallSum(place, *r.small_room)
     small.total[0] = jnp.zeros_like(small.total[0])
     for b in (0, 1):
         gather_small(small.total, b, r.bias_sums[b], r.upper_sums[b], r.wide_sums[b], r.small_sums[b])
-    for t in range(max(steps + len(sizes) - 1, small.stages + 1, ticks - count)):
-        if count + t < ticks:
-            beside(count + t)
-        for g in groups:
-            if 0 <= t - g < steps:
-                sets[0].step(g, t - g)
+    after = sorted(at for at in due if at >= 3 * count)
+    for t in range(max(len(after), small.stages + 1)):
+        if t < len(after):
+            for block, g, k in due[after[t]]:
+                sets[block].step(g, k)
         if 0 < t <= small.stages:
             small.end(t - 1)
         if t < small.stages:
             small.start(t)
     r.small_out[...] = small.total[small.stages]
+    outputs.end()
     grads.end()
 
 
@@ -821,7 +882,7 @@
     counts = jnp.pad(counts, ((0, 8 - 2), (0, 128 - TYPES)))
 
     flags = mask_flags.astype(f32)[:, None, :]
-    sizes = group_sizes(inner, width)
+    groups = groups_of(inner, width)
     residues = float(chip_seqs * lax.axis_size("dp") * LENGTH)
     deep = KERNEL * inner
     any_space, vmem = pl.BlockSpec(memory_space=pl.ANY), pl.BlockSpec(memory_space=pltpu.VMEM)
@@ -839,10 +900,14 @@
     results = [
         ("block_output", (chip_seqs, rows, half), bf16, any_space),
         ("input_grad", (chip_seqs, rows, half), bf16, any_space),
-        ("joined_total", (width + deep, inner), bf16, any_space),
+        ("narrow_total", (width, inner), bf16, any_space),
+        ("dilated_total", (deep, inner), bf16, any_space),
         ("restore_total", (inner, width), bf16, any_space),
         ("small_out", (32, inner), f32, vmem),
         ("counts_out", (8, 128), f32, vmem),
+        ("third1", (count, rows, inner), bf16, any_space),
+        ("first0", (count, rows, width), bf16, any_space),
+        ("gh0", (count, rows, inner), bf16, any_space),
         ("hidden0", (count, rows, inner), f32, any_space),
         ("hidden1", (count, rows, inner), f32, any_space),
         ("mixed0", (count, rows, inner), f32, any_space),
@@ -871,7 +936,7 @@
         ("small_room", SmallSum.scratch(32, inner, levels)),
         ("halo_rooms", [Halo.scratch(count, inner) for _ in range(4)]),
         ("halves_room", Halves.scratch(count, rows, half)),
-        ("grad_arrivals", pltpu.SemaphoreType.DMA((count,))),
+        ("grads_room", Halves.scratch(count, rows, half)),
         ("pads", sums(2, rows + 2 * REACH, inner)),
         ("narrow_sum", sums(width, inner)),
         ("dilated_sum", sums(deep, inner)),
@@ -881,11 +946,11 @@
         ("upper_sums", [sums(24, inner)] * 2),
         ("small_sums", [sums(24, inner)] * 2),
         ("parts", [pltpu.VMEM((2 * width + deep, inner), bf16)] * 2),
-        ("sum_rooms", [BlockSum.scratch(sizes, inner, levels) for _ in range(2)]),
+        ("sum_rooms", [BlockSum.scratch(groups, inner, levels) for _ in range(2)]),
     ]
     names = [a[0] for a in args] + [a[0] for a in results] + [a[0] for a in scratch]
     outs = pl.pallas_call(
-        functools.partial(whole, names, count, sizes, residues),
+        functools.partial(whole, names, count, groups, residues),
         out_shape=[jax.ShapeDtypeStruct(shape, dtype) for _, shape, dtype, _ in results],
         in_specs=[a[2] for a in args],
         out_specs=[a[3] for a in results],
@@ -895,11 +960,11 @@
         ),
         name="whole",
     )(*[a[1] for a in args])
-    block_output, input_grad, joined_total, restore_total, smalls, counts = outs[:6]
+    block_output, input_grad, narrow_total, dilated_total, restore_total, smalls, counts = outs[:7]
     accuracy = counts[:2, :TYPES].astype(jnp.int32)
     smalls = lax.dynamic_slice_in_dim(smalls, core * 16, 16, 0)
-    narrow_total = joined_total[:width].astype(f32)
-    dilated_total = joined_total[width:].astype(f32)
+    narrow_total = narrow_total.astype(f32)
+    dilated_total = dilated_total.astype(f32)
     restore_total = restore_total.astype(f32)
     outer_total = smalls[: 3 * width // inner].reshape(3, width)
     inner_total = smalls[3 * width // inner :][:6]

time: 330 us -> 283 us (0.86)
  Pallas kernels: 302 us -> 258 us
    pallas_call x1, Pallas kernels: 302 us -> 258 us  [shards(): pl.pallas_call(functools.partial(whole, names, count, groups, residues),...]
    unnamed x15 -> x17, local copies, waits for them, and re-layouts: 9.06 us -> 9.06 us
where the time goes in v5:
time: 283 us
  Pallas kernels  258 us (91%)
  other arithmetic  12.6 us (4%)
  local copies, waits for them, and re-layouts  11.8 us (4%)
    pallas_call x1, Pallas kernels, shards(): pl.pallas_call(functools.partial(whole, names, count, groups, residues),...  258 us
    unnamed x17, local copies, waits for them, and re-layouts  9.06 us

profile of v5, /device:TPU:0, one launch (start us, length us, event | category | flops | bytes accessed | tf_op | source)
XLA Modules:
  0.0 282.6 jit_solution(15366580328008659949)
XLA Ops:
  0.6 0.8 compare_select_fusion
  1.5 1.9 select_reduce_fusion.1
  3.4 0.6 pad.4.refs_3_
  4.0 0.6 broadcast_in_dim.40.refs_2_
  4.6 1.3 copy.26.refs_4_
  5.9 1.3 copy.27.refs_5_
  7.3 257.6 %whole.1 = (bf16[24,256,512]{2,1,0:T(8,128)(2,1)}, bf16[24,256,512]{2,1,0:T(8,128)(2,1)}, bf16[1024,512]{1,0:T(8,128)(2,1)}, bf16[2560,512]{1,0:T(8,128)(2,1)}, ...) custom-call(bf16[24,256,1024]{2,1,0:T(8,128)(2,1)} %refs_0_.1, ...), custom_call_target="tpu_custom_call" | custom-call | tf_op jit(solution)/shard_map/whole/pallas_call | solution.py:952
  264.9 0.0 copy-start.1
  264.9 0.9 dynamic-slice_bitcast_fusion
  265.8 0.6 broadcast_in_dim_reshape.4
  266.4 0.6 copy.29
  267.0 0.0 slice-start.2
  267.0 5.0 %convert.4 = f32[1,5,512,512]{3,2,1,0:T(8,128)} convert(bf16[1,5,512,512]{3,2,1,0:T(8,128)(2,1)} %bitcast.16) | non-fusion elementwise | flops 1310720 | bytes 7864320 | tf_op jit(solution)/shard_map/reshape | solution.py:977
  272.0 0.0 copy-done.1
  272.0 1.6 bitcast_convert_fusion
  273.5 0.0 copy-done
  273.5 1.6 bitcast_convert_fusion.1
  275.1 1.6 slice_convert_fusion
  276.8 0.0 slice-done.2
  276.8 0.0 slice-done.3
  276.8 2.8 %copy.32 = bf16[24,256,512]{2,1,0:T(8,128)(2,1)} copy(bf16[24,256,512]{2,1,0:T(8,128)(2,1)S(1)} %bitcast.15) | data formatting | bytes 12582912
  279.6 0.0 slice-done
  279.6 0.3 slice-done.1
  279.9 2.7 copy.33
  (7 shorter events, 0.0 us)
Async XLA Ops:
  264.9 7.1 %copy-start.1 = (bf16[512,1024]{1,0:T(8,128)(2,1)S(1)}, bf16[512,1024]{1,0:T(8,128)(2,1)}, u32[]{:S(2)}) copy-start(bf16[512,1024]{1,0:T(8,128)(2,1)} %get-tuple-element.20) | copy-start | bytes 3145732
  267.0 9.8 %slice-start.2 = ((s8[6291456]{0:T(1024)(128)(4,1)}), s8[4194304]{0:T(1024)(128)(4,1)S(1)}, s32[]{:S(2)}) async-start(s8[6291456]{0:T(1024)(128)(4,1)} %bitcast.14), calls=%async_computation.2 | async-start | bytes 8388608
  267.0 6.6 %copy-start = (bf16[1024,512]{1,0:T(8,128)(2,1)S(1)}, bf16[1024,512]{1,0:T(8,128)(2,1)}, u32[]{:S(2)}) copy-start(bf16[1024,512]{1,0:T(8,128)(2,1)} %get-tuple-element.18) | copy-start | bytes 3145732
  267.0 9.8 %slice-start.3 = ((s8[6291456]{0:T(1024)(128)(4,1)}), s8[2097152]{0:T(1024)(128)(4,1)S(1)}, s32[]{:S(2)}) async-start(s8[6291456]{0:T(1024)(128)(4,1)} %bitcast.14), calls=%async_computation.3 | async-start | bytes 4194304
  273.5 6.1 %slice-start = ((s8[6291456]{0:T(1024)(128)(4,1)}), s8[4194304]{0:T(1024)(128)(4,1)S(1)}, s32[]{:S(2)}) async-start(s8[6291456]{0:T(1024)(128)(4,1)} %bitcast.12), calls=%async_computation | async-start | bytes 8388608
  276.8 3.1 %slice-start.1 = ((s8[6291456]{0:T(1024)(128)(4,1)}), s8[2097152]{0:T(1024)(128)(4,1)S(1)}, s32[]{:S(2)}) async-start(s8[6291456]{0:T(1024)(128)(4,1)} %bitcast.12), calls=%async_computation.1 | async-start | bytes 4194304

commit v6 on v5

--- a/solution.py
+++ b/solution.py
@@ -19,6 +19,7 @@
 f32 = jnp.float32
 bf16 = jnp.bfloat16
 KEPT = bf16
+STEP_SEQS = (2, 2, 2, 1, 2, 2)
 
 ROOT_HALF = 0.7071067811865476
 INV_ROOT_2PI = 0.3989422804014327
@@ -292,7 +293,7 @@
 def groups_of(inner, width):
     joined = width + KERNEL * inner
     half = joined // 2
-    out, at = [(width // 2, joined, width // 2)], 0
+    out, at = [(width // 2, 0, width // 2)], 0
     while at < half:
         rows = min(width // 2, half - at)
         out.append((rows, at, half))
@@ -302,7 +303,7 @@
 
 class BlockSum:
     def __init__(self, place, block, groups, part, out, room):
-        self.place, self.block, self.part, self.out = place, block, part, out
+        self.place, self.block, self.parts, self.out = place, block, part, out
         self.groups, sizes = groups, [g[0] for g in groups]
         self.sizes = sizes
         self.theirs, self.sbuf, self.rbuf, self.res = room[:4]
@@ -353,7 +354,7 @@
     def value(self, g, s, start, n):
         lengths, spots = self.lengths(self.sizes[g], self.levels), self.spots(g)
         terms = [
-            (self.part, self.row(g, self.place.core) + (start - self.starts[g])),
+            (self.part(g), self.row(g, self.place.core) + (start - self.starts[g])),
             (self.theirs, start),
         ]
         for k in range(s):
@@ -367,6 +368,9 @@
             total = term if total is None else total + term
         return total
 
+    def part(self, g):
+        return self.parts[0 if g > 0 else 1]
+
     def row(self, g, half):
         _, at, stride = self.groups[g]
         return at + half * stride
@@ -375,7 +379,7 @@
         n = self.sizes[g]
         source = pl.multiple_of(self.row(g, 1 - self.place.core), UNIT)
         return remote(
-            self.part.at[pl.ds(source, n)],
+            self.part(g).at[pl.ds(source, n)],
             self.theirs.at[pl.ds(self.starts[g], n)],
             self.core_sems.at[g, 0],
             self.core_sems.at[g, 1],
@@ -419,11 +423,10 @@
     def target(self, g, half):
         n, at = self.sizes[g], self.row(g, half)
         narrow, dilated, restore = self.out
-        for ref in (narrow, dilated):
-            if at < ref.shape[0]:
-                return ref.at[pl.ds(at, n)]
-            at -= ref.shape[0]
-        return restore.at[:, pl.ds(at, n)]
+        if g == 0:
+            return restore.at[:, pl.ds(at, n)]
+        top = narrow.shape[0]
+        return narrow.at[pl.ds(at, n)] if at < top else dilated.at[pl.ds(at - top, n)]
 
     def keep(self, g, half):
         at = pl.ds(self.starts[g], self.sizes[g])
@@ -486,18 +489,20 @@
                         self.give(g, half).wait_send()
 
 
-STEP_TIMES = (5.0, 2.3, 2.9, 0.7)
+SEQ_TIMES = (5.0, 2.1, 2.5)
+AFTER_TIME = 0.7
 LATENCY = 2.5
 CHIP_RATE = 1.0e5
 CORE_RATE = 5.0e5
 
 
-def plan(place, groups, width, begins, count):
+def plan(place, groups, width, begins, spans):
     levels = len(place.stages)
     times, now = [], 0.0
-    for k in range(3 * count + 400):
-        times.append(now)
-        now += STEP_TIMES[min(k // count, 3)]
+    for steps, length in (*spans, (400, AFTER_TIME)):
+        for _ in range(steps):
+            times.append(now)
+            now += length
 
     def sent(g, t):
         rows = groups[g][0]
@@ -582,15 +587,14 @@
     return gm
 
 
-def convolution_back(d, hidden, gm, inner, dilated, dilated_sum, small_sum, pad, gm_pad):
-    rows = hidden.shape[0]
+def convolution_back(hidden, gm, windows, gm_taps, inner, dilated, dilated_sum, small_sum):
+    width = inner.shape[1]
     grad_second = None
-    for k, piece in enumerate(taps(gm_pad, rows, d, -1)):
-        term = dot_nt(piece, dilated[k])
+    for k, piece in enumerate(gm_taps):
+        term = dot_nt(piece, dilated[k * width : (k + 1) * width, :])
         grad_second = term if grad_second is None else grad_second + term
-    windows = jnp.concatenate(taps(pad, rows, d, 1), axis=1)
-    dilated_sum[...] += dot_tn(windows, gm)
-    back = Back(hidden, row(inner, 2), row(inner, 3))
+    dilated_sum[...] += dot_tn(windows(), gm())
+    back = Back(hidden(), row(inner, 2), row(inner, 3))
     gv, gain, shift = back.grad(grad_second)
     gh = gv.astype(bf16)
     small_sum[0:8] += fold(gh.astype(f32))
@@ -623,25 +627,33 @@
     core = place.core
     rows, width = r.inputs.shape[1:]
     inner = r.narrow.shape[2]
-    taps_rows = KERNEL * inner
     small_counts = SmallSum(place, *r.count_room)
     halos = [Halo(place, *room) for room in r.halo_rooms]
     outputs = Halves(place, count, r.block_output, *r.halves_room)
     grads = Halves(place, count, r.input_grad, *r.grads_room)
-    outer, inner_p, narrow, dilated, restore = r.outer_v, r.inner_v, r.narrow_v, r.dilated_v, r.restore_v
-    params = ((r.outer, outer), (r.inner, inner_p), (r.narrow, narrow), (r.dilated, dilated), (r.restore, restore))
-    sets = [
-        BlockSum(place, block, groups, r.parts[block], (r.narrow_total, r.dilated_total, r.restore_total), r.sum_rooms[block])
-        for block in (0, 1)
-    ]
+    outer, inner_p, joined, restore = r.outer_v, r.inner_v, r.joined_v, r.restore_v
+    narrow = [joined.at[b, 0:width] for b in (0, 1)]
+    dilated = [joined.at[b, width : width + KERNEL * inner] for b in (0, 1)]
+    params = (
+        (r.outer, lambda at: outer.at[at]),
+        (r.inner, lambda at: inner_p.at[at]),
+        (r.narrow, lambda at: joined.at[at, 0:width]),
+        (r.dilated, lambda at: joined.at[at, width : width + KERNEL * inner]),
+        (r.restore, lambda at: restore.at[at]),
+    )
+    parts = [(joined.at[1], r.restore_parts[0]), (r.joined_part, r.restore_parts[1])]
+    totals = (r.narrow_total, r.dilated_total, r.restore_total)
+    sets = [BlockSum(place, b, groups, parts[b], totals, r.sum_rooms[b]) for b in (0, 1)]
+    seqs = [n if count % n == 0 else 1 for n in STEP_SEQS]
+    stage_steps = [count // n for n in seqs]
 
     def local(k):
         src, dst = params[k]
-        return pltpu.make_async_copy(src, dst.at[pl.ds(core, 1)], r.param_sems.at[0, k])
+        return pltpu.make_async_copy(src, dst(pl.ds(core, 1)), r.param_sems.at[0, k])
 
     def away(k):
         src, dst = params[k]
-        to = dst.at[pl.ds(core, 1)]
+        to = dst(pl.ds(core, 1))
         return remote(src, to, r.param_sems.at[1, k], r.param_sems.at[2, k], place.other_core())
 
     def arrive(k, block):
@@ -653,22 +665,61 @@
         def _():
             away(k).wait_recv()
 
-    def over(body, ins, outs):
+    def over(stage, body, ins, outs):
+        n, steps = seqs[stage], stage_steps[stage]
+
         def spec(a, own):
-            shape = (1, *a.shape[1:])
+            shape = (n, *a.shape[1:])
             if own:
-                return pl.BlockSpec(shape, lambda i: (core * count + i, 0, 0))
+                return pl.BlockSpec(shape, lambda i: (core * steps + i, 0, 0))
             return pl.BlockSpec(shape, lambda i: (i, 0, 0))
 
-        in_specs = [spec(a, a is r.inputs or a is r.cotangent) for a in ins]
-        out_specs = [spec(a, False) for a in outs]
+        def flat(*blocks):
+            def reader(ref):
+                return lambda: ref[...].reshape(n * rows, ref.shape[2])
+
+            def writer(ref):
+                def write(v):
+                    ref[...] = v.astype(ref.dtype).reshape(ref.shape)
+
+                return write
+
+            cut = len(ins)
+            body(pl.program_id(0), *map(reader, blocks[:cut]), *map(writer, blocks[cut:]))
+
         pipe = pltpu.emit_pipeline(
-            lambda *blocks: body(pl.program_id(0), *blocks),
-            grid=(count,),
-            in_specs=in_specs,
-            out_specs=out_specs,
+            flat,
+            grid=(steps,),
+            in_specs=[spec(a, a is r.inputs or a is r.cotangent) for a in ins],
+            out_specs=[spec(a, False) for a in outs],
         )
         pipe(*ins, *outs)
+
+    def each(stage, i):
+        n = seqs[stage]
+        return [(i * n + j, slice(j * rows, (j + 1) * rows)) for j in range(n)]
+
+    def surround(stage, halo, pads, i, values):
+        for j, (at, part) in enumerate(each(stage, i)):
+            halo.around(pads.at[j], at, values[part])
+
+    def tapped(stage, pads, d, direction):
+        found = [taps(pads.at[j], rows, d, direction) for j in range(seqs[stage])]
+        return [jnp.concatenate(pieces, axis=0) for pieces in zip(*found)]
+
+    def windows_of(stage, pads, d):
+        return jnp.concatenate(tapped(stage, pads, d, 1), axis=1)
+
+    def take(stage, halo, i):
+        for at, _ in each(stage, i):
+            halo.take(at)
+
+    def send(stage, sender, i, values):
+        for at, part in each(stage, i):
+            sender.send(at, values[part])
+
+    def seed_of(stage, i, cot):
+        return jnp.concatenate([seeded(cot[part], flags_of(at)) for at, part in each(stage, i)], axis=0)
 
     def flags_of(i):
         masked = jnp.sum(small_counts.total[small_counts.stages][1:2, :], axis=1, keepdims=True)
@@ -686,24 +737,29 @@
     for k in range(3):
         arrive(k, 0)
 
+    def count_step(k):
+        if k > 1:
+            small_counts.end(k - 1)
+        small_counts.start(k)
+
     def first(i, x, act_out, hidden_out, second_out):
-        for k in range(1, small_counts.stages):
+        for k in range(1, min(small_counts.stages, stage_steps[0])):
 
             @pl.when(i == k)
             def _():
-                if k > 1:
-                    small_counts.end(k - 1)
-                small_counts.start(k)
-
-        act = norm_act(x[0].astype(f32), row(outer.at[0], 0), row(outer.at[0], 1))
-        act_out[0] = act
-        hidden = dot(act, narrow[0]) + row(inner_p.at[0], 0)
-        hidden_out[0] = hidden
+                count_step(k)
+
+        act = norm_act(x().astype(f32), row(outer.at[0], 0), row(outer.at[0], 1))
+        act_out(act)
+        hidden = dot(act, narrow[0][...]) + row(inner_p.at[0], 0)
+        hidden_out(hidden)
         second = norm_act(hidden, row(inner_p.at[0], 2), row(inner_p.at[0], 3))
-        second_out[0] = second
-        halos[0].send(i, second)
-
-    over(first, [r.inputs], [r.first0, r.hidden0, r.second0])
+        second_out(second)
+        send(0, halos[0], i, second)
+
+    over(0, first, [r.inputs], [r.first0, r.hidden0, r.second0])
+    for k in range(stage_steps[0], small_counts.stages):
+        count_step(k)
     small_counts.end(small_counts.stages - 1)
     r.counts_out[...] = small_counts.total[small_counts.stages]
     for k in range(len(params)):
@@ -713,47 +769,50 @@
             arrive(k, 0)
 
     def second(i, x, second_in, mixed_out, middle_out, hidden_out, second_out):
-        halos[0].take(i)
-        halos[0].around(r.pads.at[0], i, second_in[0])
-        windows = jnp.concatenate(taps(r.pads.at[0], rows, FIRST_DILATION, 1), axis=1)
-        mixed = dot(windows, dilated[0].reshape(taps_rows, inner)) + row(inner_p.at[0], 1)
-        mixed_out[0] = mixed
+        take(1, halos[0], i)
+        surround(1, halos[0], r.pads, i, second_in())
+        windows = windows_of(1, r.pads, FIRST_DILATION)
+        mixed = dot(windows, dilated[0][...]) + row(inner_p.at[0], 1)
+        mixed_out(mixed)
         third = norm_act(mixed, row(inner_p.at[0], 4), row(inner_p.at[0], 5))
-        y = x[0].astype(f32) + (dot(third, restore[0]) + row(outer.at[0], 2))
-        middle_out[0] = y.astype(middle_out.dtype)
+        y = x().astype(f32) + (dot(third, restore[0]) + row(outer.at[0], 2))
+        middle_out(y)
         act = norm_act(y, row(outer.at[1], 0), row(outer.at[1], 1))
-        hidden = dot(act, narrow[1]) + row(inner_p.at[1], 0)
-        hidden_out[0] = hidden
+        hidden = dot(act, narrow[1][...]) + row(inner_p.at[1], 0)
+        hidden_out(hidden)
         second = norm_act(hidden, row(inner_p.at[1], 2), row(inner_p.at[1], 3))
-        second_out[0] = second
-        halos[1].send(i, second)
-
-    over(second, [r.inputs, r.second0], [r.mixed0, r.middle, r.hidden1, r.second1])
+        second_out(second)
+        send(1, halos[1], i, second)
+
+    over(1, second, [r.inputs, r.second0], [r.mixed0, r.middle, r.hidden1, r.second1])
 
     def turn(i, second_in, cot, third_out, gm_out):
-        halos[1].take(i)
-        halos[1].around(r.pads.at[0], i, second_in[0])
-        windows = jnp.concatenate(taps(r.pads.at[0], rows, SECOND_DILATION, 1), axis=1)
-        mixed = dot(windows, dilated[1].reshape(taps_rows, inner)) + row(inner_p.at[1], 1)
+        take(2, halos[1], i)
+        surround(2, halos[1], r.pads, i, second_in())
+        windows = windows_of(2, r.pads, SECOND_DILATION)
+        mixed = dot(windows, dilated[1][...]) + row(inner_p.at[1], 1)
         back = Back(mixed, row(inner_p.at[1], 4), row(inner_p.at[1], 5))
-        third_out[0] = back.act
-        grad_low = seeded(cot[0], flags_of(i)).astype(bf16)
+        third_out(back.act)
+        grad_low = seed_of(2, i, cot()).astype(bf16)
         gm = block_out_back(back, grad_low, restore.at[1], r.restore_sum, r.bias_sums[1], r.upper_sums[1])
-        gm_out[0] = gm
-        halos[2].send(i, gm)
-
-    over(turn, [r.second1, r.cotangent], [r.third1, r.gm1])
-    write_restore(r.parts[1], r.restore_sum)
+        gm_out(gm)
+        send(2, halos[2], i, gm)
+
+    over(2, turn, [r.second1, r.cotangent], [r.third1, r.gm1])
+    write_restore(r.restore_parts[1], r.restore_sum)
     clear(r.restore_sum)
 
+    spans = [(steps, n * time) for steps, n, time in zip(stage_steps[3:], seqs[3:], SEQ_TIMES)]
+    fifth, sixth = stage_steps[3], stage_steps[3] + stage_steps[4]
+    ends = sixth + stage_steps[5]
     begins = [(1, 0, 0)]
-    begins += [(1, g, count) for g in range(1, len(groups))]
-    begins += [(0, 0, count + 4)]
-    begins += [(0, g, 2 * count) for g in range(1, len(groups))]
-    due = plan(place, groups, inner, begins, count)
-
-    def beside(base, i):
-        for k in range(count):
+    begins += [(1, g, fifth) for g in range(1, len(groups))]
+    begins += [(0, 0, fifth + stage_steps[4] // 3)]
+    begins += [(0, g, sixth) for g in range(1, len(groups))]
+    due = plan(place, groups, inner, begins, spans)
+
+    def beside(base, steps, i):
+        for k in range(steps):
             if base + k in due:
 
                 @pl.when(i == k)
@@ -762,72 +821,70 @@
                         sets[block].step(g, t)
 
     def between(i, middle, cot, hidden, second_in, gm, mixed, gx_out, gm_out):
-        beside(0, i)
-        halos[2].take(i)
-        halos[2].around(r.pads.at[1], i, gm[0])
-        halos[1].around(r.pads.at[0], i, second_in[0])
+        beside(0, stage_steps[3], i)
+        take(3, halos[2], i)
+        surround(3, halos[2], r.gm_pads, i, gm())
+        surround(3, halos[1], r.pads, i, second_in())
         gh = convolution_back(
-            SECOND_DILATION,
-            hidden[0],
-            gm[0],
+            hidden,
+            gm,
+            lambda: windows_of(3, r.pads, SECOND_DILATION),
+            tapped(3, r.gm_pads, SECOND_DILATION, -1),
             inner_p.at[1],
-            dilated.at[1],
+            dilated[1],
             r.dilated_sum,
             r.small_sums[1],
-            r.pads.at[0],
-            r.pads.at[1],
         )
-        first = Back(middle[0].astype(f32), row(outer.at[1], 0), row(outer.at[1], 1))
+        first = Back(middle().astype(f32), row(outer.at[1], 0), row(outer.at[1], 1))
         r.narrow_sum[...] += dot_tn(first.act, gh)
-        gx = seeded(cot[0], flags_of(i)) + stream_back(first, gh, narrow.at[1], r.wide_sums[1])
-        gx_out[0] = gx.astype(gx_out.dtype)
-        back = Back(mixed[0], row(inner_p.at[0], 4), row(inner_p.at[0], 5))
+        gx = seed_of(3, i, cot()) + stream_back(first, gh, narrow[1], r.wide_sums[1])
+        gx_out(gx)
+        back = Back(mixed(), row(inner_p.at[0], 4), row(inner_p.at[0], 5))
         gm = block_out_back(back, gx.astype(bf16), restore.at[0], r.restore_sum, r.bias_sums[0], r.upper_sums[0])
-        gm_out[0] = gm
-        halos[3].send(i, gm)
-
-    over(between, [r.middle, r.cotangent, r.hidden1, r.second1, r.gm1, r.mixed0], [r.gx1, r.gm0])
-    write_joined(r.parts[1], r.narrow_sum, r.dilated_sum)
-    write_restore(r.parts[0], r.restore_sum)
+        gm_out(gm)
+        send(3, halos[3], i, gm)
+
+    over(3, between, [r.middle, r.cotangent, r.hidden1, r.second1, r.gm1, r.mixed0], [r.gx1, r.gm0])
+    write_joined(r.joined_part, r.narrow_sum, r.dilated_sum)
+    write_restore(r.restore_parts[0], r.restore_sum)
     clear(r.narrow_sum, r.dilated_sum)
 
     def inward(i, act, hidden, second_in, gm, gh_out):
-        beside(count, i)
-        halos[3].take(i)
-        halos[3].around(r.pads.at[1], i, gm[0])
-        halos[0].around(r.pads.at[0], i, second_in[0])
+        beside(fifth, stage_steps[4], i)
+        take(4, halos[3], i)
+        surround(4, halos[3], r.gm_pads, i, gm())
+        surround(4, halos[0], r.pads, i, second_in())
         gh = convolution_back(
-            FIRST_DILATION,
-            hidden[0],
-            gm[0],
+            hidden,
+            gm,
+            lambda: windows_of(4, r.pads, FIRST_DILATION),
+            tapped(4, r.gm_pads, FIRST_DILATION, -1),
             inner_p.at[0],
-            dilated.at[0],
+            dilated[0],
             r.dilated_sum,
             r.small_sums[0],
-            r.pads.at[0],
-            r.pads.at[1],
         )
-        r.narrow_sum[...] += dot_tn(act[0], gh)
-        gh_out[0] = gh
-
-    over(inward, [r.first0, r.hidden0, r.second0, r.gm0], [r.gh0])
-    write_joined(r.parts[0], r.narrow_sum, r.dilated_sum)
+        gh_out(gh)
+        r.narrow_sum[...] += dot_tn(act(), gh)
+
+    over(4, inward, [r.first0, r.hidden0, r.second0, r.gm0], [r.gh0])
+    write_joined(joined.at[1], r.narrow_sum, r.dilated_sum)
 
     def last(i, x, gx_in, gh, middle, third):
-        beside(2 * count, i)
-        y = middle[0].astype(f32) + (dot(third[0], restore[1]) + row(outer.at[1], 2))
-        outputs.send(i, y.astype(bf16))
-        first = Back(x[0].astype(f32), row(outer.at[0], 0), row(outer.at[0], 1))
-        gx = gx_in[0].astype(f32) + stream_back(first, gh[0], narrow.at[0], r.wide_sums[0])
-        grads.send(i, gx.astype(bf16))
-
-    over(last, [r.inputs, r.gx1, r.gh0, r.middle, r.third1], [])
+        beside(sixth, stage_steps[5], i)
+        y = middle().astype(f32) + (dot(third(), restore[1]) + row(outer.at[1], 2))
+        send(5, outputs, i, y.astype(bf16))
+        first = Back(x().astype(f32), row(outer.at[0], 0), row(outer.at[0], 1))
+        gx = gx_in().astype(f32) + stream_back(first, gh(), narrow[0], r.wide_sums[0])
+        send(5, grads, i, gx.astype(bf16))
+
+    over(5, last, [r.inputs, r.gx1, r.gh0, r.middle, r.third1], [])
 
     small = SmallSum(place, *r.small_room)
     small.total[0] = jnp.zeros_like(small.total[0])
     for b in (0, 1):
         gather_small(small.total, b, r.bias_sums[b], r.upper_sums[b], r.wide_sums[b], r.small_sums[b])
-    after = sorted(at for at in due if at >= 3 * count)
+    after = sorted(at for at in due if at >= ends)
     for t in range(max(len(after), small.stages + 1)):
         if t < len(after):
             for block, g, k in due[after[t]]:
@@ -843,9 +900,8 @@
 
 def write_restore(part, total):
     inner, wide = total.shape
-    top = part.shape[0] - wide
     for j in range(wide // inner):
-        at = top + j * inner
+        at = j * inner
         part[at : at + inner, :] = total[:, j * inner : (j + 1) * inner].astype(bf16)
 
 
@@ -894,7 +950,7 @@
         ("outer", outer_params, any_space),
         ("inner", inner_params, any_space),
         ("narrow", narrow, any_space),
-        ("dilated", dilated, any_space),
+        ("dilated", dilated.reshape(1, deep, inner), any_space),
         ("restore", restore, any_space),
     ]
     results = [
@@ -911,7 +967,7 @@
         ("hidden0", (count, rows, inner), f32, any_space),
         ("hidden1", (count, rows, inner), f32, any_space),
         ("mixed0", (count, rows, inner), f32, any_space),
-        ("middle", (count, rows, width), f32, any_space),
+        ("middle", (count, rows, width), KEPT, any_space),
         ("gx1", (count, rows, width), KEPT, any_space),
         ("second0", (count, rows, inner), bf16, any_space),
         ("second1", (count, rows, inner), bf16, any_space),
@@ -928,8 +984,7 @@
     scratch = [
         ("outer_v", twice(outer_params)),
         ("inner_v", twice(inner_params)),
-        ("narrow_v", twice(narrow)),
-        ("dilated_v", twice(dilated)),
+        ("joined_v", pltpu.VMEM((2, width + deep, inner), bf16)),
         ("restore_v", twice(restore)),
         ("param_sems", pltpu.SemaphoreType.DMA((3, 5))),
         ("count_room", SmallSum.scratch(8, 128, levels)),
@@ -937,7 +992,8 @@
         ("halo_rooms", [Halo.scratch(count, inner) for _ in range(4)]),
         ("halves_room", Halves.scratch(count, rows, half)),
         ("grads_room", Halves.scratch(count, rows, half)),
-        ("pads", sums(2, rows + 2 * REACH, inner)),
+        ("pads", sums(max(STEP_SEQS), rows + 2 * REACH, inner)),
+        ("gm_pads", sums(max(STEP_SEQS[3:5]), rows + 2 * REACH, inner)),
         ("narrow_sum", sums(width, inner)),
         ("dilated_sum", sums(deep, inner)),
         ("restore_sum", sums(inner, width)),
@@ -945,7 +1001,8 @@
         ("bias_sums", [sums(8, width)] * 2),
         ("upper_sums", [sums(24, inner)] * 2),
         ("small_sums", [sums(24, inner)] * 2),
-        ("parts", [pltpu.VMEM((2 * width + deep, inner), bf16)] * 2),
+        ("restore_parts", [pltpu.VMEM((width, inner), bf16)] * 2),
+        ("joined_part", pltpu.VMEM((width + deep, inner), bf16)),
         ("sum_rooms", [BlockSum.scratch(groups, inner, levels) for _ in range(2)]),
     ]
     names = [a[0] for a in args] + [a[0] for a in results] + [a[0] for a in scratch]

time: 283 us -> 272 us (0.961)
  Pallas kernels: 258 us -> 246 us
    pallas_call x1, Pallas kernels: 258 us -> 246 us  [shards(): pl.pallas_call(functools.partial(whole, names, count, groups, residues),...]
where the time goes in v6:
time: 272 us; the launch traced here: 271 us
  Pallas kernels  246 us (90%)
  other arithmetic  12.6 us (5%)
  local copies, waits for them, and re-layouts  11.8 us (4%)
    pallas_call x1, Pallas kernels, shards(): pl.pallas_call(functools.partial(whole, names, count, groups, residues),...  246 us
    unnamed x17, local copies, waits for them, and re-layouts  9.06 us

profile of v6, /device:TPU:0, one launch (start us, length us, event | category | flops | bytes accessed | tf_op | source)
XLA Modules:
  0.0 271.2 jit_solution(5891463536596194108)
XLA Ops:
  0.6 0.8 compare_select_fusion
  1.5 1.9 select_reduce_fusion.1
  3.4 0.6 pad.4.refs_3_
  4.0 0.6 broadcast_in_dim.40.refs_2_
  4.6 1.3 copy.26.refs_4_
  5.9 1.3 copy.27.refs_5_
  7.3 246.2 %whole.1 = (bf16[24,256,512]{2,1,0:T(8,128)(2,1)}, bf16[24,256,512]{2,1,0:T(8,128)(2,1)}, bf16[1024,512]{1,0:T(8,128)(2,1)}, bf16[2560,512]{1,0:T(8,128)(2,1)}, ...) custom-call(bf16[24,256,1024]{2,1,0:T(8,128)(2,1)} %refs_0_.1, ...), custom_call_target="tpu_custom_call" | custom-call | tf_op jit(solution)/shard_map/whole/pallas_call | solution.py:1009
  253.5 0.0 copy-start.1
  253.5 0.9 dynamic-slice_bitcast_fusion
  254.4 0.6 broadcast_in_dim_reshape.4
  255.0 0.6 copy.29
  255.6 0.0 slice-start.2
  255.6 5.0 %convert.4 = f32[1,5,512,512]{3,2,1,0:T(8,128)} convert(bf16[1,5,512,512]{3,2,1,0:T(8,128)(2,1)} %bitcast.18) | non-fusion elementwise | flops 1310720 | bytes 7864320 | tf_op jit(solution)/shard_map/reshape | solution.py:1034
  260.6 0.0 copy-done.1
  260.6 1.6 bitcast_convert_fusion
  262.1 0.0 copy-done
  262.1 1.6 bitcast_convert_fusion.1
  263.7 1.6 slice_convert_fusion
  265.4 0.0 slice-done.2
  265.4 0.0 slice-done.3
  265.4 2.8 %copy.32 = bf16[24,256,512]{2,1,0:T(8,128)(2,1)} copy(bf16[24,256,512]{2,1,0:T(8,128)(2,1)S(1)} %bitcast.16) | data formatting | bytes 12582912
  268.2 0.0 slice-done
  268.2 0.3 slice-done.1
  268.5 2.7 copy.33
  (7 shorter events, 0.0 us)
Async XLA Ops:
  253.5 7.1 %copy-start.1 = (bf16[512,1024]{1,0:T(8,128)(2,1)S(1)}, bf16[512,1024]{1,0:T(8,128)(2,1)}, u32[]{:S(2)}) copy-start(bf16[512,1024]{1,0:T(8,128)(2,1)} %get-tuple-element.20) | copy-start | bytes 3145732
  255.6 9.8 %slice-start.2 = ((s8[6291456]{0:T(1024)(128)(4,1)}), s8[4194304]{0:T(1024)(128)(4,1)S(1)}, s32[]{:S(2)}) async-start(s8[6291456]{0:T(1024)(128)(4,1)} %bitcast.15), calls=%async_computation.2 | async-start | bytes 8388608
  255.6 6.6 %copy-start = (bf16[1024,512]{1,0:T(8,128)(2,1)S(1)}, bf16[1024,512]{1,0:T(8,128)(2,1)}, u32[]{:S(2)}) copy-start(bf16[1024,512]{1,0:T(8,128)(2,1)} %get-tuple-element.18) | copy-start | bytes 3145732
  255.6 9.8 %slice-start.3 = ((s8[6291456]{0:T(1024)(128)(4,1)}), s8[2097152]{0:T(1024)(128)(4,1)S(1)}, s32[]{:S(2)}) async-start(s8[6291456]{0:T(1024)(128)(4,1)} %bitcast.15), calls=%async_computation.3 | async-start | bytes 4194304
  262.1 6.1 %slice-start = ((s8[6291456]{0:T(1024)(128)(4,1)}), s8[4194304]{0:T(1024)(128)(4,1)S(1)}, s32[]{:S(2)}) async-start(s8[6291456]{0:T(1024)(128)(4,1)} %bitcast.13), calls=%async_computation | async-start | bytes 8388608
  265.4 3.1 %slice-start.1 = ((s8[6291456]{0:T(1024)(128)(4,1)}), s8[2097152]{0:T(1024)(128)(4,1)S(1)}, s32[]{:S(2)}) async-start(s8[6291456]{0:T(1024)(128)(4,1)} %bitcast.13), calls=%async_computation.1 | async-start | bytes 4194304

commit v7 on v6

--- a/solution.py
+++ b/solution.py
@@ -97,6 +97,11 @@
 
 def row(ref, i):
     return ref[i : i + 1, :]
+
+
+def inner_row(ref, i):
+    half = ref.shape[1] // 2
+    return ref[3 + i // 2 : 4 + i // 2, i % 2 * half : (i % 2 + 1) * half]
 
 
 def column(flags):
@@ -491,7 +496,7 @@
 
 SEQ_TIMES = (5.0, 2.1, 2.5)
 AFTER_TIME = 0.7
-LATENCY = 2.5
+LATENCY = 3.5
 CHIP_RATE = 1.0e5
 CORE_RATE = 5.0e5
 
@@ -588,13 +593,13 @@
 
 
 def convolution_back(hidden, gm, windows, gm_taps, inner, dilated, dilated_sum, small_sum):
-    width = inner.shape[1]
+    width = dilated.shape[1]
     grad_second = None
     for k, piece in enumerate(gm_taps):
         term = dot_nt(piece, dilated[k * width : (k + 1) * width, :])
         grad_second = term if grad_second is None else grad_second + term
     dilated_sum[...] += dot_tn(windows(), gm())
-    back = Back(hidden(), row(inner, 2), row(inner, 3))
+    back = Back(hidden(), inner_row(inner, 2), inner_row(inner, 3))
     gv, gain, shift = back.grad(grad_second)
     gh = gv.astype(bf16)
     small_sum[0:8] += fold(gh.astype(f32))
@@ -631,12 +636,11 @@
     halos = [Halo(place, *room) for room in r.halo_rooms]
     outputs = Halves(place, count, r.block_output, *r.halves_room)
     grads = Halves(place, count, r.input_grad, *r.grads_room)
-    outer, inner_p, joined, restore = r.outer_v, r.inner_v, r.joined_v, r.restore_v
+    outer, joined, restore = r.outer_v, r.joined_v, r.restore_v
     narrow = [joined.at[b, 0:width] for b in (0, 1)]
     dilated = [joined.at[b, width : width + KERNEL * inner] for b in (0, 1)]
     params = (
         (r.outer, lambda at: outer.at[at]),
-        (r.inner, lambda at: inner_p.at[at]),
         (r.narrow, lambda at: joined.at[at, 0:width]),
         (r.dilated, lambda at: joined.at[at, width : width + KERNEL * inner]),
         (r.restore, lambda at: restore.at[at]),
@@ -734,7 +738,7 @@
         halo.begin()
     clear(r.narrow_sum, r.dilated_sum, r.restore_sum)
     clear(*r.wide_sums, *r.bias_sums, *r.upper_sums, *r.small_sums)
-    for k in range(3):
+    for k in range(2):
         arrive(k, 0)
 
     def count_step(k):
@@ -751,9 +755,9 @@
 
         act = norm_act(x().astype(f32), row(outer.at[0], 0), row(outer.at[0], 1))
         act_out(act)
-        hidden = dot(act, narrow[0][...]) + row(inner_p.at[0], 0)
+        hidden = dot(act, narrow[0][...]) + inner_row(outer.at[0], 0)
         hidden_out(hidden)
-        second = norm_act(hidden, row(inner_p.at[0], 2), row(inner_p.at[0], 3))
+        second = norm_act(hidden, inner_row(outer.at[0], 2), inner_row(outer.at[0], 3))
         second_out(second)
         send(0, halos[0], i, second)
 
@@ -765,22 +769,22 @@
     for k in range(len(params)):
         away(k).wait_send()
         arrive(k, 1)
-        if k >= 3:
+        if k >= 2:
             arrive(k, 0)
 
     def second(i, x, second_in, mixed_out, middle_out, hidden_out, second_out):
         take(1, halos[0], i)
         surround(1, halos[0], r.pads, i, second_in())
         windows = windows_of(1, r.pads, FIRST_DILATION)
-        mixed = dot(windows, dilated[0][...]) + row(inner_p.at[0], 1)
+        mixed = dot(windows, dilated[0][...]) + inner_row(outer.at[0], 1)
         mixed_out(mixed)
-        third = norm_act(mixed, row(inner_p.at[0], 4), row(inner_p.at[0], 5))
+        third = norm_act(mixed, inner_row(outer.at[0], 4), inner_row(outer.at[0], 5))
         y = x().astype(f32) + (dot(third, restore[0]) + row(outer.at[0], 2))
         middle_out(y)
         act = norm_act(y, row(outer.at[1], 0), row(outer.at[1], 1))
-        hidden = dot(act, narrow[1][...]) + row(inner_p.at[1], 0)
+        hidden = dot(act, narrow[1][...]) + inner_row(outer.at[1], 0)
         hidden_out(hidden)
-        second = norm_act(hidden, row(inner_p.at[1], 2), row(inner_p.at[1], 3))
+        second = norm_act(hidden, inner_row(outer.at[1], 2), inner_row(outer.at[1], 3))
         second_out(second)
         send(1, halos[1], i, second)
 
@@ -790,8 +794,8 @@
         take(2, halos[1], i)
         surround(2, halos[1], r.pads, i, second_in())
         windows = windows_of(2, r.pads, SECOND_DILATION)
-        mixed = dot(windows, dilated[1][...]) + row(inner_p.at[1], 1)
-        back = Back(mixed, row(inner_p.at[1], 4), row(inner_p.at[1], 5))
+        mixed = dot(windows, dilated[1][...]) + inner_row(outer.at[1], 1)
+        back = Back(mixed, inner_row(outer.at[1], 4), inner_row(outer.at[1], 5))
         third_out(back.act)
         grad_low = seed_of(2, i, cot()).astype(bf16)
         gm = block_out_back(back, grad_low, restore.at[1], r.restore_sum, r.bias_sums[1], r.upper_sums[1])
@@ -830,7 +834,7 @@
             gm,
             lambda: windows_of(3, r.pads, SECOND_DILATION),
             tapped(3, r.gm_pads, SECOND_DILATION, -1),
-            inner_p.at[1],
+            outer.at[1],
             dilated[1],
             r.dilated_sum,
             r.small_sums[1],
@@ -839,7 +843,7 @@
         r.narrow_sum[...] += dot_tn(first.act, gh)
         gx = seed_of(3, i, cot()) + stream_back(first, gh, narrow[1], r.wide_sums[1])
         gx_out(gx)
-        back = Back(mixed(), row(inner_p.at[0], 4), row(inner_p.at[0], 5))
+        back = Back(mixed(), inner_row(outer.at[0], 4), inner_row(outer.at[0], 5))
         gm = block_out_back(back, gx.astype(bf16), restore.at[0], r.restore_sum, r.bias_sums[0], r.upper_sums[0])
         gm_out(gm)
         send(3, halos[3], i, gm)
@@ -859,7 +863,7 @@
             gm,
             lambda: windows_of(4, r.pads, FIRST_DILATION),
             tapped(4, r.gm_pads, FIRST_DILATION, -1),
-            inner_p.at[0],
+            outer.at[0],
             dilated[0],
             r.dilated_sum,
             r.small_sums[0],
@@ -942,13 +946,14 @@
     residues = float(chip_seqs * lax.axis_size("dp") * LENGTH)
     deep = KERNEL * inner
     any_space, vmem = pl.BlockSpec(memory_space=pl.ANY), pl.BlockSpec(memory_space=pltpu.VMEM)
+    packed = jnp.concatenate([outer_params, inner_params.reshape(1, 3, width)], axis=1)
+    packed = jnp.pad(packed, ((0, 0), (0, 2), (0, 0)))
     args = [
         ("inputs", inputs, any_space),
         ("cotangent", cotangent, any_space),
         ("flags", flags, vmem),
         ("counts", counts, vmem),
-        ("outer", outer_params, any_space),
-        ("inner", inner_params, any_space),
+        ("outer", packed, any_space),
         ("narrow", narrow, any_space),
         ("dilated", dilated.reshape(1, deep, inner), any_space),
         ("restore", restore, any_space),
@@ -982,8 +987,7 @@
         return pltpu.VMEM(shape, f32)
 
     scratch = [
-        ("outer_v", twice(outer_params)),
-        ("inner_v", twice(inner_params)),
+        ("outer_v", twice(packed)),
         ("joined_v", pltpu.VMEM((2, width + deep, inner), bf16)),
         ("restore_v", twice(restore)),
         ("param_sems", pltpu.SemaphoreType.DMA((3, 5))),

time: 272 us -> 270 us (level)
  Pallas kernels: 246 us -> 243 us
    pallas_call x1, Pallas kernels: 246 us -> 243 us  [shards(): pl.pallas_call(functools.partial(whole, names, count, groups, residues),...]
    unnamed x17 -> x16, local copies, waits for them, and re-layouts: 9.06 us -> 7.15 us
where the time goes in v7:
time: 270 us; the launch traced here: 267 us
  Pallas kernels  243 us (90%)
  other arithmetic  13.9 us (5%)
  local copies, waits for them, and re-layouts  9.87 us (4%)
    pallas_call x1, Pallas kernels, shards(): pl.pallas_call(functools.partial(whole, names, count, groups, residues),...  243 us
    unnamed x16, local copies, waits for them, and re-layouts  7.15 us

profile of v7, /device:TPU:0, one launch (start us, length us, event | category | flops | bytes accessed | tf_op | source)
XLA Modules:
  0.0 267.1 jit_solution(14039253662913083893)
XLA Ops:
  0.6 0.8 compare_select_fusion
  1.5 1.9 select_reduce_fusion.1
  3.4 0.6 pad.8.refs_3_
  4.0 0.6 broadcast_in_dim.40.refs_2_
  4.6 0.7 reduce
  5.4 0.7 copy.24
  6.1 0.6 select_maximum_fusion.refs_4_
  6.7 242.6 %whole.1 = (bf16[24,256,512]{2,1,0:T(8,128)(2,1)}, bf16[24,256,512]{2,1,0:T(8,128)(2,1)}, bf16[1024,512]{1,0:T(8,128)(2,1)}, bf16[2560,512]{1,0:T(8,128)(2,1)}, ...) custom-call(bf16[24,256,1024]{2,1,0:T(8,128)(2,1)} %refs_0_.1, ...), custom_call_target="tpu_custom_call" | custom-call | tf_op jit(solution)/shard_map/whole/pallas_call | solution.py:1013
  249.3 0.0 copy-start.1
  249.3 0.9 dynamic-slice_bitcast_fusion
  250.2 0.6 broadcast_in_dim_reshape.4
  250.8 0.6 copy.26
  251.4 5.0 %convert.4 = f32[1,5,512,512]{3,2,1,0:T(8,128)} convert(bf16[1,5,512,512]{3,2,1,0:T(8,128)(2,1)} %bitcast.18) | non-fusion elementwise | flops 1310720 | bytes 7864320 | tf_op jit(solution)/shard_map/reshape | solution.py:1038
  256.4 0.0 copy-done.1
  256.4 1.6 bitcast_convert_fusion
  258.0 0.0 copy-done
  258.0 1.6 bitcast_convert_fusion.1
  259.6 1.7 slice_convert_fusion
  261.3 0.0 slice-done.2
  261.3 0.0 slice-done.3
  261.3 2.8 %copy.29 = bf16[24,256,512]{2,1,0:T(8,128)(2,1)} copy(bf16[24,256,512]{2,1,0:T(8,128)(2,1)S(1)} %bitcast.16) | data formatting | bytes 12582912
  264.1 0.0 slice-done
  264.1 0.3 slice-done.1
  264.4 2.7 %copy.30 = bf16[24,256,512]{2,1,0:T(8,128)(2,1)} copy(bf16[24,256,512]{2,1,0:T(8,128)(2,1)S(1)} %bitcast.14) | data formatting | bytes 12582912
  (9 shorter events, 0.0 us)
Async XLA Ops:
  249.3 7.1 %copy-start.1 = (bf16[512,1024]{1,0:T(8,128)(2,1)S(1)}, bf16[512,1024]{1,0:T(8,128)(2,1)}, u32[]{:S(2)}) copy-start(bf16[512,1024]{1,0:T(8,128)(2,1)} %get-tuple-element.20) | copy-start | bytes 3145732
  251.4 9.8 %slice-start.2 = ((s8[6291456]{0:T(1024)(128)(4,1)}), s8[4194304]{0:T(1024)(128)(4,1)S(1)}, s32[]{:S(2)}) async-start(s8[6291456]{0:T(1024)(128)(4,1)} %bitcast.15), calls=%async_computation.2 | async-start | bytes 8388608
  251.4 6.6 %copy-start = (bf16[1024,512]{1,0:T(8,128)(2,1)S(1)}, bf16[1024,512]{1,0:T(8,128)(2,1)}, u32[]{:S(2)}) copy-start(bf16[1024,512]{1,0:T(8,128)(2,1)} %get-tuple-element.18) | copy-start | bytes 3145732
  251.4 9.8 %slice-start.3 = ((s8[6291456]{0:T(1024)(128)(4,1)}), s8[2097152]{0:T(1024)(128)(4,1)S(1)}, s32[]{:S(2)}) async-start(s8[6291456]{0:T(1024)(128)(4,1)} %bitcast.15), calls=%async_computation.3 | async-start | bytes 4194304
  258.0 6.1 %slice-start = ((s8[6291456]{0:T(1024)(128)(4,1)}), s8[4194304]{0:T(1024)(128)(4,1)S(1)}, s32[]{:S(2)}) async-start(s8[6291456]{0:T(1024)(128)(4,1)} %bitcast.13), calls=%async_computation | async-start | bytes 8388608
  261.3 3.1 %slice-start.1 = ((s8[6291456]{0:T(1024)(128)(4,1)}), s8[2097152]{0:T(1024)(128)(4,1)S(1)}, s32[]{:S(2)}) async-start(s8[6291456]{0:T(1024)(128)(4,1)} %bitcast.13), calls=%async_computation.1 | async-start | bytes 4194304

commit v8 on v7

--- a/solution.py
+++ b/solution.py
@@ -811,7 +811,7 @@
     ends = sixth + stage_steps[5]
     begins = [(1, 0, 0)]
     begins += [(1, g, fifth) for g in range(1, len(groups))]
-    begins += [(0, 0, fifth + stage_steps[4] // 3)]
+    begins += [(0, 0, fifth)]
     begins += [(0, g, sixth) for g in range(1, len(groups))]
     due = plan(place, groups, inner, begins, spans)
 

time: 270 us -> 269 us (level)
  no operation moved by 1% of the time
where the time goes in v8:
time: 269 us; the launch traced here: 267 us
  Pallas kernels  243 us (90%)
  other arithmetic  13.9 us (5%)
  local copies, waits for them, and re-layouts  9.87 us (4%)
    pallas_call x1, Pallas kernels, shards(): pl.pallas_call(functools.partial(whole, names, count, groups, residues),...  243 us
    unnamed x16, local copies, waits for them, and re-layouts  7.15 us

profile of v8, /device:TPU:0, one launch (start us, length us, event | category | flops | bytes accessed | tf_op | source)
XLA Modules:
  0.0 267.1 jit_solution(14702868606608485435)
XLA Ops:
  0.6 0.8 compare_select_fusion
  1.5 1.9 select_reduce_fusion.1
  3.4 0.6 pad.8.refs_3_
  4.0 0.6 broadcast_in_dim.40.refs_2_
  4.6 0.7 reduce
  5.4 0.7 copy.24
  6.1 0.6 select_maximum_fusion.refs_4_
  6.7 242.6 %whole.1 = (bf16[24,256,512]{2,1,0:T(8,128)(2,1)}, bf16[24,256,512]{2,1,0:T(8,128)(2,1)}, bf16[1024,512]{1,0:T(8,128)(2,1)}, bf16[2560,512]{1,0:T(8,128)(2,1)}, ...) custom-call(bf16[24,256,1024]{2,1,0:T(8,128)(2,1)} %refs_0_.1, ...), custom_call_target="tpu_custom_call" | custom-call | tf_op jit(solution)/shard_map/whole/pallas_call | solution.py:1013
  249.3 0.0 copy-start.1
  249.3 0.9 dynamic-slice_bitcast_fusion
  250.2 0.6 broadcast_in_dim_reshape.4
  250.8 0.6 copy.26
  251.4 5.0 %convert.4 = f32[1,5,512,512]{3,2,1,0:T(8,128)} convert(bf16[1,5,512,512]{3,2,1,0:T(8,128)(2,1)} %bitcast.18) | non-fusion elementwise | flops 1310720 | bytes 7864320 | tf_op jit(solution)/shard_map/reshape | solution.py:1038
  256.4 0.0 copy-done.1
  256.4 1.6 bitcast_convert_fusion
  258.0 0.0 copy-done
  258.0 1.6 bitcast_convert_fusion.1
  259.6 1.7 slice_convert_fusion
  261.2 0.0 slice-done.2
  261.2 0.0 slice-done.3
  261.3 2.8 %copy.29 = bf16[24,256,512]{2,1,0:T(8,128)(2,1)} copy(bf16[24,256,512]{2,1,0:T(8,128)(2,1)S(1)} %bitcast.16) | data formatting | bytes 12582912
  264.1 0.0 slice-done
  264.1 0.3 slice-done.1
  264.4 2.7 %copy.30 = bf16[24,256,512]{2,1,0:T(8,128)(2,1)} copy(bf16[24,256,512]{2,1,0:T(8,128)(2,1)S(1)} %bitcast.14) | data formatting | bytes 12582912
  (9 shorter events, 0.0 us)
Async XLA Ops:
  249.3 7.1 %copy-start.1 = (bf16[512,1024]{1,0:T(8,128)(2,1)S(1)}, bf16[512,1024]{1,0:T(8,128)(2,1)}, u32[]{:S(2)}) copy-start(bf16[512,1024]{1,0:T(8,128)(2,1)} %get-tuple-element.20) | copy-start | bytes 3145732
  251.4 9.8 %slice-start.2 = ((s8[6291456]{0:T(1024)(128)(4,1)}), s8[4194304]{0:T(1024)(128)(4,1)S(1)}, s32[]{:S(2)}) async-start(s8[6291456]{0:T(1024)(128)(4,1)} %bitcast.15), calls=%async_computation.2 | async-start | bytes 8388608
  251.4 6.6 %copy-start = (bf16[1024,512]{1,0:T(8,128)(2,1)S(1)}, bf16[1024,512]{1,0:T(8,128)(2,1)}, u32[]{:S(2)}) copy-start(bf16[1024,512]{1,0:T(8,128)(2,1)} %get-tuple-element.18) | copy-start | bytes 3145732
  251.4 9.8 %slice-start.3 = ((s8[6291456]{0:T(1024)(128)(4,1)}), s8[2097152]{0:T(1024)(128)(4,1)S(1)}, s32[]{:S(2)}) async-start(s8[6291456]{0:T(1024)(128)(4,1)} %bitcast.15), calls=%async_computation.3 | async-start | bytes 4194304
  258.0 6.1 %slice-start = ((s8[6291456]{0:T(1024)(128)(4,1)}), s8[4194304]{0:T(1024)(128)(4,1)S(1)}, s32[]{:S(2)}) async-start(s8[6291456]{0:T(1024)(128)(4,1)} %bitcast.13), calls=%async_computation | async-start | bytes 8388608
  261.3 3.1 %slice-start.1 = ((s8[6291456]{0:T(1024)(128)(4,1)}), s8[2097152]{0:T(1024)(128)(4,1)S(1)}, s32[]{:S(2)}) async-start(s8[6291456]{0:T(1024)(128)(4,1)} %bitcast.13), calls=%async_computation.1 | async-start | bytes 4194304
